TPU v7x, 128 devices: a whole 4x4x4 slice. The times are simulated.
128 devices in a mesh: wide: 16 (over x, y), narrow: 8 (over z, core).
Axes of the slice: x: 4, y: 4, z: 4, core: 2. Of those that a mesh axis runs over, the one named last changes fastest.
Arguments:
- residual: bfloat16 [384, 18432], P('wide', 'narrow'), may hold values from -6 to 6
- ln_gain: float32 [18432], P('narrow'), may hold values from 0.1 to 1.9
- w_query: bfloat16 [18432, 12288], P('narrow', 'wide'), may hold values from -0.046875 to 0.046875
- w_keyval: bfloat16 [18432, 512], P('narrow', 'wide'), may hold values from -0.046875 to 0.046875
- w_out: bfloat16 [12288, 18432], P('wide', 'narrow'), may hold values from -0.0546875 to 0.0546875
- w_up: bfloat16 [18432, 36864], P('narrow', 'wide'), may hold values from -0.046875 to 0.046875
- k_cache: bfloat16 [384, 2048, 256], P('wide', 'narrow'), may hold values from -48 to 48
- v_cache: bfloat16 [384, 2048, 256], P('wide', 'narrow'), may hold values from -6 to 6
- lengths: int32 [384], P('wide'), may hold values from 1 to 2048, as said below
Outputs:
- mixed: bfloat16 [384, 18432], P('wide', 'narrow')
- scaled: bfloat16 [384, 36864], P('narrow', 'wide')
- peak: float32 [384], P('narrow')
Inputs may be any that keep to these rules, and one draw needn't show every extreme that they name: `lengths`: one row has all 2048 positions filled.
All inputs are finite; a program needn't handle non-finite values. Where the computation divides by a largest or mean magnitude, that divisor is 1e-20 or more.
Results may differ from a plain program's by a relative error of at most 0.012.
The roundings to bfloat16 on the way count: a program that leaves them out, or rounds other values in their place, can miss the bound.
Values may be sent and summed in bfloat16 or wider, within the bound.
No kernel may reach another device: no remote copies, remote signals or barrier semaphores. Data moves between devices by JAX's collectives and lax.ppermute only.
A program may use at most 128 MiB of HBM per device.

v0:
```python
import jax
import jax.numpy as jnp
from jax import lax
from jax.sharding import PartitionSpec as P

D = 18432
HEADS = 48
HEAD = 256


norm_eps = 1e-05
peak_eps = 1e-06


def merged(value, axis, join):
    pieces = jax.tree.map(lambda part: lax.all_gather(part, axis), value)
    head = jax.tree.map(lambda part: part[0], pieces)
    tail = jax.tree.map(lambda part: part[1:], pieces)
    running, _ = lax.scan(lambda running, share: (join(running, share), None), head, tail)
    return running


def to_rows(block):
    return lax.all_to_all(block, "wide", split_axis=0, concat_axis=1, tiled=True)


def combine(first, second):
    top_a, total_a, acc_a = first
    top_b, total_b, acc_b = second
    both = jnp.maximum(top_a, top_b)
    keep_a = jnp.exp(top_a - both)
    keep_b = jnp.exp(top_b - both)
    return (
        both,
        total_a * keep_a + total_b * keep_b,
        acc_a * keep_a[..., None] + acc_b * keep_b[..., None],
    )


def shards(residual, ln_gain, w_query, w_keyval, w_out, w_up, k_cache, v_cache, lengths):
    wide_count = lax.axis_size("wide")
    local_rows = residual.shape[0]
    residual_f32 = residual.astype(jnp.float32)
    sums = lax.psum(
        (jnp.sum(residual_f32, axis=1), jnp.sum(residual_f32 * residual_f32, axis=1)), "narrow"
    )
    mean = sums[0] / D
    variance = sums[1] / D - mean * mean
    normed = (
        (residual_f32 - mean[:, None]) * lax.rsqrt(variance + norm_eps)[:, None] * ln_gain[None, :]
    ).astype(jnp.bfloat16)
    query_cols = w_query.shape[1]
    head_cols = query_cols + w_keyval.shape[1]
    piece = lax.all_gather(normed, "wide", axis=0, tiled=True)
    terms = jnp.concatenate(
        [
            jnp.dot(piece, w_query, preferred_element_type=jnp.float32),
            jnp.dot(piece, w_keyval, preferred_element_type=jnp.float32),
            jnp.dot(piece, w_up, preferred_element_type=jnp.float32),
        ],
        axis=1,
    )
    head_terms = terms[:, :head_cols]
    up_terms = terms[:, head_cols:]
    summed = lax.psum(head_terms, "narrow").astype(jnp.bfloat16)
    arranged = to_rows(summed).reshape(local_rows, wide_count, head_cols)
    query = arranged[:, :, :query_cols].reshape(local_rows, HEADS, HEAD)
    keyval = arranged[:, :, query_cols:].reshape(local_rows, 2 * HEAD)
    new_key = keyval[:, :HEAD]
    new_value = keyval[:, HEAD:]
    factor = 1.0 / HEAD**0.5
    local_len = k_cache.shape[1]
    positions = lax.axis_index("narrow") * local_len + jnp.arange(local_len, dtype=jnp.int32)
    valid = positions[None, :] < lengths[:, None]
    scores = jnp.einsum("rhd,rpd->rhp", query, k_cache, preferred_element_type=jnp.float32) * factor
    masked = jnp.where(valid[:, None, :], scores, jnp.float32(-1e30))
    top = jnp.max(masked, axis=2)
    probs = jnp.where(valid[:, None, :], jnp.exp(masked - top[..., None]), jnp.float32(0.0))
    total = jnp.sum(probs, axis=2)
    partial_value = jnp.einsum(
        "rhp,rpd->rhd", probs.astype(jnp.bfloat16), v_cache, preferred_element_type=jnp.float32
    )
    top, total, partial_value = merged((top, total, partial_value), "narrow", combine)
    own = jnp.einsum("rhd,rd->rh", query, new_key, preferred_element_type=jnp.float32) * factor
    both = jnp.maximum(top, own)
    keep = jnp.exp(top - both)
    fresh = jnp.exp(own - both)
    mass = total * keep + fresh
    new_term = jnp.einsum(
        "rh,rd->rhd", fresh.astype(jnp.bfloat16), new_value, preferred_element_type=jnp.float32
    )
    attended = ((partial_value * keep[..., None] + new_term) / mass[..., None]).astype(jnp.bfloat16)
    attended = attended.reshape(local_rows, HEADS * HEAD)
    grouped = lax.all_to_all(attended, "wide", split_axis=1, concat_axis=0, tiled=True)
    projected = lax.psum_scatter(
        jnp.dot(grouped, w_out, preferred_element_type=jnp.float32),
        "wide",
        scatter_dimension=0,
        tiled=True,
    )
    mixed = (residual_f32 + projected).astype(jnp.bfloat16)
    up = lax.psum_scatter(up_terms, "narrow", scatter_dimension=0, tiled=True)
    peak = lax.pmax(jnp.max(jnp.abs(up), axis=1), "wide")
    scaled = (up / (peak + peak_eps)[:, None]).astype(jnp.bfloat16)
    return (mixed, scaled, peak)


def solution(mesh):
    placed = (
        P("wide", "narrow"),
        P("narrow"),
        P("narrow", "wide"),
        P("narrow", "wide"),
        P("wide", "narrow"),
        P("narrow", "wide"),
        P("wide", "narrow", None),
        P("wide", "narrow", None),
        P("wide"),
    )
    return jax.shard_map(
        shards,
        mesh=mesh,
        in_specs=placed,
        out_specs=(P("wide", "narrow"), P("narrow", "wide"), P("narrow")),
        check_vma=False,
    )
```

profile of v0, /device:TPU:0, one launch (start us, length us, event | category | flops | bytes accessed | tf_op | source)
XLA Modules:
  0.0 359.7 jit_solution(11110954040917522776)
XLA Ops:
  7.2 0.0 all-gather.6.cloned.1.call-start
  7.2 1.2 convert_reduce_fusion
  8.4 16.0 %all-reduce.1 = (f32[24]{0:T(128)S(1)}, f32[24]{0:T(128)S(1)}) all-reduce(f32[24]{0:T(128)S(1)} %get-tuple-element.46, f32[24]{0:T(128)S(1)} %get-tuple-element.45), channel_id=1, replica_groups=mesh['wide'=16,'narrow'=8] {'narrow'}, use_global_device_ids=true, to_apply=%region_3.0 | all-reduce | flops 48 | bytes 384 | tf_op jit(solution)/shard_map/psum | solution.py:44
  24.4 1.6 fusion.13
  26.1 43.5 %all-gather.6.cloned.1.call-done = bf16[384,2304]{1,0:T(8,128)(2,1)} async-done(((bf16[24,2304]{1,0:T(8,128)(2,1)}), bf16[384,2304]{1,0:T(8,128)(2,1)}) %all-gather.6.cloned.1.call-update) | async-done | bytes 1769488 | tf_op jit(solution)/shard_map/all_gather | solution.py:54
  69.5 2.2 fusion.24
  71.7 3.5 fusion.23
  75.3 1.2 pad_maximum_fusion
  76.5 52.9 %all-reduce.3 = bf16[384,800]{1,0:T(8,128)(2,1)} all-reduce(f32[384,800]{1,0:T(8,128)} %pad_maximum_fusion), channel_id=1, replica_groups=mesh['wide'=16,'narrow'=8] {'narrow'}, use_global_device_ids=true, to_apply=%region_4.0 | all-reduce | flops 307200 | bytes 1843200 | tf_op jit(solution)/shard_map/psum | solution.py:65
  129.4 5.2 %all-to-all-start = ((bf16[16,24,800]{2,1,0:T(8,128)(2,1)}), bf16[16,24,800]{2,1,0:T(8,128)(2,1)}, u32[]{:S(2)}, u32[]{:S(2)}) async-start(bf16[16,24,800]{2,1,0:T(8,128)(2,1)} %bitcast.45), calls=%async_computation | async-start | bytes 1376256 | tf_op jit(solution)/shard_map/all_to_all | solution.py:24
  134.5 0.0 all-gather.8.cloned.1.call-start
  134.6 0.7 broadcast_compare_fusion
  135.3 11.0 %all-to-all-done = bf16[16,24,800]{2,1,0:T(8,128)(2,1)} async-done(((bf16[16,24,800]{2,1,0:T(8,128)(2,1)}), bf16[16,24,800]{2,1,0:T(8,128)(2,1)}, u32[]{:S(2)}, u32[]{:S(2)}) %all-to-all-start) | async-done | bytes 614432 | tf_op jit(solution)/shard_map/all_to_all | solution.py:24
  146.3 1.1 slice.46
  147.4 0.9 copy.20
  148.3 2.1 reshape.58
  150.4 3.3 fusion.22
  153.7 1.1 copy-done.1
  154.8 1.7 fusion.6
  156.4 0.0 reduce-scatter.5.cloned.1.call-start
  156.5 10.6 %fusion.26 = f32[384,2304]{1,0:T(8,128)} fusion(bf16[384,2304]{1,0:T(8,128)(2,1)} %all-gather.6.cloned.1.call-done, bf16[2304,2304]{1,0:T(8,128)(2,1)} %param.16), kind=kOutput, calls=%fused_computation.50 | convolution fusion | flops 4076863488 | bytes 15925248 | tf_op jit(solution)/shard_map/dot_general | solution.py:59
  167.1 0.0 reduce-scatter.5.cloned.1.call-update
  167.1 0.0 reduce-scatter.7.cloned.1.call-start
  167.2 0.9 slice.53
  168.1 12.8 %all-gather = f32[192,48]{1,0:T(8,128)S(1)} all-gather(f32[24,48]{1,0:T(8,128)S(1)} %get-tuple-element.74), channel_id=2, replica_groups=mesh['wide'=16,'narrow'=8] {'narrow'}, dimensions={0}, use_global_device_ids=true | all-gather | bytes 41472 | tf_op jit(solution)/shard_map/all_gather | solution.py:16
  180.9 0.6 slice.50
  181.5 1.7 fusion.5
  183.3 12.8 %all-gather.1 = f32[192,48]{1,0:T(8,128)S(1)} all-gather(f32[24,48]{1,0:T(8,128)S(1)} %fusion.5), channel_id=3, replica_groups=mesh['wide'=16,'narrow'=8] {'narrow'}, dimensions={0}, use_global_device_ids=true | all-gather | bytes 41472 | tf_op jit(solution)/shard_map/all_gather | solution.py:16
  196.0 0.6 slice.48
  196.6 0.6 slice.51
  197.3 0.7 copy.21
  197.9 1.6 reshape.59
  199.5 1.3 slice_convert_fusion
  200.9 1.9 fusion.16
  202.8 5.3 %all-gather.8.cloned.1.call-done = f32[192,48,256]{2,1,0:T(8,128)} async-done(((f32[24,48,256]{2,1,0:T(8,128)}), f32[192,48,256]{2,1,0:T(8,128)}) %all-gather.8.cloned.1.call-update) | async-done | bytes 9437200 | tf_op jit(solution)/shard_map/all_gather | solution.py:16
  208.1 2.4 slice.49
  210.5 7.3 %slice.52 = f32[168,48,256]{2,1,0:T(8,128)} slice(f32[192,48,256]{2,1,0:T(8,128)} %all-gather.8.cloned.1.call-done), slice={[24:192], [0:48], [0:256]} | slice | bytes 16515072 | tf_op jit(solution)/shard_map/slice | solution.py:18
  217.8 31.2 %while.14 = (s32[]{:T(128)}, f32[24,48]{1,0:T(8,128)S(1)}, f32[24,48]{1,0:T(8,128)}, f32[24,48,256]{2,1,0:T(8,128)}, f32[7,24,48]{2,1,0:T(8,128)}, /*index=5*/f3...) while((s32[]{:T(128)}, f32[24,48]{1,0:T(8,128)S(1)}, f32[24,48]{1,0:T(8,128)}, ...), condition=%wide.region_8.9_spmd, body=%wide.region_7.8_spmd.sunk | while | flops 891650 | bytes 3585125 | solution.py:19
  217.8 1.4 fusion.41
  219.2 3.1 fusion.42
  222.3 1.4 fusion.41
  223.6 3.1 fusion.42
  226.7 1.4 fusion.41
  228.1 3.1 fusion.42
  231.2 1.4 fusion.41
  232.5 3.1 fusion.42
  235.6 1.4 fusion.41
  237.0 3.1 fusion.42
  240.1 1.4 fusion.41
  241.4 3.1 fusion.42
  244.5 1.4 fusion.41
  245.9 3.1 fusion.42
  249.0 0.7 fusion.18
  249.7 2.6 divide_convert_fusion
  252.4 2.1 all_to_all.29
  254.5 1.2 copy.22
  255.7 19.3 %all_to_all.35 = bf16[24,16,768]{2,0,1:T(8,128)(2,1)S(1)} all-to-all(bf16[24,16,768]{2,0,1:T(8,128)(2,1)S(1)} %copy.22), channel_id=1, replica_groups=mesh['wide'=16,'narrow'=8] {'wide'}, dimensions={1} | all-to-all | bytes 1179648 | tf_op jit(solution)/shard_map/all_to_all | solution.py:94
  275.0 3.3 fusion.25
  278.3 0.0 reduce-scatter.5.cloned.1.call-done
  278.4 1.1 abs_reduce_fusion
  279.5 37.3 %pmax.7 = f32[48]{0:T(128)S(1)} all-reduce(f32[48]{0:T(128)S(1)} %abs_reduce_fusion), channel_id=1, replica_groups=mesh['wide'=16,'narrow'=8] {'wide'}, use_global_device_ids=true, to_apply=%region_12.13 | all-reduce | flops 48 | bytes 384 | tf_op jit(solution)/shard_map/pmax | solution.py:103
  316.8 1.8 divide_convert_fusion.1
  318.6 32.9 %reduce-scatter.7.cloned.1.call-done = f32[24,2304]{1,0:T(8,128)} async-done(((f32[384,2304]{1,0:T(8,128)}), f32[24,2304]{1,0:T(8,128)}) %reduce-scatter.7.cloned.1.call-update) | async-done | bytes 221200
  351.5 1.7 fusion.15
  (22 shorter events, 0.1 us)
Async XLA Ops:
  7.2 267.8 %copy-start = (bf16[768,2304]{1,0:T(8,128)(2,1)S(1)}, bf16[768,2304]{1,0:T(8,128)(2,1)}, u32[]{:S(2)}) copy-start(bf16[768,2304]{1,0:T(8,128)(2,1)} %param.15) | copy-start | bytes 10616836
  7.2 62.4 %all-gather.6.cloned.1.call-start = ((), (), s32[]{:S(2)}) async-start(), calls=%async_computation.4 | async-start | bytes 1880064 | tf_op jit(solution)/shard_map/all_gather | solution.py:54
  69.5 2.2 copy-start.6
  129.4 5.2 %copy-start.5 = (s32[24]{0:T(128)S(1)}, s32[24]{0:T(128)}, u32[]{:S(2)}) copy-start(s32[24]{0:T(128)} %param.19) | copy-start | bytes 292
  129.4 16.9 %all-to-all-start = ((bf16[16,24,800]{2,1,0:T(8,128)(2,1)}), bf16[16,24,800]{2,1,0:T(8,128)(2,1)}, u32[]{:S(2)}, u32[]{:S(2)}) async-start(bf16[16,24,800]{2,1,0:T(8,128)(2,1)} %bitcast.45), calls=%async_computation | async-start | bytes 1376256 | tf_op jit(solution)/shard_map/all_to_all | solution.py:24
  134.5 73.6 %all-gather.8.cloned.1.call-start = ((), (), s32[]{:S(2)}) async-start(), calls=%async_computation.6 | async-start | bytes 10616832 | tf_op jit(solution)/shard_map/all_gather | solution.py:16
  150.4 4.4 %copy-start.2 = (bf16[24,256,256]{2,1,0:T(8,128)(2,1)S(1)}, bf16[24,256,256]{2,1,0:T(8,128)(2,1)}, u32[]{:S(2)}) copy-start(bf16[24,256,256]{2,1,0:T(8,128)(2,1)} %param.18) | copy-start | bytes 9437188
  150.4 4.4 %copy-start.4 = (pred[24,256]{1,0:T(8,128)(4,1)S(1)}, pred[24,256]{1,0:T(8,128)(4,1)}, u32[]{:S(2)}) copy-start(pred[24,256]{1,0:T(8,128)(4,1)} %broadcast_compare_fusion) | copy-start | bytes 18436
  153.7 1.1 copy-start.1
  153.7 14.4 %copy-start.3 = (f32[24,48]{1,0:T(8,128)}, f32[24,48]{1,0:T(8,128)S(1)}, u32[]{:S(2)}) copy-start(f32[24,48]{1,0:T(8,128)S(1)} %get-tuple-element.74) | copy-start | bytes 13828
  156.4 121.9 %reduce-scatter.5.cloned.1.call-start = ((), (), s32[]{:S(2)}) async-start(), calls=%async_computation.5 | async-start | bytes 3981312 | tf_op jit(solution)/shard_map/reduce_scatter | solution.py:102
  167.1 184.4 %reduce-scatter.7.cloned.1.call-start = ((), (), s32[]{:S(2)}) async-start(), calls=%async_computation.7 | async-start | bytes 3760128
  316.8 36.4 %copy-start.7 = (f32[48]{0:T(128)}, f32[48]{0:T(128)S(1)}, u32[]{:S(2)}) copy-start(f32[48]{0:T(128)S(1)} %pmax.7) | copy-start | bytes 580
Sparse Core Ops, SparseCore 0:
  26.2 43.3 all-gather.5
  156.6 51.5 all-gather.7
  210.6 36.8 reduce-scatter.4
  278.4 73.0 reduce-scatter.6
where the time goes:
time: 361 us; the launch traced here: 360 us
  blocking collectives  151 us (42%)
  waiting for transfers between devices  92.7 us (26%)
  other arithmetic  46.9 us (13%)
  matrix products  26.5 us (7%)
  local copies, waits for them, and re-layouts  23.3 us (6%)
  between operations  13.9 us (4%)
  starting transfers between devices  5.32 us (1%)
    psum x1, blocking collectives, shards(): summed = lax.psum(head_terms, 'narrow').astype(jnp.bfloat16)  52.9 us
    all_gather x1, waiting for transfers between devices, shards(): piece = lax.all_gather(normed, 'wide', axis=0, tiled=True)  43.5 us
    pmax x1, blocking collectives, shards(): peak = lax.pmax(jnp.max(jnp.abs(up), axis=1), 'wide')  37.3 us
    unnamed x5, waiting for transfers between devices  32.9 us
    all_gather x2, blocking collectives, merged(): pieces = jax.tree.map(lambda part: lax.all_gather(part, axis), value)  25.5 us
    add x7, other arithmetic, combine(): acc_a * keep_a[..., None] + acc_b * keep_b[..., None]  21.7 us
    all_to_all x1, blocking collectives, shards(): lax.all_to_all(attended, 'wide', split_axis=1, concat_axis=0, tiled=True)  19.3 us
    psum x1, blocking collectives, shards(): lax.psum((jnp.sum(residual_f32, axis=1), jnp.sum(residual_f32 * residual_...  16 us
  transfers between devices with their start and end apart: 5, of which 4 were waited for; matrix products, arithmetic and copies ran while one was open for 20% of the time, Pallas kernels for 0%

commit v1 on v0

v1 whole, which is shorter than its diff:
```python
import functools

import jax
import jax.numpy as jnp
from jax import lax
from jax.experimental import pallas as pl
from jax.experimental.pallas import tpu as pltpu
from jax.sharding import PartitionSpec as P

D = 18432
HEADS = 48
HEAD = 256
WIDE = 16
NARROW = 8
RING = 4
ROWS = 384
LOCAL = ROWS // WIDE
EACH = LOCAL // NARROW
QCOLS = HEADS * HEAD // WIDE
HELD = QCOLS // HEAD
KVCOLS = 2 * HEAD // WIDE
HCOLS = QCOLS + 128
PACK = HEAD + 128
FEATS = D // NARROW
SHARE = ROWS // NARROW
UPCOLS = 36864 // WIDE

norm_eps = 1e-05
peak_eps = 1e-06

f32, bf16 = jnp.float32, jnp.bfloat16
SAME_CORE = [[w * NARROW + z * 2 + c for w in range(WIDE) for z in range(RING)] for c in range(2)]


def swap_core(x):
    return lax.ppermute(x, "narrow", [(i, i ^ 1) for i in range(NARROW)])


def shift_z(x, by):
    return lax.ppermute(x, "narrow", [(i, ((i // 2 + by) % RING) * 2 + i % 2) for i in range(NARROW)])


def spread(x):
    x = jnp.broadcast_to(x[:, None], (WIDE, RING) + x.shape[1:]).reshape((WIDE * RING,) + x.shape[1:])
    return lax.all_to_all(x, ("wide", "narrow"), 0, 0, axis_index_groups=SAME_CORE, tiled=True)


def dot(a, b):
    return jnp.dot(a, b, preferred_element_type=f32)


def full(shape):
    return pl.BlockSpec(shape, lambda *_: (0,) * len(shape))


def params(mib):
    return pltpu.CompilerParams(vmem_limit_bytes=mib * 1024 * 1024)


def cost(flops, moved):
    return pl.CostEstimate(flops=int(flops), bytes_accessed=int(moved), transcendentals=0)


def head_kernel(place, x_ref, wq_ref, wkv_ref, keep_ref, send_ref, acc_ref):
    z, c = place[0], place[1]
    tile = wq_ref.shape[1]

    def deal(terms, first):
        for lanes in range(terms.shape[1] // 128):
            acc_ref[lanes] = terms[:, lanes * 128 : (lanes + 1) * 128]
        for n in range(NARROW):
            at = lax.rem(n // 2 - z + RING, RING)
            for lanes in range(terms.shape[1] // 128):
                rows = acc_ref[lanes, pl.ds(n, SHARE, stride=NARROW), :]
                columns = pl.ds(pl.multiple_of(first + lanes * 128, 128), 128)

                @pl.when(c == n % 2)
                def _():
                    keep_ref[at, :, columns] = rows

                @pl.when(c != n % 2)
                def _():
                    send_ref[at, :, columns] = rows

    step = pl.program_id(0)
    deal(dot(x_ref[...], wq_ref[...]), step * tile)

    @pl.when(step == 0)
    def _():
        deal(jnp.concatenate([dot(x_ref[...], wkv_ref[...]), jnp.zeros((ROWS, 128 - KVCOLS), f32)], axis=1), QCOLS)


def head_terms(place, x, w_query, w_keyval):
    tile = 256
    out = jax.ShapeDtypeStruct((RING, SHARE, HCOLS), f32)
    return pl.pallas_call(
        head_kernel,
        grid_spec=pltpu.PrefetchScalarGridSpec(
            num_scalar_prefetch=1,
            grid=(QCOLS // tile,),
            in_specs=[
                full((ROWS, FEATS)),
                pl.BlockSpec((FEATS, tile), lambda i, _: (0, i)),
                full((FEATS, KVCOLS)),
            ],
            out_specs=[full(out.shape), full(out.shape)],
            scratch_shapes=[pltpu.VMEM((tile // 128, ROWS, 128), f32)],
        ),
        out_shape=[out, out],
        compiler_params=params(32),
        cost_estimate=cost(2 * ROWS * FEATS * (QCOLS + KVCOLS), 2 * FEATS * (ROWS + QCOLS + 128) + 8 * out.size),
    )(place, x, w_query, w_keyval)


def up_kernel(x_ref, w_ref, out_ref):
    out_ref[...] = dot(x_ref[...], w_ref[...]).astype(bf16)


def up_terms(x, w_up):
    tile = 384
    return pl.pallas_call(
        up_kernel,
        grid=(UPCOLS // tile,),
        in_specs=[full((ROWS, FEATS)), pl.BlockSpec((FEATS, tile), lambda i: (0, i))],
        out_specs=pl.BlockSpec((ROWS, tile), lambda i: (0, i)),
        out_shape=jax.ShapeDtypeStruct((ROWS, UPCOLS), bf16),
        compiler_params=params(32),
        cost_estimate=cost(2 * ROWS * FEATS * UPCOLS, 2 * (FEATS * (ROWS + UPCOLS) + ROWS * UPCOLS)),
    )(x, w_up)


def parts(value):
    high = value.astype(bf16).astype(f32)
    rest = value - high
    middle = rest.astype(bf16).astype(f32)
    return high, middle, (rest - middle).astype(bf16).astype(f32)


def packed(top, total):
    lane = lax.broadcasted_iota(jnp.int32, (top.shape[0], 128), 1)
    out = jnp.zeros(lane.shape, f32)
    for at, part in enumerate(parts(top) + parts(total)):
        out = jnp.where(lane == at, part, out)
    return out.astype(bf16)


def unpacked(block):
    held = block[:, HEAD:PACK].astype(f32)
    top = held[:, 0:1] + held[:, 1:2] + held[:, 2:3]
    total = held[:, 3:4] + held[:, 4:5] + held[:, 5:6]
    return block[:, :HEAD].astype(f32), top, total


def group_of(step, place):
    return lax.rem(place[0] + lax.rem(step, RING), RING) * 2 + (place[1] + step // RING) % 2


def chosen(rows, columns, source):
    made = lax.broadcasted_iota(jnp.int32, (rows, columns), 0)
    held = lax.broadcasted_iota(jnp.int32, (rows, columns), 1)
    return jnp.where(source(made) == held, 1.0, 0.0).astype(bf16)


def by_row(block):
    return dot(chosen(SHARE, SHARE, lambda i: lax.rem(i, WIDE) * EACH + i // WIDE), block)


def heads_of(rows):
    return jnp.concatenate([rows[:, h * HEAD : (h + 1) * HEAD] for h in range(HELD)], axis=0)


def attend_kernel(place, lengths, q_ref, k_ref, v_ref, keep_ref, send_ref):
    step = pl.program_id(0)
    group = group_of(step, place)
    start = (place[0] * 2 + place[1]) * k_ref.shape[2]
    rows = by_row(q_ref[0])
    for j in range(EACH):
        query = heads_of(rows[j * WIDE : (j + 1) * WIDE]).astype(bf16)
        scores = lax.dot_general(query, k_ref[j, 0], (((1,), (1,)), ((), ())), preferred_element_type=f32)
        scores = scores * (1.0 / HEAD**0.5)
        position = lax.broadcasted_iota(jnp.int32, scores.shape, 1) + start
        valid = position < lengths[j * NARROW + group]
        masked = jnp.where(valid, scores, f32(-1e30))
        top = jnp.max(masked, axis=1, keepdims=True)
        probs = jnp.where(valid, jnp.exp(masked - top), f32(0.0))
        total = jnp.sum(probs, axis=1, keepdims=True)
        value = dot(probs.astype(bf16), v_ref[j, 0]).astype(bf16)
        block = jnp.concatenate([value, packed(top, total)], axis=1)
        span = slice(j * HEADS, (j + 1) * HEADS)

        @pl.when(step < RING)
        def _():
            keep_ref[lax.rem(step, RING), span, :] = block

        @pl.when(step >= RING)
        def _():
            send_ref[lax.rem(step, RING), span, :] = block


def attend(place, lengths, query, k_cache, v_cache):
    positions = k_cache.shape[1]
    k_cache = k_cache.reshape(EACH, NARROW, positions, HEAD)
    v_cache = v_cache.reshape(EACH, NARROW, positions, HEAD)
    cache = pl.BlockSpec((EACH, 1, positions, HEAD), lambda i, place, _: (0, group_of(i, place), 0, 0))
    out = jax.ShapeDtypeStruct((RING, EACH * HEADS, PACK), bf16)
    return pl.pallas_call(
        attend_kernel,
        grid_spec=pltpu.PrefetchScalarGridSpec(
            num_scalar_prefetch=2,
            grid=(NARROW,),
            in_specs=[
                pl.BlockSpec(
                    (1, SHARE, HCOLS),
                    lambda i, place, _: ((i // RING) * RING + lax.rem(place[0] + lax.rem(i, RING), RING), 0, 0),
                ),
                cache,
                cache,
            ],
            out_specs=[full(out.shape), full(out.shape)],
        ),
        out_shape=[out, out],
        compiler_params=params(32),
        cost_estimate=cost(4 * LOCAL * HEADS * positions * HEAD, 4 * k_cache.size + 4 * out.size + 2 * query.size),
    )(place, lengths, query, k_cache, v_cache)


def joined(first, second):
    value_a, top_a, total_a = first
    value_b, top_b, total_b = second
    both = jnp.maximum(top_a, top_b)
    keep_a = jnp.exp(top_a - both)
    keep_b = jnp.exp(top_b - both)
    return value_a * keep_a + value_b * keep_b, both, total_a * keep_a + total_b * keep_b


def pair_kernel(a_ref, b_ref, *out_refs):
    for at, out_ref in enumerate(out_refs):
        value, top, total = joined(unpacked(a_ref[at]), unpacked(b_ref[at]))
        out_ref[...] = jnp.concatenate([value.astype(bf16), packed(top, total)], axis=1)


def pair(a, b):
    out = jax.ShapeDtypeStruct(a.shape[1:], bf16)
    return pl.pallas_call(
        pair_kernel,
        out_shape=[out] * RING,
        compiler_params=params(32),
        cost_estimate=cost(4 * a.size, 6 * a.size),
    )(a, b)


def row_of(block):
    spot = lax.broadcasted_iota(jnp.int32, (KVCOLS, HEAD), 0)
    lane = lax.broadcasted_iota(jnp.int32, (KVCOLS, HEAD), 1)
    tiled = dot(block, (lax.rem(lane, KVCOLS) == spot).astype(bf16))
    row = lax.broadcasted_iota(jnp.int32, tiled.shape, 0)
    lane = lax.broadcasted_iota(jnp.int32, tiled.shape, 1)
    return jnp.sum(jnp.where(lane // KVCOLS == row, tiled, 0.0), axis=0, keepdims=True)


def finish_kernel(q_ref, peak_ref, *refs):
    blocks, out_ref = refs[:RING], refs[RING]
    rows = by_row(q_ref[...])
    made = []
    for j in range(EACH):
        mine = rows[j * WIDE : (j + 1) * WIDE]
        query = heads_of(mine)
        keyval = mine[:, QCOLS : QCOLS + KVCOLS].astype(bf16)
        new_key = row_of(keyval[: WIDE // 2])
        new_value = row_of(keyval[WIDE // 2 :])
        own = jnp.sum(query * new_key, axis=1, keepdims=True) * (1.0 / HEAD**0.5)
        span = slice(j * HEADS, (j + 1) * HEADS)
        value, top, total = functools.reduce(joined, [unpacked(ref[span, :]) for ref in blocks])
        both = jnp.maximum(top, own)
        keep = jnp.exp(top - both)
        fresh = jnp.exp(own - both)
        mass = total * keep + fresh
        done = ((value * keep + fresh.astype(bf16).astype(f32) * new_value) / mass).astype(bf16)
        made.append(jnp.concatenate([done[h * WIDE : (h + 1) * WIDE] for h in range(HELD)], axis=1))
    each = EACH + 1
    order = chosen(WIDE * each, SHARE, lambda i: jnp.where(lax.rem(i, each) < EACH, lax.rem(i, each) * WIDE + i // each, -1))
    made = dot(order, jnp.concatenate(made, axis=0))
    peaks = jnp.concatenate(parts(peak_ref[...]) + (jnp.zeros((1, QCOLS - 3 * 128), f32),), axis=1)
    row = lax.broadcasted_iota(jnp.int32, made.shape, 0)
    out_ref[...] = jnp.where(lax.rem(row, each) == EACH, peaks, made).astype(bf16)


def finish(query, peak, blocks):
    out = (WIDE * (EACH + 1), QCOLS)
    return pl.pallas_call(
        finish_kernel,
        out_shape=jax.ShapeDtypeStruct(out, bf16),
        compiler_params=params(32),
        cost_estimate=cost(40 * blocks[0].size, 10 * blocks[0].size),
    )(query, peak, *blocks)


def out_kernel(place, own_ref, other_ref, w_ref, out_ref, rows_ref):
    @pl.when(pl.program_id(0) == 0)
    def _():
        shape = (ROWS, own_ref.shape[0])
        made = lax.broadcasted_iota(jnp.int32, shape, 0)
        held = lax.broadcasted_iota(jnp.int32, shape, 1)
        local = lax.rem(made, LOCAL)
        group = lax.rem(local, NARROW)
        source = ((made // LOCAL) * RING + group // 2) * (EACH + 1) + local // NARROW
        total = jnp.zeros((ROWS, QCOLS), f32)
        for core, ref in ((place[1], own_ref), (1 - place[1], other_ref)):
            pick = jnp.where(source == held, jnp.where(lax.rem(group, 2) == core, 1.0, 0.0), 0.0)
            total += dot(pick.astype(bf16), ref[...])
        rows_ref[...] = total.astype(bf16)

    out_ref[...] = dot(rows_ref[...], w_ref[...]).astype(bf16)


def out_terms(place, own, other, w_out):
    tile = 384
    return pl.pallas_call(
        out_kernel,
        grid_spec=pltpu.PrefetchScalarGridSpec(
            num_scalar_prefetch=1,
            grid=(FEATS // tile,),
            in_specs=[full(own.shape), full(own.shape), pl.BlockSpec((QCOLS, tile), lambda i, _: (0, i))],
            out_specs=pl.BlockSpec((ROWS, tile), lambda i, _: (0, i)),
            scratch_shapes=[pltpu.VMEM((ROWS, QCOLS), bf16)],
        ),
        out_shape=jax.ShapeDtypeStruct((ROWS, FEATS), bf16),
        compiler_params=params(32),
        cost_estimate=cost(2 * ROWS * QCOLS * FEATS, 2 * (QCOLS * FEATS + ROWS * FEATS)),
    )(place, own, other, w_out)


def shards(residual, ln_gain, w_query, w_keyval, w_out, w_up, k_cache, v_cache, lengths):
    narrow = lax.axis_index("narrow")
    place = jnp.stack([narrow // 2, narrow % 2]).astype(jnp.int32)
    residual_f32 = residual.astype(f32)
    sums = jnp.stack([jnp.sum(residual_f32, axis=1), jnp.sum(residual_f32 * residual_f32, axis=1)])
    sums = sums + swap_core(sums)
    sums = sums + shift_z(sums, 1) + shift_z(sums, 2) + shift_z(sums, 3)
    mean = sums[0] / D
    variance = sums[1] / D - mean * mean
    normed = (
        (residual_f32 - mean[:, None]) * lax.rsqrt(variance + norm_eps)[:, None] * ln_gain[None, :]
    ).astype(bf16)
    rows = lax.all_to_all(jnp.broadcast_to(normed[None], (WIDE,) + normed.shape), "wide", 0, 0, tiled=True)
    rows = rows.reshape(ROWS, FEATS)

    keep, send = head_terms(place, rows, w_query, w_keyval)
    both = keep + swap_core(send)
    query = (both[0] + shift_z(both[1], 1) + shift_z(both[2], 2) + shift_z(both[3], 3)).astype(bf16)

    up = lax.psum_scatter(up_terms(rows, w_up), "narrow", scatter_dimension=0, tiled=True).astype(f32)
    peak = jnp.max(jnp.abs(up), axis=1)

    query = spread(query.reshape(WIDE, EACH, HCOLS)).reshape(WIDE, RING, EACH, HCOLS)
    query = query.transpose(1, 0, 2, 3).reshape(RING, SHARE, HCOLS)
    query = jnp.concatenate([query, swap_core(query)])
    keep, send = attend(place, lengths, query, k_cache, v_cache)
    blocks = pair(keep, swap_core(send))
    blocks = [blocks[0]] + [shift_z(blocks[d], d) for d in range(1, RING)]
    mine = lax.dynamic_index_in_dim(query, place[0], keepdims=False)
    attended = finish(mine, jnp.pad(peak, (0, 128 - SHARE))[None], blocks)

    own = spread(attended.reshape(WIDE, EACH + 1, QCOLS))
    peaks = lax.dynamic_index_in_dim(own.reshape(WIDE, RING, EACH + 1, QCOLS)[:, :, EACH], place[0], 1, keepdims=False)
    peaks = peaks.astype(f32)
    peaks = peaks[:, :SHARE] + peaks[:, 128 : 128 + SHARE] + peaks[:, 256 : 256 + SHARE]
    peak = jnp.max(peaks, axis=0)
    own = own.reshape(WIDE * RING * (EACH + 1), QCOLS)
    projected = out_terms(place, own, swap_core(own), w_out)
    projected = lax.all_to_all(projected.reshape(WIDE, LOCAL, FEATS), "wide", 0, 0, tiled=True)
    mixed = (residual_f32 + jnp.sum(projected.astype(f32), axis=0)).astype(bf16)
    scaled = (up / (peak + peak_eps)[:, None]).astype(bf16)
    return (mixed, scaled, peak)


def solution(mesh):
    placed = (
        P("wide", "narrow"),
        P("narrow"),
        P("narrow", "wide"),
        P("narrow", "wide"),
        P("wide", "narrow"),
        P("narrow", "wide"),
        P("wide", "narrow", None),
        P("wide", "narrow", None),
        P("wide"),
    )
    return jax.shard_map(
        shards,
        mesh=mesh,
        in_specs=placed,
        out_specs=(P("wide", "narrow"), P("narrow", "wide"), P("narrow")),
        check_vma=False,
    )
```

time: 361 us -> 213 us (0.59)
  blocking collectives: 151 us -> 65.4 us
  other arithmetic: 46.9 us -> 5.13 us
  waiting for transfers between devices: 92.7 us -> 51.3 us
  Pallas kernels: 0 us -> 35.5 us
  matrix products: 26.5 us -> 0 us
  starting transfers between devices: 5.32 us -> 19.4 us
    psum x2 -> x0, blocking collectives: 68.8 us -> none  [the longest x1 52.9 us: shards(): summed = lax.psum(head_terms, 'narrow').astype(jnp.bfloat16)]
    all_gather x2 -> x0, waiting for transfers between devices: 48.8 us -> none  [the longest x1 43.5 us: shards(): piece = lax.all_gather(normed, 'wide', axis=0, tiled=True)]
    all_to_all x1 -> x3, blocking collectives: 19.3 us -> 65.4 us  [the longest x2 35.2 us: spread(): lax.all_to_all(x, ('wide', 'narrow'), 0, 0, axis_index_groups=SAME_CORE,...]
    pmax x1 -> x0, blocking collectives: 37.3 us -> none  [shards(): peak = lax.pmax(jnp.max(jnp.abs(up), axis=1), 'wide')]
    pallas_call x0 -> x6, Pallas kernels: none -> 35.5 us  [the longest x1 12.4 us: attend(): pl.pallas_call(attend_kernel, grid_spec=pltpu.PrefetchScalarGridSpec(num_...]
    unnamed x5 -> x1, waiting for transfers between devices: 32.9 us -> 0.02 us
    add x16 -> x4, other arithmetic: 31.2 us -> 0.09 us  [the longest x1 0.07 us: shards(): both = keep + swap_core(send)]
    dot_general x7 -> x0, matrix products: 26.5 us -> none  [the longest x1 10.6 us: shards(): jnp.dot(piece, w_up, preferred_element_type=jnp.float32)]
  transfers between devices with their start and end apart: 5 -> 16, of which waited for: 4 -> 12; matrix products, arithmetic and copies ran while one was open for 20% -> 2% of each run, Pallas kernels for 0% -> 9%
where the time goes in v1:
time: 213 us; the launch traced here: 212 us
  blocking collectives  65.4 us (31%)
  waiting for transfers between devices  51.3 us (24%)
  Pallas kernels  35.5 us (17%)
  local copies, waits for them, and re-layouts  21.2 us (10%)
  starting transfers between devices  19.4 us (9%)
  between operations  14.4 us (7%)
  other arithmetic  5.13 us (2%)
    all_to_all x2, blocking collectives, spread(): lax.all_to_all(x, ('wide', 'narrow'), 0, 0, axis_index_groups=SAME_CORE,...  35.2 us
    all_to_all x1, blocking collectives, shards(): lax.all_to_all(jnp.broadcast_to(normed[None], (WIDE,) + normed.shape), 'w...  30.2 us
    all_to_all x1, waiting for transfers between devices, shards(): lax.all_to_all(projected.reshape(WIDE, LOCAL, FEATS), 'wide', 0, 0, tiled...  26.3 us
    ppermute x9, waiting for transfers between devices, shift_z(): lax.ppermute(x, 'narrow', [(i, (i // 2 + by) % RING * 2 + i % 2) for i in...  17.9 us
    ppermute x9, starting transfers between devices, shift_z(): lax.ppermute(x, 'narrow', [(i, (i // 2 + by) % RING * 2 + i % 2) for i in...  15.1 us
    unnamed x40, local copies, waits for them, and re-layouts  14.4 us
    pallas_call x1, Pallas kernels, attend(): pl.pallas_call(attend_kernel, grid_spec=pltpu.PrefetchScalarGridSpec(num_...  12.4 us
    pallas_call x1, Pallas kernels, up_terms(): pl.pallas_call(up_kernel, grid=(UPCOLS // tile,), in_specs=[full((ROWS, F...  8.42 us
  transfers between devices with their start and end apart: 16, of which 12 were waited for; matrix products, arithmetic and copies ran while one was open for 2% of the time, Pallas kernels for 9%

profile of v1, /device:TPU:0, one launch (start us, length us, event | category | flops | bytes accessed | tf_op | source)
XLA Modules:
  0.0 212.3 jit_solution(4736265913194320660)
XLA Ops:
  7.2 1.0 convert_reduce_fusion.1
  8.3 0.1 collective-permute-start
  8.3 1.1 collective-permute-done
  9.5 2.1 collective-permute-start.1
  11.6 3.6 %collective-permute-start.2 = (f32[2,24]{1,0:T(2,128)S(1)}, f32[2,24]{1,0:T(2,128)S(1)}, u32[]{:S(2)}, u32[]{:S(2)}) collective-permute-start(f32[2,24]{1,0:T(2,128)S(1)} %fusion.14), channel_id=1, source_target_pairs={{0,4},{1,5},{2,6},{3,7},{4,0},{5,1},{6,2},{7,3},{8,12},{9,13},{10,... | collective-permute-start | bytes 584 | tf_op jit(solution)/shard_map/ppermute | solution.py:40
  15.1 1.0 collective-permute-start.3
  16.2 0.5 collective-permute-done.2
  16.7 2.0 collective-permute-done.3
  18.7 1.0 fusion.5
  19.8 0.1 broadcast_in_dim.12
  19.9 30.2 %all_to_all.20 = bf16[16,24,2304]{2,1,0:T(8,128)(2,1)S(1)} all-to-all(bf16[16,24,2304]{2,1,0:T(8,128)(2,1)S(1)} %broadcast_in_dim.12), channel_id=1, replica_groups=mesh['wide'=16,'narrow'=8] {'wide'}, dimensions={0} | all-to-all | bytes 3538944 | tf_op jit(solution)/shard_map/all_to_all | solution.py:345
  50.1 4.0 %copy-done.13 = bf16[2304,2304]{1,0:T(8,128)(2,1)S(1)} copy-done((bf16[2304,2304]{1,0:T(8,128)(2,1)S(1)}, bf16[2304,2304]{1,0:T(8,128)(2,1)}, u32[]{:S(2)}) %copy-start.13) | copy-done | bytes 10616856
  54.1 8.4 %shard_map.113 = bf16[384,2304]{1,0:T(8,128)(2,1)} custom-call(bf16[384,2304]{1,0:T(8,128)(2,1)S(1)} %bitcast.49, bf16[2304,2304]{1,0:T(8,128)(2,1)S(1)} %copy-done.13), custom_call_target="tpu_custom_call" | custom-call | flops 4076863488 | bytes 14155776 | tf_op jit(solution)/shard_map/pallas_call | solution.py:121
  62.5 0.3 copy.18.wkv_ref
  62.9 0.1 pad_add_fusion.place
  63.0 2.0 copy-done.1
  65.0 4.1 %shard_map.112 = (f32[4,48,896]{2,1,0:T(8,128)S(1)}, f32[4,48,896]{2,1,0:T(8,128)S(1)}) custom-call(s32[2]{0:T(128)S(1)} %pad_add_fusion.place, bf16[384,2304]{1,0:T(8,128)(2,1)S(1)} %bitcast.50, bf16[2304,768]{1,0:T(8,128)(2,1)S(1)} %copy-done.1, bf16[2304,32]{1,0:T(8,128)(2,1)S(1)} %copy.18.wkv_ref), custom_call_target="tpu_custom_call" | custom-call | flops 1415577600 | bytes 7274496 | tf_op jit(solution)/shard_map/pallas_call | solution.py:96
  69.1 0.1 collective-permute-start.4
  69.2 2.1 %collective-permute-done.4 = f32[4,48,896]{2,1,0:T(8,128)S(1)} collective-permute-done((f32[4,48,896]{2,1,0:T(8,128)S(1)}, f32[4,48,896]{2,1,0:T(8,128)S(1)}, u32[]{:S(2)}, u32[]{:S(2)}) %collective-permute-start.4) | collective-permute-done | bytes 688160 | tf_op jit(solution)/shard_map/ppermute | solution.py:36
  71.3 0.1 add.73
  71.4 0.2 collective-permute-start.5
  71.7 3.5 %collective-permute-start.6 = (f32[48,896]{1,0:T(8,128)S(1)}, f32[48,896]{1,0:T(8,128)S(1)}, u32[]{:S(2)}, u32[]{:S(2)}) collective-permute-start(f32[48,896]{1,0:T(8,128)S(1)} %get-tuple-element.23), channel_id=1, source_target_pairs={{0,4},{1,5},{2,6},{3,7},{4,0},{5,1},{6,2},{7,3},{8,12},{9,13},{10,... | collective-permute-start | bytes 516104 | tf_op jit(solution)/shard_map/ppermute | solution.py:40
  75.2 0.7 collective-permute-start.7
  75.9 4.0 %collective-permute-done.5 = f32[48,896]{1,0:T(8,128)S(1)} collective-permute-done((f32[48,896]{1,0:T(8,128)S(1)}, f32[48,896]{1,0:T(8,128)S(1)}, u32[]{:S(2)}, u32[]{:S(2)}) %collective-permute-start.5) | collective-permute-done | bytes 172064 | tf_op jit(solution)/shard_map/ppermute | solution.py:40
  79.9 6.8 %collective-permute-done.6 = f32[48,896]{1,0:T(8,128)S(1)} collective-permute-done((f32[48,896]{1,0:T(8,128)S(1)}, f32[48,896]{1,0:T(8,128)S(1)}, u32[]{:S(2)}, u32[]{:S(2)}) %collective-permute-start.6) | collective-permute-done | bytes 172064 | tf_op jit(solution)/shard_map/ppermute | solution.py:40
  86.8 0.1 broadcast_in_dim.14
  86.9 17.1 %all_to_all.21 = bf16[64,3,896]{2,1,0:T(4,128)(2,1)S(1)} all-to-all(bf16[64,3,896]{2,1,0:T(4,128)(2,1)S(1)} %bitcast.55), channel_id=1, replica_groups={{0,2,4,6,8,10,12,14,16,18,20,22,24,26,28,30,32,34,36,38,40,42,44,46,48,..., dimensions={0} | all-to-all | bytes 688128 | tf_op jit(solution)/shard_map/all_to_all | solution.py:45
  104.0 0.1 copy.20
  104.2 0.1 fusion.15
  104.3 0.1 collective-permute-start.8
  104.4 1.6 collective-permute-done.8
  106.1 2.1 copy-done.3
  108.2 12.4 %shard_map.114 = (bf16[4,144,384]{2,1,0:T(8,128)(2,1)S(1)}, bf16[4,144,384]{2,1,0:T(8,128)(2,1)}) custom-call(s32[2]{0:T(128)S(1)} %pad_add_fusion.place, s32[24]{0:T(128)S(1)} %copy-done.12, bf16[8,48,896]{2,1,0:T(8,128)(2,1)S(1)} %constant_dynamic-update-slice_fusion.q_ref, bf16[3,8,256,256]{3,2,1,0:T(8,128)(2,1)S(1)} %bitcast.51, ...), custom_call_target="tpu_custom_call" | custom-call | flops 301989888 | bytes 7864320 | tf_op jit(solution)/shard_map/pallas_call | solution.py:206
  120.6 0.8 copy-done.6
  121.4 0.1 collective-permute-start.9
  121.5 1.7 dynamic-slice_bitcast_fusion.q_ref
  123.2 0.3 collective-permute-done.9.b_ref
  123.5 1.0 copy-done.7
  124.5 2.9 %shard_map.115 = (bf16[144,384]{1,0:T(8,128)(2,1)S(1)}, bf16[144,384]{1,0:T(8,128)(2,1)}, bf16[144,384]{1,0:T(8,128)(2,1)}, bf16[144,384]{1,0:T(8,128)(2,1)}) custom-call(bf16[4,144,384]{2,1,0:T(8,128)(2,1)S(1)} %copy-done.7, bf16[4,144,384]{2,1,0:T(8,128)(2,1)} %collective-permute-done.9.b_ref), custom_call_target="tpu_custom_call" | custom-call | flops 884736 | bytes 1327104 | tf_op jit(solution)/shard_map/pallas_call | solution.py:244
  127.4 0.6 copy-done.10
  128.1 0.6 collective-permute-start.10
  128.7 1.8 collective-permute-start.11
  130.5 1.5 collective-permute-start.12
  132.0 1.1 fusion
  133.1 4.0 %collective-permute-done.10.refs_1_ = bf16[144,384]{1,0:T(8,128)(2,1)} collective-permute-done((bf16[144,384]{1,0:T(8,128)(2,1)}, bf16[144,384]{1,0:T(8,128)(2,1)}, u32[]{:S(2)}, u32[]{:S(2)}) %collective-permute-start.10) | collective-permute-done | bytes 110624 | tf_op jit(solution)/shard_map/ppermute | solution.py:40
  137.0 0.6 collective-permute-done.12.refs_3_
  137.6 0.9 copy-done.9
  138.5 0.9 copy-done.11
  139.4 1.9 shard_map.116
  141.3 0.6 copy-done.8
  141.9 1.6 broadcast_in_dim.31
  143.5 1.0 broadcast_in_dim.32
  144.5 18.1 %all_to_all.22 = bf16[64,4,768]{2,1,0:T(4,128)(2,1)} all-to-all(bf16[64,4,768]{2,1,0:T(4,128)(2,1)S(1)} %bitcast.56), channel_id=1, replica_groups={{0,2,4,6,8,10,12,14,16,18,20,22,24,26,28,30,32,34,36,38,40,42,44,46,48,..., dimensions={0} | all-to-all | bytes 786432 | tf_op jit(solution)/shard_map/all_to_all | solution.py:45
  162.6 1.8 reshape.75.own_ref
  164.4 1.9 collective-permute-done.13.other_ref
  166.3 1.0 copy-done.5
  167.3 5.8 %shard_map.117 = bf16[384,2304]{1,0:T(8,128)(2,1)} custom-call(s32[2]{0:T(128)S(1)} %pad_add_fusion.place, bf16[256,768]{1,0:T(8,128)(2,1)S(1)} %copy-done.5, bf16[256,768]{1,0:T(8,128)(2,1)S(1)} %collective-permute-done.13.other_ref, bf16[768,2304]{1,0:T(8,128)(2,1)S(1)} %copy-done), custom_call_target="tpu_custom_call" | custom-call | flops 1358954496 | bytes 5308416 | tf_op jit(solution)/shard_map/pallas_call | solution.py:318
  173.2 3.8 %all-to-all-start.3 = ((bf16[16,24,2304]{2,1,0:T(8,128)(2,1)}), bf16[16,24,2304]{2,1,0:T(8,128)(2,1)S(1)}, u32[]{:S(2)}, u32[]{:S(2)}) async-start(bf16[16,24,2304]{2,1,0:T(8,128)(2,1)} %bitcast.21), calls=%async_computation.4 | async-start | bytes 3538944 | tf_op jit(solution)/shard_map/all_to_all | solution.py:371
  177.0 0.2 slice.44
  177.3 0.1 dynamic-slice_convert_fusion
  177.4 0.8 fusion.1
  178.2 26.3 %all-to-all-done.3 = bf16[16,24,2304]{2,1,0:T(8,128)(2,1)S(1)} async-done(((bf16[16,24,2304]{2,1,0:T(8,128)(2,1)}), bf16[16,24,2304]{2,1,0:T(8,128)(2,1)S(1)}, u32[]{:S(2)}, u32[]{:S(2)}) %all-to-all-start.3) | async-done | bytes 1769504 | tf_op jit(solution)/shard_map/all_to_all | solution.py:371
  204.5 0.2 convert_reduce_fusion
  204.8 0.7 fusion.6
  (48 shorter events, 0.4 us)
Async XLA Ops:
  7.2 124.8 %reduce-scatter.2.cloned.1.call-start = ((), (), s32[]{:S(2)}) async-start(), calls=%async_computation.5 | async-start | bytes 1990656 | tf_op jit(solution)/shard_map/reduce_scatter | solution.py:352
  8.3 1.2 collective-permute-start
  9.5 6.7 %collective-permute-start.1 = (f32[2,24]{1,0:T(2,128)S(1)}, f32[2,24]{1,0:T(2,128)S(1)}, u32[]{:S(2)}, u32[]{:S(2)}) collective-permute-start(f32[2,24]{1,0:T(2,128)S(1)} %fusion.14), channel_id=1, source_target_pairs={{0,2},{1,3},{2,4},{3,5},{4,6},{5,7},{6,0},{7,1},{8,10},{9,11},{10,... | collective-permute-start | bytes 584 | tf_op jit(solution)/shard_map/ppermute | solution.py:40
  11.6 5.1 %collective-permute-start.2 = (f32[2,24]{1,0:T(2,128)S(1)}, f32[2,24]{1,0:T(2,128)S(1)}, u32[]{:S(2)}, u32[]{:S(2)}) collective-permute-start(f32[2,24]{1,0:T(2,128)S(1)} %fusion.14), channel_id=1, source_target_pairs={{0,4},{1,5},{2,6},{3,7},{4,0},{5,1},{6,2},{7,3},{8,12},{9,13},{10,... | collective-permute-start | bytes 584 | tf_op jit(solution)/shard_map/ppermute | solution.py:40
  15.1 3.6 %collective-permute-start.3 = (f32[2,24]{1,0:T(2,128)S(1)}, f32[2,24]{1,0:T(2,128)S(1)}, u32[]{:S(2)}, u32[]{:S(2)}) collective-permute-start(f32[2,24]{1,0:T(2,128)S(1)} %fusion.14), channel_id=1, source_target_pairs={{0,6},{1,7},{2,0},{3,1},{4,2},{5,3},{6,4},{7,5},{8,14},{9,15},{10,... | collective-permute-start | bytes 584 | tf_op jit(solution)/shard_map/ppermute | solution.py:40
  50.1 4.0 %copy-start.13 = (bf16[2304,2304]{1,0:T(8,128)(2,1)S(1)}, bf16[2304,2304]{1,0:T(8,128)(2,1)}, u32[]{:S(2)}) copy-start(bf16[2304,2304]{1,0:T(8,128)(2,1)} %w_ref.2) | copy-start | bytes 31850500
  54.1 8.5 %copy-start.17 = (bf16[2304,32]{0,1:T(8,128)(2,1)S(1)}, bf16[2304,32]{0,1:T(8,128)(2,1)}, u32[]{:S(2)}) copy-start(bf16[2304,32]{0,1:T(8,128)(2,1)} %param.12) | copy-start | bytes 442372
  63.0 2.0 copy-start.1
  69.1 2.2 %collective-permute-start.4 = (f32[4,48,896]{2,1,0:T(8,128)S(1)}, f32[4,48,896]{2,1,0:T(8,128)S(1)}, u32[]{:S(2)}, u32[]{:S(2)}) collective-permute-start(f32[4,48,896]{2,1,0:T(8,128)S(1)} %get-tuple-element.12), channel_id=1, source_target_pairs={{0,1},{1,0},{2,3},{3,2},{4,5},{5,4},{6,7},{7,6},{8,9},{9,8},{10,11... | collective-permute-start | bytes 2064392 | tf_op jit(solution)/shard_map/ppermute | solution.py:36
  71.4 34.7 %copy-start.2 = (bf16[24,256,256]{2,1,0:T(8,128)(2,1)S(1)}, bf16[24,256,256]{2,1,0:T(8,128)(2,1)}, u32[]{:S(2)}) copy-start(bf16[24,256,256]{2,1,0:T(8,128)(2,1)} %param.15) | copy-start | bytes 9437188
  71.4 34.7 %copy-start.12 = (s32[24]{0:T(128)S(1)}, s32[24]{0:T(128)}, u32[]{:S(2)}) copy-start(s32[24]{0:T(128)} %lengths.1) | copy-start | bytes 292
  71.4 8.5 %collective-permute-start.5 = (f32[48,896]{1,0:T(8,128)S(1)}, f32[48,896]{1,0:T(8,128)S(1)}, u32[]{:S(2)}, u32[]{:S(2)}) collective-permute-start(f32[48,896]{1,0:T(8,128)S(1)} %get-tuple-element.21), channel_id=1, source_target_pairs={{0,2},{1,3},{2,4},{3,5},{4,6},{5,7},{6,0},{7,1},{8,10},{9,11},{10,... | collective-permute-start | bytes 516104 | tf_op jit(solution)/shard_map/ppermute | solution.py:40
  71.7 15.0 %collective-permute-start.6 = (f32[48,896]{1,0:T(8,128)S(1)}, f32[48,896]{1,0:T(8,128)S(1)}, u32[]{:S(2)}, u32[]{:S(2)}) collective-permute-start(f32[48,896]{1,0:T(8,128)S(1)} %get-tuple-element.23), channel_id=1, source_target_pairs={{0,4},{1,5},{2,6},{3,7},{4,0},{5,1},{6,2},{7,3},{8,12},{9,13},{10,... | collective-permute-start | bytes 516104 | tf_op jit(solution)/shard_map/ppermute | solution.py:40
  75.2 11.5 %collective-permute-start.7 = (f32[48,896]{1,0:T(8,128)S(1)}, f32[48,896]{1,0:T(8,128)S(1)}, u32[]{:S(2)}, u32[]{:S(2)}) collective-permute-start(f32[48,896]{1,0:T(8,128)S(1)} %get-tuple-element.22), channel_id=1, source_target_pairs={{0,6},{1,7},{2,0},{3,1},{4,2},{5,3},{6,4},{7,5},{8,14},{9,15},{10,... | collective-permute-start | bytes 516104 | tf_op jit(solution)/shard_map/ppermute | solution.py:40
  104.3 1.7 collective-permute-start.8
  106.0 14.5 %copy-start.4 = (bf16[8,48,896]{2,1,0:T(8,128)(2,1)}, bf16[8,48,896]{2,1,0:T(8,128)(2,1)S(1)}, u32[]{:S(2)}) copy-start(bf16[8,48,896]{2,1,0:T(8,128)(2,1)S(1)} %constant_dynamic-update-slice_fusion.q_ref) | copy-start | bytes 2064388
  106.1 2.1 %copy-start.3 = (bf16[24,256,256]{2,1,0:T(8,128)(2,1)S(1)}, bf16[24,256,256]{2,1,0:T(8,128)(2,1)}, u32[]{:S(2)}) copy-start(bf16[24,256,256]{2,1,0:T(8,128)(2,1)} %param.16) | copy-start | bytes 9437188
  120.6 0.8 copy-start.6
  121.4 45.0 %copy-start = (bf16[768,2304]{1,0:T(8,128)(2,1)S(1)}, bf16[768,2304]{1,0:T(8,128)(2,1)}, u32[]{:S(2)}) copy-start(bf16[768,2304]{1,0:T(8,128)(2,1)} %w_ref.3) | copy-start | bytes 10616836
  121.4 2.1 %collective-permute-start.9 = (bf16[4,144,384]{2,1,0:T(8,128)(2,1)}, bf16[4,144,384]{2,1,0:T(8,128)(2,1)}, u32[]{:S(2)}, u32[]{:S(2)}) collective-permute-start(bf16[4,144,384]{2,1,0:T(8,128)(2,1)} %get-tuple-element.14), channel_id=1, source_target_pairs={{0,1},{1,0},{2,3},{3,2},{4,5},{5,4},{6,7},{7,6},{8,9},{9,8},{10,11... | collective-permute-start | bytes 1327112 | tf_op jit(solution)/shard_map/ppermute | solution.py:36
  123.5 1.0 copy-start.7
  127.4 0.6 copy-start.10
  128.1 9.0 %collective-permute-start.10 = (bf16[144,384]{1,0:T(8,128)(2,1)}, bf16[144,384]{1,0:T(8,128)(2,1)}, u32[]{:S(2)}, u32[]{:S(2)}) collective-permute-start(bf16[144,384]{1,0:T(8,128)(2,1)} %get-tuple-element.16), channel_id=1, source_target_pairs={{0,2},{1,3},{2,4},{3,5},{4,6},{5,7},{6,0},{7,1},{8,10},{9,11},{10,... | collective-permute-start | bytes 331784 | tf_op jit(solution)/shard_map/ppermute | solution.py:40
  128.7 8.4 %collective-permute-start.11 = (bf16[144,384]{1,0:T(8,128)(2,1)}, bf16[144,384]{1,0:T(8,128)(2,1)}, u32[]{:S(2)}, u32[]{:S(2)}) collective-permute-start(bf16[144,384]{1,0:T(8,128)(2,1)} %get-tuple-element.17), channel_id=1, source_target_pairs={{0,4},{1,5},{2,6},{3,7},{4,0},{5,1},{6,2},{7,3},{8,12},{9,13},{10,... | collective-permute-start | bytes 331784 | tf_op jit(solution)/shard_map/ppermute | solution.py:40
  130.5 7.1 %collective-permute-start.12 = (bf16[144,384]{1,0:T(8,128)(2,1)}, bf16[144,384]{1,0:T(8,128)(2,1)}, u32[]{:S(2)}, u32[]{:S(2)}) collective-permute-start(bf16[144,384]{1,0:T(8,128)(2,1)} %get-tuple-element.18), channel_id=1, source_target_pairs={{0,6},{1,7},{2,0},{3,1},{4,2},{5,3},{6,4},{7,5},{8,14},{9,15},{10,... | collective-permute-start | bytes 331784 | tf_op jit(solution)/shard_map/ppermute | solution.py:40
  137.6 0.9 copy-start.9
  138.5 0.9 copy-start.11
  141.3 0.6 copy-start.8
  164.4 1.9 collective-permute-start.13
  166.3 1.0 copy-start.5
  173.2 3.9 %copy-start.14 = (bf16[64,4,768]{2,1,0:T(4,128)(2,1)S(1)}, bf16[64,4,768]{2,1,0:T(4,128)(2,1)}, u32[]{:S(2)}) copy-start(bf16[64,4,768]{2,1,0:T(4,128)(2,1)} %all_to_all.22) | copy-start | bytes 1179652
  173.2 4.2 %copy-start.16 = (bf16[48,2304]{1,0:T(8,128)(2,1)S(1)}, bf16[48,2304]{1,0:T(8,128)(2,1)}, u32[]{:S(2)}) copy-start(bf16[48,2304]{1,0:T(8,128)(2,1)} %reduce-scatter.2.cloned.1.call-done) | copy-start | bytes 663556
  173.2 31.6 %copy-start.15 = (bf16[24,2304]{1,0:T(8,128)(2,1)S(1)}, bf16[24,2304]{1,0:T(8,128)(2,1)}, u32[]{:S(2)}) copy-start(bf16[24,2304]{1,0:T(8,128)(2,1)} %param.9) | copy-start | bytes 331780
  173.2 31.3 %all-to-all-start.3 = ((bf16[16,24,2304]{2,1,0:T(8,128)(2,1)}), bf16[16,24,2304]{2,1,0:T(8,128)(2,1)S(1)}, u32[]{:S(2)}, u32[]{:S(2)}) async-start(bf16[16,24,2304]{2,1,0:T(8,128)(2,1)} %bitcast.21), calls=%async_computation.4 | async-start | bytes 3538944 | tf_op jit(solution)/shard_map/all_to_all | solution.py:371
  177.4 28.0 %copy-start.18 = (f32[48]{0:T(128)}, f32[48]{0:T(128)S(1)}, u32[]{:S(2)}) copy-start(f32[48]{0:T(128)S(1)} %fusion.11) | copy-start | bytes 580
Sparse Core Ops, SparseCore 0:
  62.6 34.4 reduce-scatter.1

commit v2 on v1

v2 whole, which is shorter than its diff:
```python
import functools

import jax
import jax.numpy as jnp
from jax import lax
from jax.experimental import pallas as pl
from jax.experimental.pallas import tpu as pltpu
from jax.sharding import PartitionSpec as P

D = 18432
HEADS = 48
HEAD = 256
WIDE = 16
NARROW = 8
RING = 4
ROWS = 384
LOCAL = ROWS // WIDE
EACH = LOCAL // NARROW
QCOLS = HEADS * HEAD // WIDE
HELD = QCOLS // HEAD
KVCOLS = 2 * HEAD // WIDE
HCOLS = QCOLS + 128
PACK = HEAD + 128
FEATS = D // NARROW
SHARE = ROWS // NARROW
UPCOLS = 36864 // WIDE
HALF = FEATS // 2

norm_eps = 1e-05
peak_eps = 1e-06

f32, bf16 = jnp.float32, jnp.bfloat16
SAME_CORE = [[w * NARROW + z * 2 + c for w in range(WIDE) for z in range(RING)] for c in range(2)]


def swap_core(x):
    return lax.ppermute(x, "narrow", [(i, i ^ 1) for i in range(NARROW)])


def shift_z(x, by):
    return lax.ppermute(x, "narrow", [(i, ((i // 2 + by) % RING) * 2 + i % 2) for i in range(NARROW)])


def shift_x(x, by):
    return lax.ppermute(x, "wide", [(i, ((i // RING + by) % RING) * RING + i % RING) for i in range(WIDE)])


def shift_y(x, by):
    return lax.ppermute(x, "wide", [(i, (i // RING) * RING + (i + by) % RING) for i in range(WIDE)])


def gathered(normed):
    left, right = normed[:, :HALF], normed[:, HALF:]
    left = jnp.concatenate([left] + [shift_x(left, by) for by in range(1, RING)])
    right = jnp.concatenate([right] + [shift_y(right, by) for by in range(1, RING)])
    return (
        [left] + [shift_y(left, by) for by in range(1, RING)],
        [right] + [shift_x(right, by) for by in range(1, RING)],
    )


def spread(x):
    x = jnp.broadcast_to(x[:, None], (WIDE, RING) + x.shape[1:]).reshape((WIDE * RING,) + x.shape[1:])
    return lax.all_to_all(x, ("wide", "narrow"), 0, 0, axis_index_groups=SAME_CORE, tiled=True)


def dot(a, b):
    return jnp.dot(a, b, preferred_element_type=f32)


def full(shape):
    return pl.BlockSpec(shape, lambda *_: (0,) * len(shape))


def params(mib):
    return pltpu.CompilerParams(vmem_limit_bytes=mib * 1024 * 1024)


def cost(flops, moved):
    return pl.CostEstimate(flops=int(flops), bytes_accessed=int(moved), transcendentals=0)


WHOLE = pl.BlockSpec(memory_space=pltpu.VMEM)


def slot_of(wide, z, c):
    to_z, to_c = lax.rem((wide >> 2) - z + RING, RING), (wide >> 1) & 1
    return ((to_c ^ c) * RING + to_z) * 2 + (wide & 1)


def held_in(slot, z, c):
    to_z, to_c = lax.rem((slot >> 1) % RING + z, RING), (slot >> 3) ^ c
    return (to_z * 2 + to_c) * 2 + (slot & 1)


def head_kernel(place, *refs):
    left, right = refs[:RING], refs[RING : 2 * RING]
    wq_ref, wkv_ref, keep_ref, send_ref, x_ref, acc_ref, rows_ref = refs[2 * RING :]
    z, c, x, y = place[0], place[1], place[2], place[3]
    for outer in range(RING):
        for first, ref in ((0, left[outer]), (HALF, right[outer])):
            held = ref[...].astype(f32)
            for inner in range(RING):
                by_x, by_y = (inner, outer) if first == 0 else (outer, inner)
                source = lax.rem(x - by_x + RING, RING) * RING + lax.rem(y - by_y + RING, RING)
                at = pl.ds(pl.multiple_of(slot_of(source, z, c) * LOCAL, 8), LOCAL)
                rows_ref[at, first : first + HALF] = held[inner * LOCAL : (inner + 1) * LOCAL]
    x_ref[...] = rows_ref[...].astype(bf16)

    def deal(terms, first):
        for at in range(WIDE):
            rows = pl.ds(pl.multiple_of(held_in(at, z, c) * LOCAL, 8), LOCAL)
            for lanes in range(terms.shape[1] // 128):
                acc_ref[lanes, rows, :] = terms[at * LOCAL : (at + 1) * LOCAL, lanes * 128 : (lanes + 1) * 128]
        for n in range(NARROW):
            at = lax.rem(n // 2 - z + RING, RING)
            for lanes in range(terms.shape[1] // 128):
                rows = acc_ref[lanes, pl.ds(n, SHARE, stride=NARROW), :]
                columns = slice(first + lanes * 128, first + (lanes + 1) * 128)

                @pl.when(c == n % 2)
                def _():
                    keep_ref[at, :, columns] = rows

                @pl.when(c != n % 2)
                def _():
                    send_ref[at, :, columns] = rows

    for first in range(0, QCOLS, 256):
        deal(dot(x_ref[...], wq_ref[:, first : first + 256]), first)
    deal(jnp.concatenate([dot(x_ref[...], wkv_ref[...]), jnp.zeros((ROWS, 128 - KVCOLS), f32)], axis=1), QCOLS)


def head_terms(place, left, right, w_query, w_keyval):
    out = jax.ShapeDtypeStruct((RING, SHARE, HCOLS), f32)
    rows = jax.ShapeDtypeStruct((ROWS, FEATS), bf16)
    return pl.pallas_call(
        head_kernel,
        grid_spec=pltpu.PrefetchScalarGridSpec(
            num_scalar_prefetch=1,
            grid=(1,),
            in_specs=[WHOLE] * (2 * RING + 2),
            out_specs=[WHOLE] * 3,
            scratch_shapes=[pltpu.VMEM((2, ROWS, 128), f32), pltpu.VMEM((ROWS, FEATS), f32)],
        ),
        out_shape=[out, out, rows],
        compiler_params=params(20),
        cost_estimate=cost(2 * ROWS * FEATS * (QCOLS + KVCOLS), 2 * FEATS * (ROWS + QCOLS + 128) + 8 * out.size),
    )(place, *left, *right, w_query, w_keyval)


def up_kernel(x_ref, w_ref, keep_ref, send_ref):
    half = ROWS // 2
    terms = dot(x_ref[...], w_ref[...]).astype(bf16)
    for at in range(RING):
        keep_ref[at] = terms[at * SHARE : (at + 1) * SHARE]
        send_ref[at] = terms[half + at * SHARE : half + (at + 1) * SHARE]


def up_terms(x, w_up):
    tile = 768
    out = jax.ShapeDtypeStruct((RING, SHARE, UPCOLS), bf16)
    block = pl.BlockSpec((RING, SHARE, tile), lambda i: (0, 0, i))
    return pl.pallas_call(
        up_kernel,
        grid=(UPCOLS // tile,),
        in_specs=[full((ROWS, FEATS)), pl.BlockSpec((FEATS, tile), lambda i: (0, i))],
        out_specs=[block, block],
        out_shape=[out, out],
        compiler_params=params(16),
        cost_estimate=cost(2 * ROWS * FEATS * UPCOLS, 2 * (FEATS * (ROWS + UPCOLS) + ROWS * UPCOLS)),
    )(x, w_up)


def parts(value):
    high = value.astype(bf16).astype(f32)
    rest = value - high
    middle = rest.astype(bf16).astype(f32)
    return high, middle, (rest - middle).astype(bf16).astype(f32)


def packed(top, total):
    lane = lax.broadcasted_iota(jnp.int32, (top.shape[0], 128), 1)
    out = jnp.zeros(lane.shape, f32)
    for at, part in enumerate(parts(top) + parts(total)):
        out = jnp.where(lane == at, part, out)
    return out.astype(bf16)


def unpacked(block):
    held = block[:, HEAD:PACK].astype(f32)
    top = held[:, 0:1] + held[:, 1:2] + held[:, 2:3]
    total = held[:, 3:4] + held[:, 4:5] + held[:, 5:6]
    return block[:, :HEAD].astype(f32), top, total


def chosen(rows, columns, source):
    made = lax.broadcasted_iota(jnp.int32, (rows, columns), 0)
    held = lax.broadcasted_iota(jnp.int32, (rows, columns), 1)
    return jnp.where(source(made) == held, 1.0, 0.0).astype(bf16)


def by_row(block):
    return dot(chosen(SHARE, SHARE, lambda i: lax.rem(i, WIDE) * EACH + i // WIDE), block)


def heads_of(rows):
    return jnp.concatenate([rows[:, h * HEAD : (h + 1) * HEAD] for h in range(HELD)], axis=0)


def attend_kernel(away, place, lengths, q_ref, k_ref, v_ref, out_ref):
    group = group_of(away, pl.program_id(0), place)
    positions = k_ref.shape[2]
    start = (place[0] * 2 + place[1]) * positions
    rows = by_row(q_ref[0])
    position = lax.broadcasted_iota(jnp.int32, (HEADS, positions), 1) + start
    valid = jnp.concatenate([position < lengths[j * NARROW + group] for j in range(EACH)], axis=0)
    scores = jnp.concatenate(
        [
            lax.dot_general(
                heads_of(rows[j * WIDE : (j + 1) * WIDE]).astype(bf16),
                k_ref[j, 0],
                (((1,), (1,)), ((), ())),
                preferred_element_type=f32,
            )
            for j in range(EACH)
        ],
        axis=0,
    )
    masked = jnp.where(valid, scores * (1.0 / HEAD**0.5), f32(-1e30))
    top = jnp.max(masked, axis=1, keepdims=True)
    probs = jnp.where(valid, jnp.exp(masked - top), f32(0.0))
    total = jnp.sum(probs, axis=1, keepdims=True)
    weights = probs.astype(bf16)
    for j in range(EACH):
        span = slice(j * HEADS, (j + 1) * HEADS)
        out_ref[0, span, :HEAD] = dot(weights[span], v_ref[j, 0]).astype(bf16)
    out_ref[0, :, HEAD:] = packed(top, total)


def group_of(away, step, place):
    at = lax.rem(place[0] + step, RING) * 2
    return at + (1 - place[1] if away else place[1])


def attend(away, place, lengths, query, k_cache, v_cache):
    positions = k_cache.shape[1]
    k_cache = k_cache.reshape(EACH, NARROW, positions, HEAD)
    v_cache = v_cache.reshape(EACH, NARROW, positions, HEAD)
    cache = pl.BlockSpec((EACH, 1, positions, HEAD), lambda i, place, _: (0, group_of(away, i, place), 0, 0))
    out = jax.ShapeDtypeStruct((RING, EACH * HEADS, PACK), bf16)
    return pl.pallas_call(
        functools.partial(attend_kernel, away),
        grid_spec=pltpu.PrefetchScalarGridSpec(
            num_scalar_prefetch=2,
            grid=(RING,),
            in_specs=[
                pl.BlockSpec((1, SHARE, HCOLS), lambda i, place, _: (lax.rem(place[0] + i, RING), 0, 0)),
                cache,
                cache,
            ],
            out_specs=pl.BlockSpec((1, EACH * HEADS, PACK), lambda i, *_: (i, 0, 0)),
        ),
        out_shape=out,
        compiler_params=params(6),
        cost_estimate=cost(2 * LOCAL * HEADS * positions * HEAD, 2 * k_cache.size + 2 * out.size + 2 * query.size),
    )(place, lengths, query, k_cache, v_cache)


def joined(first, second):
    value_a, top_a, total_a = first
    value_b, top_b, total_b = second
    both = jnp.maximum(top_a, top_b)
    keep_a = jnp.exp(top_a - both)
    keep_b = jnp.exp(top_b - both)
    return value_a * keep_a + value_b * keep_b, both, total_a * keep_a + total_b * keep_b


def pair_kernel(a_ref, b_ref, up_a_ref, up_b_ref, own_ref, up_ref, *send_refs):
    for at in range(RING):
        value, top, total = joined(unpacked(a_ref[at]), unpacked(b_ref[at]))
        block = jnp.concatenate([value.astype(bf16), packed(top, total)], axis=1)
        up = up_a_ref[at].astype(f32) + up_b_ref[at].astype(f32)
        if at == 0:
            own_ref[...] = block
            up_ref[...] = up
        else:
            ref = send_refs[at - 1]
            for j in range(EACH):
                ref[:, j * PACK : (j + 1) * PACK] = block[j * HEADS : (j + 1) * HEADS]
            ref[:, EACH * PACK :] = up.astype(bf16)


def pair(a, b, up_a, up_b):
    out = [jax.ShapeDtypeStruct(a.shape[1:], bf16), jax.ShapeDtypeStruct(up_a.shape[1:], f32)]
    out += [jax.ShapeDtypeStruct((SHARE, EACH * PACK + UPCOLS), bf16)] * (RING - 1)
    return pl.pallas_call(
        pair_kernel,
        out_shape=out,
        compiler_params=params(12),
        cost_estimate=cost(4 * a.size, 6 * a.size + 6 * up_a.size),
    )(a, b, up_a, up_b)


def row_of(block):
    spot = lax.broadcasted_iota(jnp.int32, (KVCOLS, HEAD), 0)
    lane = lax.broadcasted_iota(jnp.int32, (KVCOLS, HEAD), 1)
    tiled = dot(block, (lax.rem(lane, KVCOLS) == spot).astype(bf16))
    row = lax.broadcasted_iota(jnp.int32, tiled.shape, 0)
    lane = lax.broadcasted_iota(jnp.int32, tiled.shape, 1)
    return jnp.sum(jnp.where(lane // KVCOLS == row, tiled, 0.0), axis=0, keepdims=True)


def finish_kernel(place, q_ref, own_ref, up_own_ref, *refs):
    blocks, (out_ref, up_ref) = refs[: RING - 1], refs[RING - 1 :]
    up = sum((ref[:, EACH * PACK :].astype(f32) for ref in blocks), up_own_ref[...])
    up_ref[...] = up
    rows = by_row(q_ref[place[0]])
    made = []
    for j in range(EACH):
        mine = rows[j * WIDE : (j + 1) * WIDE]
        query = heads_of(mine)
        keyval = mine[:, QCOLS : QCOLS + KVCOLS].astype(bf16)
        new_key = row_of(keyval[: WIDE // 2])
        new_value = row_of(keyval[WIDE // 2 :])
        own = jnp.sum(query * new_key, axis=1, keepdims=True) * (1.0 / HEAD**0.5)
        span = slice(j * HEADS, (j + 1) * HEADS)
        held = [own_ref[span, :]] + [ref[:, j * PACK : (j + 1) * PACK] for ref in blocks]
        value, top, total = functools.reduce(joined, [unpacked(block) for block in held])
        both = jnp.maximum(top, own)
        keep = jnp.exp(top - both)
        fresh = jnp.exp(own - both)
        mass = total * keep + fresh
        done = ((value * keep + fresh.astype(bf16).astype(f32) * new_value) / mass).astype(bf16)
        made.append(jnp.concatenate([done[h * WIDE : (h + 1) * WIDE] for h in range(HELD)], axis=1))
    each = EACH + 1
    order = chosen(WIDE * each, SHARE, lambda i: jnp.where(lax.rem(i, each) < EACH, lax.rem(i, each) * WIDE + i // each, -1))
    made = dot(order, jnp.concatenate(made, axis=0))
    column = jnp.max(jnp.abs(up), axis=1, keepdims=True)
    row = lax.broadcasted_iota(jnp.int32, (SHARE, 128), 0)
    lane = lax.broadcasted_iota(jnp.int32, (SHARE, 128), 1)
    peak = jnp.sum(jnp.where(row == lane, column, 0.0), axis=0, keepdims=True)
    peaks = jnp.concatenate(parts(peak) + (jnp.zeros((1, QCOLS - 3 * 128), f32),), axis=1)
    row = lax.broadcasted_iota(jnp.int32, made.shape, 0)
    out_ref[...] = jnp.where(lax.rem(row, each) == EACH, peaks, made).astype(bf16)


def finish(place, query, own, up_own, blocks):
    out = [
        jax.ShapeDtypeStruct((WIDE * (EACH + 1), QCOLS), bf16),
        jax.ShapeDtypeStruct(up_own.shape, f32),
    ]
    return pl.pallas_call(
        finish_kernel,
        grid_spec=pltpu.PrefetchScalarGridSpec(
            num_scalar_prefetch=1,
            grid=(1,),
            in_specs=[WHOLE] * (len(blocks) + 3),
            out_specs=[WHOLE] * 2,
        ),
        out_shape=out,
        compiler_params=params(12),
        cost_estimate=cost(40 * own.size, 10 * own.size + 14 * up_own.size),
    )(place, query, own, up_own, *blocks)


def out_kernel(place, own_ref, other_ref, w_ref, out_ref, peak_ref):
    each = EACH + 1
    shape = (ROWS, own_ref.shape[0])
    made = lax.broadcasted_iota(jnp.int32, shape, 0)
    held = lax.broadcasted_iota(jnp.int32, shape, 1)
    local = lax.rem(made, LOCAL)
    group = lax.rem(local, NARROW)
    source = ((made // LOCAL) * RING + group // 2) * each + local // NARROW
    rows = jnp.zeros((ROWS, QCOLS), f32)
    for core, ref in ((place[1], own_ref), (1 - place[1], other_ref)):
        pick = jnp.where(source == held, jnp.where(lax.rem(group, 2) == core, 1.0, 0.0), 0.0)
        rows += dot(pick.astype(bf16), ref[...])
    rows = rows.astype(bf16)
    for first in range(0, FEATS, 768):
        out_ref[:, first : first + 768] = dot(rows, w_ref[:, first : first + 768]).astype(bf16)
    peaks = own_ref[...].astype(f32)
    peaks = peaks[:, 0:128] + peaks[:, 128:256] + peaks[:, 256:384]
    row = lax.broadcasted_iota(jnp.int32, peaks.shape, 0)
    mine = jnp.where(lax.rem(row, each) == EACH, lax.rem(row // each, RING), -1) == place[0]
    peak_ref[...] = jnp.max(jnp.where(mine, peaks, 0.0), axis=0, keepdims=True)


def out_terms(place, own, other, w_out):
    out = jax.ShapeDtypeStruct((ROWS, FEATS), bf16)
    return pl.pallas_call(
        out_kernel,
        grid_spec=pltpu.PrefetchScalarGridSpec(
            num_scalar_prefetch=1,
            grid=(1,),
            in_specs=[WHOLE] * 3,
            out_specs=[WHOLE] * 2,
        ),
        out_shape=[out, jax.ShapeDtypeStruct((1, 128), f32)],
        compiler_params=params(16),
        cost_estimate=cost(2 * ROWS * QCOLS * FEATS, 2 * (QCOLS * FEATS + ROWS * FEATS)),
    )(place, own, other, w_out)


def last_kernel(residual_ref, terms_ref, out_ref):
    total = residual_ref[...].astype(f32)
    for at in range(WIDE):
        total += terms_ref[at].astype(f32)
    out_ref[...] = total.astype(bf16)


def last(residual, terms):
    return pl.pallas_call(
        last_kernel,
        out_shape=jax.ShapeDtypeStruct(residual.shape, bf16),
        compiler_params=params(8),
        cost_estimate=cost(16 * residual.size, 36 * residual.size),
    )(residual, terms)


def scale_kernel(up_ref, peak_ref, out_ref):
    row = lax.broadcasted_iota(jnp.int32, (SHARE, 128), 0)
    lane = lax.broadcasted_iota(jnp.int32, (SHARE, 128), 1)
    column = jnp.sum(jnp.where(row == lane, peak_ref[...], 0.0), axis=1, keepdims=True)
    out_ref[...] = (up_ref[...] / (column + peak_eps)).astype(bf16)


def scale(up, peak):
    return pl.pallas_call(
        scale_kernel,
        out_shape=jax.ShapeDtypeStruct(up.shape, bf16),
        compiler_params=params(4),
        cost_estimate=cost(4 * up.size, 6 * up.size),
    )(up, peak)


def brought(shift, blocks):
    return [blocks[0]] + [shift(blocks[by], by) for by in range(1, RING)]


def added(shift, blocks):
    return sum((block.astype(f32) for block in brought(shift, blocks)[1:]), blocks[0].astype(f32))


def shards(residual, ln_gain, w_query, w_keyval, w_out, w_up, k_cache, v_cache, lengths):
    narrow, wide = lax.axis_index("narrow"), lax.axis_index("wide")
    place = jnp.stack([narrow >> 1, narrow & 1, wide >> 2, wide & 3]).astype(jnp.int32)
    residual_f32 = residual.astype(f32)
    sums = jnp.stack([jnp.sum(residual_f32, axis=1), jnp.sum(residual_f32 * residual_f32, axis=1)])
    sums = lax.all_to_all(jnp.broadcast_to(sums[None], (NARROW,) + sums.shape), "narrow", 0, 0, tiled=True)
    sums = jnp.sum(sums, axis=0)
    mean = sums[0] / D
    variance = sums[1] / D - mean * mean
    normed = (
        (residual_f32 - mean[:, None]) * lax.rsqrt(variance + norm_eps)[:, None] * ln_gain[None, :]
    ).astype(bf16)
    left, right = gathered(normed)

    keep, send, rows = head_terms(place, left, right, w_query, w_keyval)
    both = keep + swap_core(send)
    rows, both = lax.optimization_barrier((rows, both))
    query = added(shift_z, [both[by] for by in range(RING)]).astype(bf16)
    up_keep, up_send = up_terms(rows, w_up)
    query, up_keep, up_send = lax.optimization_barrier((query, up_keep, up_send))

    query = spread(query.reshape(WIDE, EACH, HCOLS)).reshape(WIDE, RING, EACH, HCOLS)
    query = query.transpose(1, 0, 2, 3).reshape(RING, SHARE, HCOLS)
    other = swap_core(query)
    keep = attend(False, place, lengths, query, k_cache, v_cache)
    send = attend(True, place, lengths, other, k_cache, v_cache)
    part, up, *blocks = pair(keep, swap_core(send), up_keep, swap_core(up_send))
    blocks = [shift_z(block, by + 1) for by, block in enumerate(blocks)]
    attended, up = finish(place, query, part, up, blocks)

    own = spread(attended.reshape(WIDE, EACH + 1, QCOLS)).reshape(WIDE * RING * (EACH + 1), QCOLS)
    terms, peak = out_terms(place, own, swap_core(own), w_out)
    terms = lax.all_to_all(terms.reshape(WIDE, LOCAL, FEATS), "wide", 0, 0, tiled=True)
    return (last(residual, terms), scale(up, peak), peak[0, :SHARE])


def solution(mesh):
    placed = (
        P("wide", "narrow"),
        P("narrow"),
        P("narrow", "wide"),
        P("narrow", "wide"),
        P("wide", "narrow"),
        P("narrow", "wide"),
        P("wide", "narrow", None),
        P("wide", "narrow", None),
        P("wide"),
    )
    return jax.shard_map(
        shards,
        mesh=mesh,
        in_specs=placed,
        out_specs=(P("wide", "narrow"), P("narrow", "wide"), P("narrow")),
        check_vma=False,
    )
```

time: 213 us -> 181 us (0.85)
  blocking collectives: 65.4 us -> 28.5 us
  starting transfers between devices: 19.4 us -> 40.7 us
  between operations: 14.4 us -> 0.89 us
  waiting for transfers between devices: 51.3 us -> 64.8 us
  Pallas kernels: 35.5 us -> 27.4 us
  local copies, waits for them, and re-layouts: 21.2 us -> 16 us
  other arithmetic: 5.13 us -> 2.32 us
    all_to_all x1, blocking collectives: 30.2 us -> 10.5 us  [shards(): lax.all_to_all(jnp.broadcast_to(sums[None], (NARROW,) + sums.shape), 'nar...]
    ppermute x0 -> x12, starting transfers between devices: none -> 19.4 us  [the longest x6 10.1 us: shift_x(): lax.ppermute(x, 'wide', [(i, (i // RING + by) % RING * RING + i % RING) f...]
    all_to_all x2 -> x1, blocking collectives: 35.2 us -> 18 us  [spread(): lax.all_to_all(x, ('wide', 'narrow'), 0, 0, axis_index_groups=SAME_CORE,...]
    all_to_all x1 -> x2, waiting for transfers between devices: 26.3 us -> 37.6 us  [the longest x1 26.1 us: shards(): lax.all_to_all(terms.reshape(WIDE, LOCAL, FEATS), 'wide', 0, 0, tiled=True)]
    all_to_all x1 -> x2, starting transfers between devices: 3.84 us -> 13.4 us  [the longest x1 9.56 us: spread(): lax.all_to_all(x, ('wide', 'narrow'), 0, 0, axis_index_groups=SAME_CORE,...]
    ppermute x9 -> x6, starting transfers between devices: 15.1 us -> 7.35 us  [shift_z(): lax.ppermute(x, 'narrow', [(i, (i // 2 + by) % RING * 2 + i % 2) for i in...]
    ppermute x0 -> x12, waiting for transfers between devices: none -> 6.59 us  [the longest x6 3.52 us: shift_x(): lax.ppermute(x, 'wide', [(i, (i // RING + by) % RING * RING + i % RING) f...]
    pallas_call x3 -> x6, Pallas kernels: 17.2 us -> 12.1 us  [the longest x2 6.13 us: attend(): pl.pallas_call(functools.partial(attend_kernel, away), grid_spec=pltpu.Pr...]
  transfers between devices with their start and end apart: 16 -> 25, of which waited for: 12 -> 11; matrix products, arithmetic and copies ran while one was open for 2% -> 2% of each run, Pallas kernels for 9% -> 7%
where the time goes in v2:
time: 181 us; the launch traced here: 180 us
  waiting for transfers between devices  64.8 us (36%)
  starting transfers between devices  40.7 us (22%)
  blocking collectives  28.5 us (16%)
  Pallas kernels  27.4 us (15%)
  local copies, waits for them, and re-layouts  16 us (9%)
  other arithmetic  2.32 us (1%)
    all_to_all x1, waiting for transfers between devices, shards(): lax.all_to_all(terms.reshape(WIDE, LOCAL, FEATS), 'wide', 0, 0, tiled=True)  26.1 us
    all_to_all x1, blocking collectives, spread(): lax.all_to_all(x, ('wide', 'narrow'), 0, 0, axis_index_groups=SAME_CORE,...  18 us
    ppermute x6, waiting for transfers between devices, shift_z(): lax.ppermute(x, 'narrow', [(i, (i // 2 + by) % RING * 2 + i % 2) for i in...  15 us
    unnamed x23, local copies, waits for them, and re-layouts  13.1 us
    all_to_all x1, waiting for transfers between devices, spread(): lax.all_to_all(x, ('wide', 'narrow'), 0, 0, axis_index_groups=SAME_CORE,...  11.5 us
    all_to_all x1, blocking collectives, shards(): lax.all_to_all(jnp.broadcast_to(sums[None], (NARROW,) + sums.shape), 'nar...  10.5 us
    ppermute x6, starting transfers between devices, shift_x(): lax.ppermute(x, 'wide', [(i, (i // RING + by) % RING * RING + i % RING) f...  10.1 us
    all_to_all x1, starting transfers between devices, spread(): lax.all_to_all(x, ('wide', 'narrow'), 0, 0, axis_index_groups=SAME_CORE,...  9.56 us
  transfers between devices with their start and end apart: 25, of which 11 were waited for; matrix products, arithmetic and copies ran while one was open for 2% of the time, Pallas kernels for 7%

profile of v2, /device:TPU:0, one launch (start us, length us, event | category | flops | bytes accessed | tf_op | source)
XLA Modules:
  0.0 180.5 jit_solution(4017140471261875768)
XLA Ops:
  0.6 1.0 convert_reduce_fusion
  1.7 10.5 %all_to_all.20 = f32[8,2,24]{2,1,0:T(2,128)S(1)} all-to-all(f32[8,2,24]{2,1,0:T(2,128)S(1)} %broadcast_in_dim.10), channel_id=1, replica_groups=mesh['wide'=16,'narrow'=8] {'narrow'}, dimensions={0} | all-to-all | bytes 3072 | tf_op jit(solution)/shard_map/all_to_all | solution.py:450
  12.2 1.0 fusion.3
  13.3 2.8 %collective-permute-start.2 = (bf16[24,1152]{1,0:T(8,128)(2,1)S(1)}, bf16[24,1152]{1,0:T(8,128)(2,1)S(1)}, u32[]{:S(2)}, u32[]{:S(2)}) collective-permute-start(bf16[24,1152]{1,0:T(8,128)(2,1)S(1)} %get-tuple-element.47), channel_id=1, source_target_pairs={{0,96},{8,104},{16,112},{24,120},{32,0},{40,8},{48,16},{56,24},{64... | collective-permute-start | bytes 165896 | tf_op jit(solution)/shard_map/ppermute | solution.py:45
  16.1 0.8 collective-permute-start.1
  16.9 0.9 collective-permute-start
  17.8 3.0 %collective-permute-start.8 = (bf16[24,1152]{1,0:T(8,128)(2,1)S(1)}, bf16[24,1152]{1,0:T(8,128)(2,1)S(1)}, u32[]{:S(2)}, u32[]{:S(2)}) collective-permute-start(bf16[24,1152]{1,0:T(8,128)(2,1)S(1)} %get-tuple-element.46), channel_id=1, source_target_pairs={{0,24},{8,0},{16,8},{24,16},{32,56},{40,32},{48,40},{56,48},{64,88... | collective-permute-start | bytes 165896 | tf_op jit(solution)/shard_map/ppermute | solution.py:49
  20.8 0.6 collective-permute-start.7
  21.4 1.0 collective-permute-start.6
  22.4 3.0 %collective-permute-start.5 = (bf16[96,1152]{1,0:T(8,128)(2,1)S(1)}, bf16[96,1152]{1,0:T(8,128)(2,1)S(1)}, u32[]{:S(2)}, u32[]{:S(2)}) collective-permute-start(bf16[96,1152]{1,0:T(8,128)(2,1)S(1)} %pad_maximum_fusion.refs_0_), channel_id=1, source_target_pairs={{0,24},{8,0},{16,8},{24,16},{32,56},{40,32},{48,40},{56,48},{64,88... | collective-permute-start | bytes 663560 | tf_op jit(solution)/shard_map/ppermute | solution.py:49
  25.4 1.0 collective-permute-start.4
  26.4 0.6 collective-permute-start.3
  27.1 2.8 %collective-permute-start.11 = (bf16[96,1152]{1,0:T(8,128)(2,1)S(1)}, bf16[96,1152]{1,0:T(8,128)(2,1)S(1)}, u32[]{:S(2)}, u32[]{:S(2)}) collective-permute-start(bf16[96,1152]{1,0:T(8,128)(2,1)S(1)} %pad_maximum_fusion.1.refs_4_), channel_id=1, source_target_pairs={{0,96},{8,104},{16,112},{24,120},{32,0},{40,8},{48,16},{56,24},{64... | collective-permute-start | bytes 663560 | tf_op jit(solution)/shard_map/ppermute | solution.py:45
  29.8 1.5 collective-permute-start.10
  31.4 2.1 %collective-permute-done.5.refs_3_ = bf16[96,1152]{1,0:T(8,128)(2,1)S(1)} collective-permute-done((bf16[96,1152]{1,0:T(8,128)(2,1)S(1)}, bf16[96,1152]{1,0:T(8,128)(2,1)S(1)}, u32[]{:S(2)}, u32[]{:S(2)}) %collective-permute-start.5) | collective-permute-done | bytes 221216 | tf_op jit(solution)/shard_map/ppermute | solution.py:49
  33.5 1.3 collective-permute-start.9
  34.8 1.3 copy.32.refs_9_
  36.1 0.1 pad_add_fusion.place
  36.2 0.9 collective-permute-done.3.refs_1_
  37.1 0.8 collective-permute-done.10.refs_6_
  37.9 2.7 %collective-permute-done.9.refs_5_ = bf16[96,1152]{1,0:T(8,128)(2,1)S(1)} collective-permute-done((bf16[96,1152]{1,0:T(8,128)(2,1)S(1)}, bf16[96,1152]{1,0:T(8,128)(2,1)S(1)}, u32[]{:S(2)}, u32[]{:S(2)}) %collective-permute-start.9) | collective-permute-done | bytes 221216 | tf_op jit(solution)/shard_map/ppermute | solution.py:45
  40.6 2.0 %copy-done.3 = bf16[2304,768]{1,0:T(8,128)(2,1)S(1)} copy-done((bf16[2304,768]{1,0:T(8,128)(2,1)S(1)}, bf16[2304,768]{1,0:T(8,128)(2,1)}, u32[]{:S(2)}) %copy-start.3) | copy-done | bytes 3538968
  42.6 5.7 %shard_map.112 = (f32[4,48,896]{2,1,0:T(8,128)S(1)}, f32[4,48,896]{2,1,0:T(8,128)S(1)}, bf16[384,2304]{1,0:T(8,128)(2,1)S(1)}) custom-call(s32[4]{0:T(128)S(1)} %pad_add_fusion.place, bf16[96,1152]{1,0:T(8,128)(2,1)S(1)} %pad_maximum_fusion.refs_0_, bf16[96,1152]{1,0:T(8,128)(2,1)S(1)} %collective-permute-done.3.refs_1_, ...), custom_call_target="tpu_custom_call" | custom-call | flops 1415577600 | bytes 7274496 | tf_op jit(solution)/shard_map/pallas_call | solution.py:137
  48.4 0.1 collective-permute-start.12
  48.4 2.1 %collective-permute-done.12 = f32[4,48,896]{2,1,0:T(8,128)S(1)} collective-permute-done((f32[4,48,896]{2,1,0:T(8,128)S(1)}, f32[4,48,896]{2,1,0:T(8,128)S(1)}, u32[]{:S(2)}, u32[]{:S(2)}) %collective-permute-start.12) | collective-permute-done | bytes 688160 | tf_op jit(solution)/shard_map/ppermute | solution.py:37
  50.6 0.1 add.20
  50.7 0.6 collective-permute-start.13
  51.3 2.7 %collective-permute-start.15 = (f32[48,896]{1,0:T(8,128)S(1)}, f32[48,896]{1,0:T(8,128)S(1)}, u32[]{:S(2)}, u32[]{:S(2)}) collective-permute-start(f32[48,896]{1,0:T(8,128)S(1)} %get-tuple-element.44), channel_id=1, source_target_pairs={{0,6},{1,7},{2,0},{3,1},{4,2},{5,3},{6,4},{7,5},{8,14},{9,15},{10,... | collective-permute-start | bytes 516104 | tf_op jit(solution)/shard_map/ppermute | solution.py:41
  54.0 4.0 %copy-done.8 = bf16[2304,2304]{1,0:T(8,128)(2,1)S(1)} copy-done((bf16[2304,2304]{1,0:T(8,128)(2,1)S(1)}, bf16[2304,2304]{1,0:T(8,128)(2,1)}, u32[]{:S(2)}) %copy-start.8) | copy-done | bytes 10616856
  58.0 5.4 %shard_map.113 = (bf16[4,48,2304]{2,1,0:T(8,128)(2,1)S(1)}, bf16[4,48,2304]{2,1,0:T(8,128)(2,1)S(1)}) custom-call(bf16[384,2304]{1,0:T(8,128)(2,1)S(1)} %get-tuple-element.26.x_ref, bf16[2304,2304]{1,0:T(8,128)(2,1)S(1)} %copy-done.8), custom_call_target="tpu_custom_call" | custom-call | flops 4076863488 | bytes 14155776 | tf_op jit(solution)/shard_map/pallas_call | solution.py:164
  63.5 0.9 copy-done.5
  64.4 0.9 copy-done.10
  65.3 0.1 fusion.6
  65.4 0.1 broadcast_in_dim.11
  65.5 0.9 broadcast_in_dim.12
  66.4 9.6 %all-to-all-start.1 = ((bf16[64,3,896]{2,1,0:T(4,128)(2,1)}), bf16[64,3,896]{2,1,0:T(4,128)(2,1)}, u32[]{:S(2)}, u32[]{:S(2)}) async-start(bf16[64,3,896]{2,1,0:T(4,128)(2,1)} %bitcast.46), calls=%async_computation.1 | async-start | bytes 917504 | tf_op jit(solution)/shard_map/all_to_all | solution.py:64
  75.9 0.1 collective-permute-start.18
  76.0 11.5 %all-to-all-done.1 = bf16[64,3,896]{2,1,0:T(4,128)(2,1)} async-done(((bf16[64,3,896]{2,1,0:T(4,128)(2,1)}), bf16[64,3,896]{2,1,0:T(4,128)(2,1)}, u32[]{:S(2)}, u32[]{:S(2)}) %all-to-all-start.1) | async-done | bytes 344096 | tf_op jit(solution)/shard_map/all_to_all | solution.py:64
  87.5 1.2 copy.34
  88.7 0.1 collective-permute-start.16
  88.8 1.6 collective-permute-done.16.q_ref
  90.5 1.9 %copy-done.1 = bf16[24,256,256]{2,1,0:T(8,128)(2,1)S(1)} copy-done((bf16[24,256,256]{2,1,0:T(8,128)(2,1)S(1)}, bf16[24,256,256]{2,1,0:T(8,128)(2,1)}, u32[]{:S(2)}) %copy-start.1) | copy-done | bytes 3145752
  92.4 3.1 %shard_map.115 = bf16[4,144,384]{2,1,0:T(8,128)(2,1)S(1)} custom-call(s32[4]{0:T(128)S(1)} %pad_add_fusion.place, s32[24]{0:T(128)S(1)} %copy-done.7, bf16[4,48,896]{2,1,0:T(8,128)(2,1)S(1)} %collective-permute-done.16.q_ref, bf16[3,8,256,256]{3,2,1,0:T(8,128)(2,1)S(1)} %bitcast.42, bf16[3,8,256,256]{3,2,1,0:T(8,128)(2,1)S(1)} %bitcast.44), custom_call_target="tpu_custom_call" | custom-call | flops 150994944 | bytes 3932160 | tf_op jit(solution)/shard_map/pallas_call | solution.py:252
  95.5 0.2 collective-permute-start.17
  95.7 3.1 %shard_map.114.a_ref = bf16[4,144,384]{2,1,0:T(8,128)(2,1)S(1)} custom-call(s32[4]{0:T(128)S(1)} %pad_add_fusion.place, s32[24]{0:T(128)S(1)} %copy-done.7, bf16[4,48,896]{2,1,0:T(8,128)(2,1)S(1)} %copy.37.q_ref, bf16[3,8,256,256]{3,2,1,0:T(8,128)(2,1)S(1)} %bitcast.43, bf16[3,8,256,256]{3,2,1,0:T(8,128)(2,1)S(1)} %bitcast.45), custom_call_target="tpu_custom_call" | custom-call | flops 150994944 | bytes 3932160 | tf_op jit(solution)/shard_map/pallas_call | solution.py:252
  98.8 2.7 %shard_map.116 = (bf16[144,384]{1,0:T(8,128)(2,1)S(1)}, f32[48,2304]{1,0:T(8,128)S(1)}, bf16[48,3456]{1,0:T(8,128)(2,1)S(1)}, bf16[48,3456]{1,0:T(8,128)(2,1)S(1)}, bf16[48,3456]{1,0:T(8,128)(2,1)S(1)}) custom-call(bf16[4,144,384]{2,1,0:T(8,128)(2,1)S(1)} %shard_map.114.a_ref, bf16[4,144,384]{2,1,0:T(8,128)(2,1)S(1)} %collective-permute-done.17.b_ref, ...), custom_call_target="tpu_custom_call" | custom-call | flops 884736 | bytes 3981312 | tf_op jit(solution)/shard_map/pallas_call | solution.py:297
  101.5 0.7 collective-permute-start.19
  102.3 1.8 collective-permute-start.20
  104.0 1.5 collective-permute-start.21
  105.6 14.4 %collective-permute-done.19.refs_0_ = bf16[48,3456]{1,0:T(8,128)(2,1)S(1)} collective-permute-done((bf16[48,3456]{1,0:T(8,128)(2,1)S(1)}, bf16[48,3456]{1,0:T(8,128)(2,1)S(1)}, u32[]{:S(2)}, u32[]{:S(2)}) %collective-permute-start.19) | collective-permute-done | bytes 331808 | tf_op jit(solution)/shard_map/ppermute | solution.py:41
  120.0 0.6 collective-permute-done.21.refs_2_
  120.6 1.5 shard_map.117
  122.2 0.1 broadcast_in_dim.27
  122.3 18.0 %all_to_all.21 = bf16[64,4,768]{2,1,0:T(4,128)(2,1)S(1)} all-to-all(bf16[64,4,768]{2,1,0:T(4,128)(2,1)S(1)} %bitcast.47), channel_id=1, replica_groups={{0,2,4,6,8,10,12,14,16,18,20,22,24,26,28,30,32,34,36,38,40,42,44,46,48,..., dimensions={0} | all-to-all | bytes 786432 | tf_op jit(solution)/shard_map/all_to_all | solution.py:64
  140.3 0.1 reshape.63.own_ref
  140.3 0.1 collective-permute-start.22
  140.4 1.7 collective-permute-done.22.other_ref
  142.2 2.0 %copy-done.9 = bf16[768,2304]{1,0:T(8,128)(2,1)S(1)} copy-done((bf16[768,2304]{1,0:T(8,128)(2,1)S(1)}, bf16[768,2304]{1,0:T(8,128)(2,1)}, u32[]{:S(2)}) %copy-start.9) | copy-done | bytes 3538968
  144.2 4.1 %shard_map.118 = (bf16[384,2304]{1,0:T(8,128)(2,1)}, f32[1,128]{1,0:T(1,128)S(1)}) custom-call(s32[4]{0:T(128)S(1)} %pad_add_fusion.place, bf16[256,768]{1,0:T(8,128)(2,1)S(1)} %reshape.63.own_ref, bf16[256,768]{1,0:T(8,128)(2,1)S(1)} %collective-permute-done.22.other_ref, bf16[768,2304]{1,0:T(8,128)(2,1)S(1)} %copy-done.9), custom_call_target="tpu_custom_call" | custom-call | flops 1358954496 | bytes 5308416 | tf_op jit(solution)/shard_map/pallas_call | solution.py:391
  148.3 3.8 %all-to-all-start.3 = ((bf16[16,24,2304]{2,1,0:T(8,128)(2,1)}), bf16[16,24,2304]{2,1,0:T(8,128)(2,1)S(1)}, u32[]{:S(2)}, u32[]{:S(2)}) async-start(bf16[16,24,2304]{2,1,0:T(8,128)(2,1)} %bitcast.20), calls=%async_computation.3 | async-start | bytes 3538944 | tf_op jit(solution)/shard_map/all_to_all | solution.py:477
  152.1 0.8 shard_map.120
  153.0 0.5 slice_bitcast_fusion.3
  153.5 26.1 %all-to-all-done.3.terms_ref = bf16[16,24,2304]{2,1,0:T(8,128)(2,1)S(1)} async-done(((bf16[16,24,2304]{2,1,0:T(8,128)(2,1)}), bf16[16,24,2304]{2,1,0:T(8,128)(2,1)S(1)}, u32[]{:S(2)}, u32[]{:S(2)}) %all-to-all-start.3) | async-done | bytes 1769504 | tf_op jit(solution)/shard_map/all_to_all | solution.py:477
  179.6 0.9 shard_map.119
  (42 shorter events, 0.3 us)
Async XLA Ops:
  13.3 8.2 %collective-permute-start.2 = (bf16[24,1152]{1,0:T(8,128)(2,1)S(1)}, bf16[24,1152]{1,0:T(8,128)(2,1)S(1)}, u32[]{:S(2)}, u32[]{:S(2)}) collective-permute-start(bf16[24,1152]{1,0:T(8,128)(2,1)S(1)} %get-tuple-element.47), channel_id=1, source_target_pairs={{0,96},{8,104},{16,112},{24,120},{32,0},{40,8},{48,16},{56,24},{64... | collective-permute-start | bytes 165896 | tf_op jit(solution)/shard_map/ppermute | solution.py:45
  16.1 6.3 %collective-permute-start.1 = (bf16[24,1152]{1,0:T(8,128)(2,1)S(1)}, bf16[24,1152]{1,0:T(8,128)(2,1)S(1)}, u32[]{:S(2)}, u32[]{:S(2)}) collective-permute-start(bf16[24,1152]{1,0:T(8,128)(2,1)S(1)} %get-tuple-element.47), channel_id=1, source_target_pairs={{0,64},{8,72},{16,80},{24,88},{32,96},{40,104},{48,112},{56,120},{... | collective-permute-start | bytes 165896 | tf_op jit(solution)/shard_map/ppermute | solution.py:45
  16.9 5.5 %collective-permute-start = (bf16[24,1152]{1,0:T(8,128)(2,1)S(1)}, bf16[24,1152]{1,0:T(8,128)(2,1)S(1)}, u32[]{:S(2)}, u32[]{:S(2)}) collective-permute-start(bf16[24,1152]{1,0:T(8,128)(2,1)S(1)} %get-tuple-element.47), channel_id=1, source_target_pairs={{0,32},{8,40},{16,48},{24,56},{32,64},{40,72},{48,80},{56,88},{64,... | collective-permute-start | bytes 165896 | tf_op jit(solution)/shard_map/ppermute | solution.py:45
  17.8 8.7 %collective-permute-start.8 = (bf16[24,1152]{1,0:T(8,128)(2,1)S(1)}, bf16[24,1152]{1,0:T(8,128)(2,1)S(1)}, u32[]{:S(2)}, u32[]{:S(2)}) collective-permute-start(bf16[24,1152]{1,0:T(8,128)(2,1)S(1)} %get-tuple-element.46), channel_id=1, source_target_pairs={{0,24},{8,0},{16,8},{24,16},{32,56},{40,32},{48,40},{56,48},{64,88... | collective-permute-start | bytes 165896 | tf_op jit(solution)/shard_map/ppermute | solution.py:49
  20.8 6.3 %collective-permute-start.7 = (bf16[24,1152]{1,0:T(8,128)(2,1)S(1)}, bf16[24,1152]{1,0:T(8,128)(2,1)S(1)}, u32[]{:S(2)}, u32[]{:S(2)}) collective-permute-start(bf16[24,1152]{1,0:T(8,128)(2,1)S(1)} %get-tuple-element.46), channel_id=1, source_target_pairs={{0,16},{8,24},{16,0},{24,8},{32,48},{40,56},{48,32},{56,40},{64,80... | collective-permute-start | bytes 165896 | tf_op jit(solution)/shard_map/ppermute | solution.py:49
  21.4 5.6 %collective-permute-start.6 = (bf16[24,1152]{1,0:T(8,128)(2,1)S(1)}, bf16[24,1152]{1,0:T(8,128)(2,1)S(1)}, u32[]{:S(2)}, u32[]{:S(2)}) collective-permute-start(bf16[24,1152]{1,0:T(8,128)(2,1)S(1)} %get-tuple-element.46), channel_id=1, source_target_pairs={{0,8},{8,16},{16,24},{24,0},{32,40},{40,48},{48,56},{56,32},{64,72... | collective-permute-start | bytes 165896 | tf_op jit(solution)/shard_map/ppermute | solution.py:49
  22.4 11.1 %collective-permute-start.5 = (bf16[96,1152]{1,0:T(8,128)(2,1)S(1)}, bf16[96,1152]{1,0:T(8,128)(2,1)S(1)}, u32[]{:S(2)}, u32[]{:S(2)}) collective-permute-start(bf16[96,1152]{1,0:T(8,128)(2,1)S(1)} %pad_maximum_fusion.refs_0_), channel_id=1, source_target_pairs={{0,24},{8,0},{16,8},{24,16},{32,56},{40,32},{48,40},{56,48},{64,88... | collective-permute-start | bytes 663560 | tf_op jit(solution)/shard_map/ppermute | solution.py:49
  25.4 10.8 %collective-permute-start.4 = (bf16[96,1152]{1,0:T(8,128)(2,1)S(1)}, bf16[96,1152]{1,0:T(8,128)(2,1)S(1)}, u32[]{:S(2)}, u32[]{:S(2)}) collective-permute-start(bf16[96,1152]{1,0:T(8,128)(2,1)S(1)} %pad_maximum_fusion.refs_0_), channel_id=1, source_target_pairs={{0,16},{8,24},{16,0},{24,8},{32,48},{40,56},{48,32},{56,40},{64,80... | collective-permute-start | bytes 663560 | tf_op jit(solution)/shard_map/ppermute | solution.py:49
  26.4 10.7 %collective-permute-start.3 = (bf16[96,1152]{1,0:T(8,128)(2,1)S(1)}, bf16[96,1152]{1,0:T(8,128)(2,1)S(1)}, u32[]{:S(2)}, u32[]{:S(2)}) collective-permute-start(bf16[96,1152]{1,0:T(8,128)(2,1)S(1)} %pad_maximum_fusion.refs_0_), channel_id=1, source_target_pairs={{0,8},{8,16},{16,24},{24,0},{32,40},{40,48},{48,56},{56,32},{64,72... | collective-permute-start | bytes 663560 | tf_op jit(solution)/shard_map/ppermute | solution.py:49
  27.1 10.0 %collective-permute-start.11 = (bf16[96,1152]{1,0:T(8,128)(2,1)S(1)}, bf16[96,1152]{1,0:T(8,128)(2,1)S(1)}, u32[]{:S(2)}, u32[]{:S(2)}) collective-permute-start(bf16[96,1152]{1,0:T(8,128)(2,1)S(1)} %pad_maximum_fusion.1.refs_4_), channel_id=1, source_target_pairs={{0,96},{8,104},{16,112},{24,120},{32,0},{40,8},{48,16},{56,24},{64... | collective-permute-start | bytes 663560 | tf_op jit(solution)/shard_map/ppermute | solution.py:45
  29.8 8.1 %collective-permute-start.10 = (bf16[96,1152]{1,0:T(8,128)(2,1)S(1)}, bf16[96,1152]{1,0:T(8,128)(2,1)S(1)}, u32[]{:S(2)}, u32[]{:S(2)}) collective-permute-start(bf16[96,1152]{1,0:T(8,128)(2,1)S(1)} %pad_maximum_fusion.1.refs_4_), channel_id=1, source_target_pairs={{0,64},{8,72},{16,80},{24,88},{32,96},{40,104},{48,112},{56,120},{... | collective-permute-start | bytes 663560 | tf_op jit(solution)/shard_map/ppermute | solution.py:45
  33.5 7.1 %collective-permute-start.9 = (bf16[96,1152]{1,0:T(8,128)(2,1)S(1)}, bf16[96,1152]{1,0:T(8,128)(2,1)S(1)}, u32[]{:S(2)}, u32[]{:S(2)}) collective-permute-start(bf16[96,1152]{1,0:T(8,128)(2,1)S(1)} %pad_maximum_fusion.1.refs_4_), channel_id=1, source_target_pairs={{0,32},{8,40},{16,48},{24,56},{32,64},{40,72},{48,80},{56,88},{64,... | collective-permute-start | bytes 663560 | tf_op jit(solution)/shard_map/ppermute | solution.py:45
  40.6 2.0 %copy-start.3 = (bf16[2304,768]{1,0:T(8,128)(2,1)S(1)}, bf16[2304,768]{1,0:T(8,128)(2,1)}, u32[]{:S(2)}) copy-start(bf16[2304,768]{1,0:T(8,128)(2,1)} %refs_8_.1) | copy-start | bytes 10616836
  48.4 2.2 %collective-permute-start.12 = (f32[4,48,896]{2,1,0:T(8,128)S(1)}, f32[4,48,896]{2,1,0:T(8,128)S(1)}, u32[]{:S(2)}, u32[]{:S(2)}) collective-permute-start(f32[4,48,896]{2,1,0:T(8,128)S(1)} %get-tuple-element.24), channel_id=1, source_target_pairs={{0,1},{1,0},{2,3},{3,2},{4,5},{5,4},{6,7},{7,6},{8,9},{9,8},{10,11... | collective-permute-start | bytes 2064392 | tf_op jit(solution)/shard_map/ppermute | solution.py:37
  50.7 14.6 %collective-permute-start.13 = (f32[48,896]{1,0:T(8,128)S(1)}, f32[48,896]{1,0:T(8,128)S(1)}, u32[]{:S(2)}, u32[]{:S(2)}) collective-permute-start(f32[48,896]{1,0:T(8,128)S(1)} %get-tuple-element.43), channel_id=1, source_target_pairs={{0,2},{1,3},{2,4},{3,5},{4,6},{5,7},{6,0},{7,1},{8,10},{9,11},{10,... | collective-permute-start | bytes 516104 | tf_op jit(solution)/shard_map/ppermute | solution.py:41
  51.3 14.0 %collective-permute-start.15 = (f32[48,896]{1,0:T(8,128)S(1)}, f32[48,896]{1,0:T(8,128)S(1)}, u32[]{:S(2)}, u32[]{:S(2)}) collective-permute-start(f32[48,896]{1,0:T(8,128)S(1)} %get-tuple-element.44), channel_id=1, source_target_pairs={{0,6},{1,7},{2,0},{3,1},{4,2},{5,3},{6,4},{7,5},{8,14},{9,15},{10,... | collective-permute-start | bytes 516104 | tf_op jit(solution)/shard_map/ppermute | solution.py:41
  54.0 11.3 %collective-permute-start.14 = (f32[48,896]{1,0:T(8,128)S(1)}, f32[48,896]{1,0:T(8,128)S(1)}, u32[]{:S(2)}, u32[]{:S(2)}) collective-permute-start(f32[48,896]{1,0:T(8,128)S(1)} %get-tuple-element.45), channel_id=1, source_target_pairs={{0,4},{1,5},{2,6},{3,7},{4,0},{5,1},{6,2},{7,3},{8,12},{9,13},{10,... | collective-permute-start | bytes 516104 | tf_op jit(solution)/shard_map/ppermute | solution.py:41
  54.0 4.0 %copy-start.8 = (bf16[2304,2304]{1,0:T(8,128)(2,1)S(1)}, bf16[2304,2304]{1,0:T(8,128)(2,1)}, u32[]{:S(2)}) copy-start(bf16[2304,2304]{1,0:T(8,128)(2,1)} %w_ref.2) | copy-start | bytes 31850500
  63.5 0.9 copy-start.5
  64.4 0.9 copy-start.10
  65.3 25.1 %copy-start = (bf16[24,256,256]{2,1,0:T(8,128)(2,1)S(1)}, bf16[24,256,256]{2,1,0:T(8,128)(2,1)}, u32[]{:S(2)}) copy-start(bf16[24,256,256]{2,1,0:T(8,128)(2,1)} %param.15) | copy-start | bytes 9437188
  65.3 25.1 %copy-start.7 = (s32[24]{0:T(128)S(1)}, s32[24]{0:T(128)}, u32[]{:S(2)}) copy-start(s32[24]{0:T(128)} %lengths.3) | copy-start | bytes 292
  66.4 21.2 %all-to-all-start.1 = ((bf16[64,3,896]{2,1,0:T(4,128)(2,1)}), bf16[64,3,896]{2,1,0:T(4,128)(2,1)}, u32[]{:S(2)}, u32[]{:S(2)}) async-start(bf16[64,3,896]{2,1,0:T(4,128)(2,1)} %bitcast.46), calls=%async_computation.1 | async-start | bytes 917504 | tf_op jit(solution)/shard_map/all_to_all | solution.py:64
  75.9 22.8 %collective-permute-start.18 = (bf16[4,48,2304]{2,1,0:T(8,128)(2,1)}, bf16[4,48,2304]{2,1,0:T(8,128)(2,1)}, u32[]{:S(2)}, u32[]{:S(2)}) collective-permute-start(bf16[4,48,2304]{2,1,0:T(8,128)(2,1)} %copy-done.10), channel_id=1, source_target_pairs={{0,1},{1,0},{2,3},{3,2},{4,5},{5,4},{6,7},{7,6},{8,9},{9,8},{10,11... | collective-permute-start | bytes 2654216 | tf_op jit(solution)/shard_map/ppermute | solution.py:37
  88.7 1.7 collective-permute-start.16
  90.5 1.9 %copy-start.1 = (bf16[24,256,256]{2,1,0:T(8,128)(2,1)S(1)}, bf16[24,256,256]{2,1,0:T(8,128)(2,1)}, u32[]{:S(2)}) copy-start(bf16[24,256,256]{2,1,0:T(8,128)(2,1)} %param.16) | copy-start | bytes 9437188
  92.4 3.3 %copy-start.2 = (bf16[24,256,256]{2,1,0:T(8,128)(2,1)S(1)}, bf16[24,256,256]{2,1,0:T(8,128)(2,1)}, u32[]{:S(2)}) copy-start(bf16[24,256,256]{2,1,0:T(8,128)(2,1)} %param.16) | copy-start | bytes 9437188
  95.4 3.3 %copy-start.6 = (bf16[4,48,2304]{2,1,0:T(8,128)(2,1)S(1)}, bf16[4,48,2304]{2,1,0:T(8,128)(2,1)}, u32[]{:S(2)}) copy-start(bf16[4,48,2304]{2,1,0:T(8,128)(2,1)} %copy-done.5) | copy-start | bytes 2654212
  95.5 3.3 %collective-permute-start.17 = (bf16[4,144,384]{2,1,0:T(8,128)(2,1)S(1)}, bf16[4,144,384]{2,1,0:T(8,128)(2,1)S(1)}, u32[]{:S(2)}, u32[]{:S(2)}) collective-permute-start(bf16[4,144,384]{2,1,0:T(8,128)(2,1)S(1)} %shard_map.115), channel_id=1, source_target_pairs={{0,1},{1,0},{2,3},{3,2},{4,5},{5,4},{6,7},{7,6},{8,9},{9,8},{10,11... | collective-permute-start | bytes 1327112 | tf_op jit(solution)/shard_map/ppermute | solution.py:37
  101.5 18.5 %collective-permute-start.19 = (bf16[48,3456]{1,0:T(8,128)(2,1)S(1)}, bf16[48,3456]{1,0:T(8,128)(2,1)S(1)}, u32[]{:S(2)}, u32[]{:S(2)}) collective-permute-start(bf16[48,3456]{1,0:T(8,128)(2,1)S(1)} %get-tuple-element.34), channel_id=1, source_target_pairs={{0,2},{1,3},{2,4},{3,5},{4,6},{5,7},{6,0},{7,1},{8,10},{9,11},{10,... | collective-permute-start | bytes 995336 | tf_op jit(solution)/shard_map/ppermute | solution.py:41
  102.3 17.7 %collective-permute-start.20 = (bf16[48,3456]{1,0:T(8,128)(2,1)S(1)}, bf16[48,3456]{1,0:T(8,128)(2,1)S(1)}, u32[]{:S(2)}, u32[]{:S(2)}) collective-permute-start(bf16[48,3456]{1,0:T(8,128)(2,1)S(1)} %get-tuple-element.35), channel_id=1, source_target_pairs={{0,4},{1,5},{2,6},{3,7},{4,0},{5,1},{6,2},{7,3},{8,12},{9,13},{10,... | collective-permute-start | bytes 995336 | tf_op jit(solution)/shard_map/ppermute | solution.py:41
  104.0 16.6 %collective-permute-start.21 = (bf16[48,3456]{1,0:T(8,128)(2,1)S(1)}, bf16[48,3456]{1,0:T(8,128)(2,1)S(1)}, u32[]{:S(2)}, u32[]{:S(2)}) collective-permute-start(bf16[48,3456]{1,0:T(8,128)(2,1)S(1)} %get-tuple-element.36), channel_id=1, source_target_pairs={{0,6},{1,7},{2,0},{3,1},{4,2},{5,3},{6,4},{7,5},{8,14},{9,15},{10,... | collective-permute-start | bytes 995336 | tf_op jit(solution)/shard_map/ppermute | solution.py:41
  140.3 1.8 collective-permute-start.22
  142.2 2.0 %copy-start.9 = (bf16[768,2304]{1,0:T(8,128)(2,1)S(1)}, bf16[768,2304]{1,0:T(8,128)(2,1)}, u32[]{:S(2)}) copy-start(bf16[768,2304]{1,0:T(8,128)(2,1)} %w_ref.3) | copy-start | bytes 10616836
  148.3 31.3 %copy-start.4 = (bf16[24,2304]{1,0:T(8,128)(2,1)S(1)}, bf16[24,2304]{1,0:T(8,128)(2,1)}, u32[]{:S(2)}) copy-start(bf16[24,2304]{1,0:T(8,128)(2,1)} %residual_ref.1) | copy-start | bytes 331780
  148.3 31.3 %all-to-all-start.3 = ((bf16[16,24,2304]{2,1,0:T(8,128)(2,1)}), bf16[16,24,2304]{2,1,0:T(8,128)(2,1)S(1)}, u32[]{:S(2)}, u32[]{:S(2)}) async-start(bf16[16,24,2304]{2,1,0:T(8,128)(2,1)} %bitcast.20), calls=%async_computation.3 | async-start | bytes 3538944 | tf_op jit(solution)/shard_map/all_to_all | solution.py:477

commit v3 on v2

--- a/solution.py
+++ b/solution.py
@@ -25,6 +25,7 @@
 SHARE = ROWS // NARROW
 UPCOLS = 36864 // WIDE
 HALF = FEATS // 2
+SPAN = RING * LOCAL
 
 norm_eps = 1e-05
 peak_eps = 1e-06
@@ -112,19 +113,12 @@
             rows = pl.ds(pl.multiple_of(held_in(at, z, c) * LOCAL, 8), LOCAL)
             for lanes in range(terms.shape[1] // 128):
                 acc_ref[lanes, rows, :] = terms[at * LOCAL : (at + 1) * LOCAL, lanes * 128 : (lanes + 1) * 128]
-        for n in range(NARROW):
-            at = lax.rem(n // 2 - z + RING, RING)
+        for at in range(RING):
+            n = lax.rem(z + at, RING) * 2
             for lanes in range(terms.shape[1] // 128):
-                rows = acc_ref[lanes, pl.ds(n, SHARE, stride=NARROW), :]
                 columns = slice(first + lanes * 128, first + (lanes + 1) * 128)
-
-                @pl.when(c == n % 2)
-                def _():
-                    keep_ref[at, :, columns] = rows
-
-                @pl.when(c != n % 2)
-                def _():
-                    send_ref[at, :, columns] = rows
+                keep_ref[at, :, columns] = acc_ref[lanes, pl.ds(n + c, SHARE, stride=NARROW), :]
+                send_ref[at, :, columns] = acc_ref[lanes, pl.ds(n + 1 - c, SHARE, stride=NARROW), :]
 
     for first in range(0, QCOLS, 256):
         deal(dot(x_ref[...], wq_ref[:, first : first + 256]), first)
@@ -144,30 +138,29 @@
             scratch_shapes=[pltpu.VMEM((2, ROWS, 128), f32), pltpu.VMEM((ROWS, FEATS), f32)],
         ),
         out_shape=[out, out, rows],
-        compiler_params=params(20),
+        compiler_params=params(8),
         cost_estimate=cost(2 * ROWS * FEATS * (QCOLS + KVCOLS), 2 * FEATS * (ROWS + QCOLS + 128) + 8 * out.size),
     )(place, *left, *right, w_query, w_keyval)
 
 
 def up_kernel(x_ref, w_ref, keep_ref, send_ref):
-    half = ROWS // 2
-    terms = dot(x_ref[...], w_ref[...]).astype(bf16)
-    for at in range(RING):
-        keep_ref[at] = terms[at * SHARE : (at + 1) * SHARE]
-        send_ref[at] = terms[half + at * SHARE : half + (at + 1) * SHARE]
+    half, tile = ROWS // 2, 768
+    for first in range(0, UPCOLS, tile):
+        columns = slice(first, first + tile)
+        terms = dot(x_ref[...], w_ref[:, columns]).astype(bf16)
+        for at in range(RING):
+            keep_ref[at, :, columns] = terms[at * SHARE : (at + 1) * SHARE]
+            send_ref[at, :, columns] = terms[half + at * SHARE : half + (at + 1) * SHARE]
 
 
 def up_terms(x, w_up):
-    tile = 768
     out = jax.ShapeDtypeStruct((RING, SHARE, UPCOLS), bf16)
-    block = pl.BlockSpec((RING, SHARE, tile), lambda i: (0, 0, i))
     return pl.pallas_call(
         up_kernel,
-        grid=(UPCOLS // tile,),
-        in_specs=[full((ROWS, FEATS)), pl.BlockSpec((FEATS, tile), lambda i: (0, i))],
-        out_specs=[block, block],
+        in_specs=[WHOLE] * 2,
+        out_specs=[WHOLE] * 2,
         out_shape=[out, out],
-        compiler_params=params(16),
+        compiler_params=params(4),
         cost_estimate=cost(2 * ROWS * FEATS * UPCOLS, 2 * (FEATS * (ROWS + UPCOLS) + ROWS * UPCOLS)),
     )(x, w_up)
 
@@ -209,33 +202,34 @@
 
 
 def attend_kernel(away, place, lengths, q_ref, k_ref, v_ref, out_ref):
-    group = group_of(away, pl.program_id(0), place)
     positions = k_ref.shape[2]
     start = (place[0] * 2 + place[1]) * positions
-    rows = by_row(q_ref[0])
     position = lax.broadcasted_iota(jnp.int32, (HEADS, positions), 1) + start
-    valid = jnp.concatenate([position < lengths[j * NARROW + group] for j in range(EACH)], axis=0)
-    scores = jnp.concatenate(
-        [
-            lax.dot_general(
-                heads_of(rows[j * WIDE : (j + 1) * WIDE]).astype(bf16),
-                k_ref[j, 0],
-                (((1,), (1,)), ((), ())),
-                preferred_element_type=f32,
-            )
-            for j in range(EACH)
-        ],
-        axis=0,
-    )
-    masked = jnp.where(valid, scores * (1.0 / HEAD**0.5), f32(-1e30))
-    top = jnp.max(masked, axis=1, keepdims=True)
-    probs = jnp.where(valid, jnp.exp(masked - top), f32(0.0))
-    total = jnp.sum(probs, axis=1, keepdims=True)
-    weights = probs.astype(bf16)
-    for j in range(EACH):
-        span = slice(j * HEADS, (j + 1) * HEADS)
-        out_ref[0, span, :HEAD] = dot(weights[span], v_ref[j, 0]).astype(bf16)
-    out_ref[0, :, HEAD:] = packed(top, total)
+    for step in range(RING):
+        group = group_of(away, step, place)
+        rows = by_row(q_ref[lax.rem(place[0] + step, RING)])
+        valid = jnp.concatenate([position < lengths[j * NARROW + group] for j in range(EACH)], axis=0)
+        scores = jnp.concatenate(
+            [
+                lax.dot_general(
+                    heads_of(rows[j * WIDE : (j + 1) * WIDE]).astype(bf16),
+                    k_ref[j, group],
+                    (((1,), (1,)), ((), ())),
+                    preferred_element_type=f32,
+                )
+                for j in range(EACH)
+            ],
+            axis=0,
+        )
+        masked = jnp.where(valid, scores * (1.0 / HEAD**0.5), f32(-1e30))
+        top = jnp.max(masked, axis=1, keepdims=True)
+        probs = jnp.where(valid, jnp.exp(masked - top), f32(0.0))
+        total = jnp.sum(probs, axis=1, keepdims=True)
+        weights = probs.astype(bf16)
+        for j in range(EACH):
+            span = slice(j * HEADS, (j + 1) * HEADS)
+            out_ref[step, span, :HEAD] = dot(weights[span], v_ref[j, group]).astype(bf16)
+        out_ref[step, :, HEAD:] = packed(top, total)
 
 
 def group_of(away, step, place):
@@ -247,22 +241,17 @@
     positions = k_cache.shape[1]
     k_cache = k_cache.reshape(EACH, NARROW, positions, HEAD)
     v_cache = v_cache.reshape(EACH, NARROW, positions, HEAD)
-    cache = pl.BlockSpec((EACH, 1, positions, HEAD), lambda i, place, _: (0, group_of(away, i, place), 0, 0))
     out = jax.ShapeDtypeStruct((RING, EACH * HEADS, PACK), bf16)
     return pl.pallas_call(
         functools.partial(attend_kernel, away),
         grid_spec=pltpu.PrefetchScalarGridSpec(
             num_scalar_prefetch=2,
-            grid=(RING,),
-            in_specs=[
-                pl.BlockSpec((1, SHARE, HCOLS), lambda i, place, _: (lax.rem(place[0] + i, RING), 0, 0)),
-                cache,
-                cache,
-            ],
-            out_specs=pl.BlockSpec((1, EACH * HEADS, PACK), lambda i, *_: (i, 0, 0)),
+            grid=(1,),
+            in_specs=[WHOLE] * 3,
+            out_specs=WHOLE,
         ),
         out_shape=out,
-        compiler_params=params(6),
+        compiler_params=params(3),
         cost_estimate=cost(2 * LOCAL * HEADS * positions * HEAD, 2 * k_cache.size + 2 * out.size + 2 * query.size),
     )(place, lengths, query, k_cache, v_cache)
 
@@ -297,7 +286,7 @@
     return pl.pallas_call(
         pair_kernel,
         out_shape=out,
-        compiler_params=params(12),
+        compiler_params=params(3),
         cost_estimate=cost(4 * a.size, 6 * a.size + 6 * up_a.size),
     )(a, b, up_a, up_b)
 
@@ -359,26 +348,34 @@
             out_specs=[WHOLE] * 2,
         ),
         out_shape=out,
-        compiler_params=params(12),
+        compiler_params=params(3),
         cost_estimate=cost(40 * own.size, 10 * own.size + 14 * up_own.size),
     )(place, query, own, up_own, *blocks)
 
 
-def out_kernel(place, own_ref, other_ref, w_ref, out_ref, peak_ref):
+def out_kernel(place, own_ref, other_ref, w_ref, peak_ref, *out_refs):
     each = EACH + 1
     shape = (ROWS, own_ref.shape[0])
     made = lax.broadcasted_iota(jnp.int32, shape, 0)
     held = lax.broadcasted_iota(jnp.int32, shape, 1)
-    local = lax.rem(made, LOCAL)
+    at, local = made // LOCAL, lax.rem(made, LOCAL)
     group = lax.rem(local, NARROW)
-    source = ((made // LOCAL) * RING + group // 2) * each + local // NARROW
-    rows = jnp.zeros((ROWS, QCOLS), f32)
-    for core, ref in ((place[1], own_ref), (1 - place[1], other_ref)):
-        pick = jnp.where(source == held, jnp.where(lax.rem(group, 2) == core, 1.0, 0.0), 0.0)
-        rows += dot(pick.astype(bf16), ref[...])
-    rows = rows.astype(bf16)
-    for first in range(0, FEATS, 768):
-        out_ref[:, first : first + 768] = dot(rows, w_ref[:, first : first + 768]).astype(bf16)
+    for along_x in (True, False):
+        outer, inner = at // RING, lax.rem(at, RING)
+        by_x, by_y = (outer, inner) if along_x else (inner, outer)
+        wide = lax.rem(place[2] + by_x, RING) * RING + lax.rem(place[3] + by_y, RING)
+        source = (wide * RING + group // 2) * each + local // NARROW
+        rows = jnp.zeros((ROWS, QCOLS), f32)
+        for core, ref in ((place[1], own_ref), (1 - place[1], other_ref)):
+            pick = jnp.where(source == held, jnp.where(lax.rem(group, 2) == core, 1.0, 0.0), 0.0)
+            rows += dot(pick.astype(bf16), ref[...])
+        rows = rows.astype(bf16)
+        refs = out_refs[:RING] if along_x else out_refs[RING:]
+        start = 0 if along_x else HALF
+        for first in range(0, HALF, 384):
+            terms = dot(rows, w_ref[:, start + first : start + first + 384]).astype(bf16)
+            for slot, ref in enumerate(refs):
+                ref[:, first : first + 384] = terms[slot * SPAN : (slot + 1) * SPAN]
     peaks = own_ref[...].astype(f32)
     peaks = peaks[:, 0:128] + peaks[:, 128:256] + peaks[:, 256:384]
     row = lax.broadcasted_iota(jnp.int32, peaks.shape, 0)
@@ -387,35 +384,52 @@
 
 
 def out_terms(place, own, other, w_out):
-    out = jax.ShapeDtypeStruct((ROWS, FEATS), bf16)
     return pl.pallas_call(
         out_kernel,
         grid_spec=pltpu.PrefetchScalarGridSpec(
             num_scalar_prefetch=1,
             grid=(1,),
             in_specs=[WHOLE] * 3,
-            out_specs=[WHOLE] * 2,
+            out_specs=[WHOLE] * (1 + 2 * RING),
         ),
-        out_shape=[out, jax.ShapeDtypeStruct((1, 128), f32)],
-        compiler_params=params(16),
+        out_shape=[jax.ShapeDtypeStruct((1, 128), f32)] + [jax.ShapeDtypeStruct((SPAN, HALF), bf16)] * (2 * RING),
+        compiler_params=params(6),
         cost_estimate=cost(2 * ROWS * QCOLS * FEATS, 2 * (QCOLS * FEATS + ROWS * FEATS)),
     )(place, own, other, w_out)
 
 
-def last_kernel(residual_ref, terms_ref, out_ref):
-    total = residual_ref[...].astype(f32)
-    for at in range(WIDE):
-        total += terms_ref[at].astype(f32)
-    out_ref[...] = total.astype(bf16)
-
-
-def last(residual, terms):
+def middle_kernel(*refs):
+    blocks, (own_ref, *send_refs) = refs[:RING], refs[RING:]
+    total = sum((ref[...].astype(f32) for ref in blocks[1:]), blocks[0][...].astype(f32))
+    own_ref[...] = total[:LOCAL]
+    for at, ref in enumerate(send_refs):
+        ref[...] = total[(at + 1) * LOCAL : (at + 2) * LOCAL].astype(bf16)
+
+
+def middle(blocks):
+    return pl.pallas_call(
+        middle_kernel,
+        out_shape=[jax.ShapeDtypeStruct((LOCAL, HALF), f32)] + [jax.ShapeDtypeStruct((LOCAL, HALF), bf16)] * (RING - 1),
+        compiler_params=params(4),
+        cost_estimate=cost(4 * blocks[0].size, 12 * blocks[0].size),
+    )(*blocks)
+
+
+def last_kernel(residual_ref, *refs):
+    left, right, out_ref = refs[:RING], refs[RING : 2 * RING], refs[2 * RING]
+    for first, blocks in ((0, left), (HALF, right)):
+        total = sum((ref[...].astype(f32) for ref in blocks[1:]), blocks[0][...])
+        columns = slice(first, first + HALF)
+        out_ref[:, columns] = (residual_ref[:, columns].astype(f32) + total).astype(bf16)
+
+
+def last(residual, left, right):
     return pl.pallas_call(
         last_kernel,
         out_shape=jax.ShapeDtypeStruct(residual.shape, bf16),
-        compiler_params=params(8),
-        cost_estimate=cost(16 * residual.size, 36 * residual.size),
-    )(residual, terms)
+        compiler_params=params(2),
+        cost_estimate=cost(8 * residual.size, 12 * residual.size),
+    )(residual, *left, *right)
 
 
 def scale_kernel(up_ref, peak_ref, out_ref):
@@ -429,7 +443,7 @@
     return pl.pallas_call(
         scale_kernel,
         out_shape=jax.ShapeDtypeStruct(up.shape, bf16),
-        compiler_params=params(4),
+        compiler_params=params(2),
         cost_estimate=cost(4 * up.size, 6 * up.size),
     )(up, peak)
 
@@ -468,14 +482,17 @@
     other = swap_core(query)
     keep = attend(False, place, lengths, query, k_cache, v_cache)
     send = attend(True, place, lengths, other, k_cache, v_cache)
+    send, up_send = lax.optimization_barrier((send, up_send))
     part, up, *blocks = pair(keep, swap_core(send), up_keep, swap_core(up_send))
     blocks = [shift_z(block, by + 1) for by, block in enumerate(blocks)]
     attended, up = finish(place, query, part, up, blocks)
 
     own = spread(attended.reshape(WIDE, EACH + 1, QCOLS)).reshape(WIDE * RING * (EACH + 1), QCOLS)
-    terms, peak = out_terms(place, own, swap_core(own), w_out)
-    terms = lax.all_to_all(terms.reshape(WIDE, LOCAL, FEATS), "wide", 0, 0, tiled=True)
-    return (last(residual, terms), scale(up, peak), peak[0, :SHARE])
+    peak, *terms = out_terms(place, own, swap_core(own), w_out)
+    left = middle(brought(shift_x, terms[:RING]))
+    right = middle(brought(shift_y, terms[RING:]))
+    mixed = last(residual, brought(shift_y, left), brought(shift_x, right))
+    return (mixed, scale(up, peak), peak[0, :SHARE])
 
 
 def solution(mesh):

time: 181 us -> 169 us (0.934)
  waiting for transfers between devices: 64.8 us -> 38.5 us
  blocking collectives: 28.5 us -> 49.3 us
  Pallas kernels: 27.4 us -> 20.5 us
  local copies, waits for them, and re-layouts: 16 us -> 14.1 us
    all_to_all x2 -> x0, waiting for transfers between devices: 37.6 us -> none  [the longest x1 26.1 us: shards(): lax.all_to_all(terms.reshape(WIDE, LOCAL, FEATS), 'wide', 0, 0, tiled=True)]
    all_to_all x1 -> x2, blocking collectives: 18 us -> 38.8 us  [spread(): lax.all_to_all(x, ('wide', 'narrow'), 0, 0, axis_index_groups=SAME_CORE,...]
    all_to_all x2 -> x0, starting transfers between devices: 13.4 us -> none  [the longest x1 9.56 us: spread(): lax.all_to_all(x, ('wide', 'narrow'), 0, 0, axis_index_groups=SAME_CORE,...]
    ppermute x6 -> x12, waiting for transfers between devices: 3.52 us -> 13 us  [shift_x(): lax.ppermute(x, 'wide', [(i, (i // RING + by) % RING * RING + i % RING) f...]
    ppermute x6 -> x12, starting transfers between devices: 9.24 us -> 17.2 us  [shift_y(): lax.ppermute(x, 'wide', [(i, i // RING * RING + (i + by) % RING) for i in...]
    ppermute x6 -> x12, starting transfers between devices: 10.1 us -> 17 us  [shift_x(): lax.ppermute(x, 'wide', [(i, (i // RING + by) % RING * RING + i % RING) f...]
    pallas_call x1, Pallas kernels: 5.71 us -> 3.25 us  [head_terms(): pl.pallas_call(head_kernel, grid_spec=pltpu.PrefetchScalarGridSpec(num_sc...]
    pallas_call x2 -> x4, Pallas kernels: 8.18 us -> 6.05 us  [the longest x1 4.27 us: up_terms(): pl.pallas_call(up_kernel, in_specs=[WHOLE] * 2, out_specs=[WHOLE] * 2, ou...]
  transfers between devices with their start and end apart: 25 -> 35, of which waited for: 11 -> 15; matrix products, arithmetic and copies ran while one was open for 2% -> 1% of each run, Pallas kernels for 7% -> 4%
where the time goes in v3:
time: 169 us; the launch traced here: 168 us
  blocking collectives  49.3 us (29%)
  starting transfers between devices  42.4 us (25%)
  waiting for transfers between devices  38.5 us (23%)
  Pallas kernels  20.5 us (12%)
  local copies, waits for them, and re-layouts  14.1 us (8%)
  other arithmetic  2.32 us (1%)
    all_to_all x2, blocking collectives, spread(): lax.all_to_all(x, ('wide', 'narrow'), 0, 0, axis_index_groups=SAME_CORE,...  38.8 us
    ppermute x12, starting transfers between devices, shift_y(): lax.ppermute(x, 'wide', [(i, i // RING * RING + (i + by) % RING) for i in...  17.2 us
    ppermute x12, starting transfers between devices, shift_x(): lax.ppermute(x, 'wide', [(i, (i // RING + by) % RING * RING + i % RING) f...  17 us
    ppermute x6, waiting for transfers between devices, shift_z(): lax.ppermute(x, 'narrow', [(i, (i // 2 + by) % RING * 2 + i % 2) for i in...  14.8 us
    ppermute x12, waiting for transfers between devices, shift_x(): lax.ppermute(x, 'wide', [(i, (i // RING + by) % RING * RING + i % RING) f...  13 us
    unnamed x25, local copies, waits for them, and re-layouts  13 us
    all_to_all x1, blocking collectives, shards(): lax.all_to_all(jnp.broadcast_to(sums[None], (NARROW,) + sums.shape), 'nar...  10.5 us
    ppermute x6, starting transfers between devices, shift_z(): lax.ppermute(x, 'narrow', [(i, (i // 2 + by) % RING * 2 + i % 2) for i in...  7.34 us
  transfers between devices with their start and end apart: 35, of which 15 were waited for; matrix products, arithmetic and copies ran while one was open for 1% of the time, Pallas kernels for 4%

profile of v3, /device:TPU:0, one launch (start us, length us, event | category | flops | bytes accessed | tf_op | source)
XLA Modules:
  0.0 168.1 jit_solution(16975622973416973719)
XLA Ops:
  0.6 1.0 convert_reduce_fusion
  1.7 10.5 %all_to_all.15 = f32[8,2,24]{2,1,0:T(2,128)S(1)} all-to-all(f32[8,2,24]{2,1,0:T(2,128)S(1)} %broadcast_in_dim.10), channel_id=1, replica_groups=mesh['wide'=16,'narrow'=8] {'narrow'}, dimensions={0} | all-to-all | bytes 3072 | tf_op jit(solution)/shard_map/all_to_all | solution.py:464
  12.2 1.0 fusion.3
  13.3 2.8 %collective-permute-start.2 = (bf16[24,1152]{1,0:T(8,128)(2,1)S(1)}, bf16[24,1152]{1,0:T(8,128)(2,1)S(1)}, u32[]{:S(2)}, u32[]{:S(2)}) collective-permute-start(bf16[24,1152]{1,0:T(8,128)(2,1)S(1)} %get-tuple-element.81), channel_id=1, source_target_pairs={{0,96},{8,104},{16,112},{24,120},{32,0},{40,8},{48,16},{56,24},{64... | collective-permute-start | bytes 165896 | tf_op jit(solution)/shard_map/ppermute | solution.py:46
  16.1 0.8 collective-permute-start.1
  16.9 0.9 collective-permute-start
  17.8 3.0 %collective-permute-start.8 = (bf16[24,1152]{1,0:T(8,128)(2,1)S(1)}, bf16[24,1152]{1,0:T(8,128)(2,1)S(1)}, u32[]{:S(2)}, u32[]{:S(2)}) collective-permute-start(bf16[24,1152]{1,0:T(8,128)(2,1)S(1)} %get-tuple-element.80), channel_id=1, source_target_pairs={{0,24},{8,0},{16,8},{24,16},{32,56},{40,32},{48,40},{56,48},{64,88... | collective-permute-start | bytes 165896 | tf_op jit(solution)/shard_map/ppermute | solution.py:50
  20.8 0.6 collective-permute-start.7
  21.4 1.0 collective-permute-start.6
  22.4 3.0 %collective-permute-start.5 = (bf16[96,1152]{1,0:T(8,128)(2,1)S(1)}, bf16[96,1152]{1,0:T(8,128)(2,1)S(1)}, u32[]{:S(2)}, u32[]{:S(2)}) collective-permute-start(bf16[96,1152]{1,0:T(8,128)(2,1)S(1)} %pad_maximum_fusion.refs_0_), channel_id=1, source_target_pairs={{0,24},{8,0},{16,8},{24,16},{32,56},{40,32},{48,40},{56,48},{64,88... | collective-permute-start | bytes 663560 | tf_op jit(solution)/shard_map/ppermute | solution.py:50
  25.4 1.0 collective-permute-start.4
  26.4 0.6 collective-permute-start.3
  27.1 2.8 %collective-permute-start.11 = (bf16[96,1152]{1,0:T(8,128)(2,1)S(1)}, bf16[96,1152]{1,0:T(8,128)(2,1)S(1)}, u32[]{:S(2)}, u32[]{:S(2)}) collective-permute-start(bf16[96,1152]{1,0:T(8,128)(2,1)S(1)} %pad_maximum_fusion.1.refs_4_), channel_id=1, source_target_pairs={{0,96},{8,104},{16,112},{24,120},{32,0},{40,8},{48,16},{56,24},{64... | collective-permute-start | bytes 663560 | tf_op jit(solution)/shard_map/ppermute | solution.py:46
  29.8 1.5 collective-permute-start.10
  31.4 2.1 %collective-permute-done.5.refs_3_ = bf16[96,1152]{1,0:T(8,128)(2,1)S(1)} collective-permute-done((bf16[96,1152]{1,0:T(8,128)(2,1)S(1)}, bf16[96,1152]{1,0:T(8,128)(2,1)S(1)}, u32[]{:S(2)}, u32[]{:S(2)}) %collective-permute-start.5) | collective-permute-done | bytes 221216 | tf_op jit(solution)/shard_map/ppermute | solution.py:50
  33.5 1.3 collective-permute-start.9
  34.8 1.2 copy.32.refs_9_
  36.1 1.0 collective-permute-done.3.refs_1_
  37.1 0.8 collective-permute-done.10.refs_6_
  37.9 2.7 %collective-permute-done.9.refs_5_ = bf16[96,1152]{1,0:T(8,128)(2,1)S(1)} collective-permute-done((bf16[96,1152]{1,0:T(8,128)(2,1)S(1)}, bf16[96,1152]{1,0:T(8,128)(2,1)S(1)}, u32[]{:S(2)}, u32[]{:S(2)}) %collective-permute-start.9) | collective-permute-done | bytes 221216 | tf_op jit(solution)/shard_map/ppermute | solution.py:46
  40.6 2.0 %copy-done.3 = bf16[2304,768]{1,0:T(8,128)(2,1)S(1)} copy-done((bf16[2304,768]{1,0:T(8,128)(2,1)S(1)}, bf16[2304,768]{1,0:T(8,128)(2,1)}, u32[]{:S(2)}) %copy-start.3) | copy-done | bytes 3538968
  42.6 3.2 %shard_map.112 = (f32[4,48,896]{2,1,0:T(8,128)S(1)}, f32[4,48,896]{2,1,0:T(8,128)S(1)}, bf16[384,2304]{1,0:T(8,128)(2,1)S(1)}) custom-call(s32[4]{0:T(128)S(1)} %pad_add_fusion.place, bf16[96,1152]{1,0:T(8,128)(2,1)S(1)} %pad_maximum_fusion.refs_0_, bf16[96,1152]{1,0:T(8,128)(2,1)S(1)} %collective-permute-done.3.refs_1_, ...), custom_call_target="tpu_custom_call" | custom-call | flops 1415577600 | bytes 7274496 | tf_op jit(solution)/shard_map/pallas_call | solution.py:131
  46.0 2.1 %collective-permute-done.12 = f32[4,48,896]{2,1,0:T(8,128)S(1)} collective-permute-done((f32[4,48,896]{2,1,0:T(8,128)S(1)}, f32[4,48,896]{2,1,0:T(8,128)S(1)}, u32[]{:S(2)}, u32[]{:S(2)}) %collective-permute-start.12) | collective-permute-done | bytes 688160 | tf_op jit(solution)/shard_map/ppermute | solution.py:38
  48.2 0.6 collective-permute-start.13
  48.9 2.7 %collective-permute-start.15 = (f32[48,896]{1,0:T(8,128)S(1)}, f32[48,896]{1,0:T(8,128)S(1)}, u32[]{:S(2)}, u32[]{:S(2)}) collective-permute-start(f32[48,896]{1,0:T(8,128)S(1)} %get-tuple-element.78), channel_id=1, source_target_pairs={{0,6},{1,7},{2,0},{3,1},{4,2},{5,3},{6,4},{7,5},{8,14},{9,15},{10,... | collective-permute-start | bytes 516104 | tf_op jit(solution)/shard_map/ppermute | solution.py:42
  51.5 4.0 %copy-done.8 = bf16[2304,2304]{1,0:T(8,128)(2,1)S(1)} copy-done((bf16[2304,2304]{1,0:T(8,128)(2,1)S(1)}, bf16[2304,2304]{1,0:T(8,128)(2,1)}, u32[]{:S(2)}) %copy-start.8) | copy-done | bytes 10616856
  55.6 4.3 %shard_map.113 = (bf16[4,48,2304]{2,1,0:T(8,128)(2,1)S(1)}, bf16[4,48,2304]{2,1,0:T(8,128)(2,1)S(1)}) custom-call(bf16[384,2304]{1,0:T(8,128)(2,1)S(1)} %get-tuple-element.43.x_ref, bf16[2304,2304]{1,0:T(8,128)(2,1)S(1)} %copy-done.8), custom_call_target="tpu_custom_call" | custom-call | flops 4076863488 | bytes 14155776 | tf_op jit(solution)/shard_map/pallas_call | solution.py:158
  59.9 0.9 copy-done.5
  60.8 0.9 copy-done.10
  61.9 20.8 %all_to_all.16 = bf16[64,3,896]{2,1,0:T(4,128)(2,1)S(1)} all-to-all(bf16[64,3,896]{2,1,0:T(4,128)(2,1)S(1)} %bitcast.46), channel_id=1, replica_groups={{0,2,4,6,8,10,12,14,16,18,20,22,24,26,28,30,32,34,36,38,40,42,44,46,48,..., dimensions={0} | all-to-all | bytes 688128 | tf_op jit(solution)/shard_map/all_to_all | solution.py:65
  83.1 1.6 collective-permute-done.16.q_ref
  84.7 1.9 %copy-done.1 = bf16[24,256,256]{2,1,0:T(8,128)(2,1)S(1)} copy-done((bf16[24,256,256]{2,1,0:T(8,128)(2,1)S(1)}, bf16[24,256,256]{2,1,0:T(8,128)(2,1)}, u32[]{:S(2)}) %copy-start.1) | copy-done | bytes 3145752
  86.6 2.2 %shard_map.115 = bf16[4,144,384]{2,1,0:T(8,128)(2,1)S(1)} custom-call(s32[4]{0:T(128)S(1)} %pad_add_fusion.place, s32[24]{0:T(128)S(1)} %copy-done.7, bf16[4,48,896]{2,1,0:T(8,128)(2,1)S(1)} %collective-permute-done.16.q_ref, bf16[3,8,256,256]{3,2,1,0:T(8,128)(2,1)S(1)} %bitcast.41, bf16[3,8,256,256]{3,2,1,0:T(8,128)(2,1)S(1)} %bitcast.43), custom_call_target="tpu_custom_call" | custom-call | flops 150994944 | bytes 3932160 | tf_op jit(solution)/shard_map/pallas_call | solution.py:245
  89.1 0.4 collective-permute-start.17
  89.4 2.2 %shard_map.114.a_ref = bf16[4,144,384]{2,1,0:T(8,128)(2,1)S(1)} custom-call(s32[4]{0:T(128)S(1)} %pad_add_fusion.place, s32[24]{0:T(128)S(1)} %copy-done.7, bf16[4,48,896]{2,1,0:T(8,128)(2,1)S(1)} %copy.37.q_ref, bf16[3,8,256,256]{3,2,1,0:T(8,128)(2,1)S(1)} %bitcast.42, bf16[3,8,256,256]{3,2,1,0:T(8,128)(2,1)S(1)} %bitcast.44), custom_call_target="tpu_custom_call" | custom-call | flops 150994944 | bytes 3932160 | tf_op jit(solution)/shard_map/pallas_call | solution.py:245
  92.0 1.6 shard_map.116
  93.5 0.7 collective-permute-start.19
  94.3 1.8 %collective-permute-start.20 = (bf16[48,3456]{1,0:T(8,128)(2,1)S(1)}, bf16[48,3456]{1,0:T(8,128)(2,1)S(1)}, u32[]{:S(2)}, u32[]{:S(2)}) collective-permute-start(bf16[48,3456]{1,0:T(8,128)(2,1)S(1)} %get-tuple-element.54), channel_id=1, source_target_pairs={{0,4},{1,5},{2,6},{3,7},{4,0},{5,1},{6,2},{7,3},{8,12},{9,13},{10,... | collective-permute-start | bytes 995336 | tf_op jit(solution)/shard_map/ppermute | solution.py:42
  96.0 1.5 collective-permute-start.21
  97.6 14.2 %collective-permute-done.19.refs_0_ = bf16[48,3456]{1,0:T(8,128)(2,1)S(1)} collective-permute-done((bf16[48,3456]{1,0:T(8,128)(2,1)S(1)}, bf16[48,3456]{1,0:T(8,128)(2,1)S(1)}, u32[]{:S(2)}, u32[]{:S(2)}) %collective-permute-start.19) | collective-permute-done | bytes 331808 | tf_op jit(solution)/shard_map/ppermute | solution.py:42
  111.8 0.6 collective-permute-done.21.refs_2_
  112.4 1.5 shard_map.117
  114.1 18.0 %all_to_all.17 = bf16[64,4,768]{2,1,0:T(4,128)(2,1)S(1)} all-to-all(bf16[64,4,768]{2,1,0:T(4,128)(2,1)S(1)} %bitcast.47), channel_id=1, replica_groups={{0,2,4,6,8,10,12,14,16,18,20,22,24,26,28,30,32,34,36,38,40,42,44,46,48,..., dimensions={0} | all-to-all | bytes 786432 | tf_op jit(solution)/shard_map/all_to_all | solution.py:65
  132.2 1.7 %collective-permute-done.22.other_ref = bf16[256,768]{1,0:T(8,128)(2,1)S(1)} collective-permute-done((bf16[256,768]{1,0:T(8,128)(2,1)S(1)}, bf16[256,768]{1,0:T(8,128)(2,1)S(1)}, u32[]{:S(2)}, u32[]{:S(2)}) %collective-permute-start.22) | collective-permute-done | bytes 393248 | tf_op jit(solution)/shard_map/ppermute | solution.py:38
  133.9 2.0 %copy-done.9 = bf16[768,2304]{1,0:T(8,128)(2,1)S(1)} copy-done((bf16[768,2304]{1,0:T(8,128)(2,1)S(1)}, bf16[768,2304]{1,0:T(8,128)(2,1)}, u32[]{:S(2)}) %copy-start.9) | copy-done | bytes 3538968
  135.9 3.8 %shard_map.118 = (f32[1,128]{1,0:T(1,128)S(1)}, bf16[96,1152]{1,0:T(8,128)(2,1)S(1)}, bf16[96,1152]{1,0:T(8,128)(2,1)S(1)}, bf16[96,1152]{1,0:T(8,128)(2,1)S(1)}...) custom-call(s32[4]{0:T(128)S(1)} %pad_add_fusion.place, ...), custom_call_target="tpu_custom_call" | custom-call | flops 1358954496 | bytes 5308416 | tf_op jit(solution)/shard_map/pallas_call | solution.py:387
  139.8 0.7 collective-permute-start.23
  140.4 1.8 %collective-permute-start.24 = (bf16[96,1152]{1,0:T(8,128)(2,1)S(1)}, bf16[96,1152]{1,0:T(8,128)(2,1)S(1)}, u32[]{:S(2)}, u32[]{:S(2)}) collective-permute-start(bf16[96,1152]{1,0:T(8,128)(2,1)S(1)} %get-tuple-element.59), channel_id=1, source_target_pairs={{0,64},{8,72},{16,80},{24,88},{32,96},{40,104},{48,112},{56,120},{... | collective-permute-start | bytes 663560 | tf_op jit(solution)/shard_map/ppermute | solution.py:46
  142.3 1.0 collective-permute-start.25
  143.3 0.7 collective-permute-start.29
  144.1 2.1 %collective-permute-start.30 = (bf16[96,1152]{1,0:T(8,128)(2,1)S(1)}, bf16[96,1152]{1,0:T(8,128)(2,1)S(1)}, u32[]{:S(2)}, u32[]{:S(2)}) collective-permute-start(bf16[96,1152]{1,0:T(8,128)(2,1)S(1)} %get-tuple-element.67), channel_id=1, source_target_pairs={{0,16},{8,24},{16,0},{24,8},{32,48},{40,56},{48,32},{56,40},{64,80... | collective-permute-start | bytes 663560 | tf_op jit(solution)/shard_map/ppermute | solution.py:50
  146.1 7.1 %collective-permute-done.23.refs_1_ = bf16[96,1152]{1,0:T(8,128)(2,1)S(1)} collective-permute-done((bf16[96,1152]{1,0:T(8,128)(2,1)S(1)}, bf16[96,1152]{1,0:T(8,128)(2,1)S(1)}, u32[]{:S(2)}, u32[]{:S(2)}) %collective-permute-start.23) | collective-permute-done | bytes 221216 | tf_op jit(solution)/shard_map/ppermute | solution.py:46
  153.2 0.5 collective-permute-start.31
  154.0 1.5 collective-permute-start.26
  155.5 0.7 collective-permute-start.27
  156.1 2.5 %collective-permute-start.28 = (bf16[24,1152]{1,0:T(8,128)(2,1)S(1)}, bf16[24,1152]{1,0:T(8,128)(2,1)S(1)}, u32[]{:S(2)}, u32[]{:S(2)}) collective-permute-start(bf16[24,1152]{1,0:T(8,128)(2,1)S(1)} %get-tuple-element.64), channel_id=1, source_target_pairs={{0,24},{8,0},{16,8},{24,16},{32,56},{40,32},{48,40},{56,48},{64,88... | collective-permute-start | bytes 165896 | tf_op jit(solution)/shard_map/ppermute | solution.py:50
  158.7 1.7 %collective-permute-done.31.refs_3_ = bf16[96,1152]{1,0:T(8,128)(2,1)S(1)} collective-permute-done((bf16[96,1152]{1,0:T(8,128)(2,1)S(1)}, bf16[96,1152]{1,0:T(8,128)(2,1)S(1)}, u32[]{:S(2)}, u32[]{:S(2)}) %collective-permute-start.31) | collective-permute-done | bytes 221216 | tf_op jit(solution)/shard_map/ppermute | solution.py:50
  160.6 1.1 collective-permute-start.33
  161.7 2.1 %collective-permute-start.34 = (bf16[24,1152]{1,0:T(8,128)(2,1)S(1)}, bf16[24,1152]{1,0:T(8,128)(2,1)S(1)}, u32[]{:S(2)}, u32[]{:S(2)}) collective-permute-start(bf16[24,1152]{1,0:T(8,128)(2,1)S(1)} %get-tuple-element.72), channel_id=1, source_target_pairs={{0,96},{8,104},{16,112},{24,120},{32,0},{40,8},{48,16},{56,24},{64... | collective-permute-start | bytes 165896 | tf_op jit(solution)/shard_map/ppermute | solution.py:46
  163.8 0.5 slice_bitcast_fusion.3
  164.3 0.8 shard_map.122
  165.1 1.4 collective-permute-done.32.refs_5_
  166.5 0.9 collective-permute-done.34.refs_7_
  167.4 0.7 shard_map.121
  (67 shorter events, 2.3 us)
Async XLA Ops:
  13.3 8.2 %collective-permute-start.2 = (bf16[24,1152]{1,0:T(8,128)(2,1)S(1)}, bf16[24,1152]{1,0:T(8,128)(2,1)S(1)}, u32[]{:S(2)}, u32[]{:S(2)}) collective-permute-start(bf16[24,1152]{1,0:T(8,128)(2,1)S(1)} %get-tuple-element.81), channel_id=1, source_target_pairs={{0,96},{8,104},{16,112},{24,120},{32,0},{40,8},{48,16},{56,24},{64... | collective-permute-start | bytes 165896 | tf_op jit(solution)/shard_map/ppermute | solution.py:46
  16.1 6.3 %collective-permute-start.1 = (bf16[24,1152]{1,0:T(8,128)(2,1)S(1)}, bf16[24,1152]{1,0:T(8,128)(2,1)S(1)}, u32[]{:S(2)}, u32[]{:S(2)}) collective-permute-start(bf16[24,1152]{1,0:T(8,128)(2,1)S(1)} %get-tuple-element.81), channel_id=1, source_target_pairs={{0,64},{8,72},{16,80},{24,88},{32,96},{40,104},{48,112},{56,120},{... | collective-permute-start | bytes 165896 | tf_op jit(solution)/shard_map/ppermute | solution.py:46
  16.9 5.5 %collective-permute-start = (bf16[24,1152]{1,0:T(8,128)(2,1)S(1)}, bf16[24,1152]{1,0:T(8,128)(2,1)S(1)}, u32[]{:S(2)}, u32[]{:S(2)}) collective-permute-start(bf16[24,1152]{1,0:T(8,128)(2,1)S(1)} %get-tuple-element.81), channel_id=1, source_target_pairs={{0,32},{8,40},{16,48},{24,56},{32,64},{40,72},{48,80},{56,88},{64,... | collective-permute-start | bytes 165896 | tf_op jit(solution)/shard_map/ppermute | solution.py:46
  17.8 8.7 %collective-permute-start.8 = (bf16[24,1152]{1,0:T(8,128)(2,1)S(1)}, bf16[24,1152]{1,0:T(8,128)(2,1)S(1)}, u32[]{:S(2)}, u32[]{:S(2)}) collective-permute-start(bf16[24,1152]{1,0:T(8,128)(2,1)S(1)} %get-tuple-element.80), channel_id=1, source_target_pairs={{0,24},{8,0},{16,8},{24,16},{32,56},{40,32},{48,40},{56,48},{64,88... | collective-permute-start | bytes 165896 | tf_op jit(solution)/shard_map/ppermute | solution.py:50
  20.8 6.3 %collective-permute-start.7 = (bf16[24,1152]{1,0:T(8,128)(2,1)S(1)}, bf16[24,1152]{1,0:T(8,128)(2,1)S(1)}, u32[]{:S(2)}, u32[]{:S(2)}) collective-permute-start(bf16[24,1152]{1,0:T(8,128)(2,1)S(1)} %get-tuple-element.80), channel_id=1, source_target_pairs={{0,16},{8,24},{16,0},{24,8},{32,48},{40,56},{48,32},{56,40},{64,80... | collective-permute-start | bytes 165896 | tf_op jit(solution)/shard_map/ppermute | solution.py:50
  21.4 5.6 %collective-permute-start.6 = (bf16[24,1152]{1,0:T(8,128)(2,1)S(1)}, bf16[24,1152]{1,0:T(8,128)(2,1)S(1)}, u32[]{:S(2)}, u32[]{:S(2)}) collective-permute-start(bf16[24,1152]{1,0:T(8,128)(2,1)S(1)} %get-tuple-element.80), channel_id=1, source_target_pairs={{0,8},{8,16},{16,24},{24,0},{32,40},{40,48},{48,56},{56,32},{64,72... | collective-permute-start | bytes 165896 | tf_op jit(solution)/shard_map/ppermute | solution.py:50
  22.4 11.1 %collective-permute-start.5 = (bf16[96,1152]{1,0:T(8,128)(2,1)S(1)}, bf16[96,1152]{1,0:T(8,128)(2,1)S(1)}, u32[]{:S(2)}, u32[]{:S(2)}) collective-permute-start(bf16[96,1152]{1,0:T(8,128)(2,1)S(1)} %pad_maximum_fusion.refs_0_), channel_id=1, source_target_pairs={{0,24},{8,0},{16,8},{24,16},{32,56},{40,32},{48,40},{56,48},{64,88... | collective-permute-start | bytes 663560 | tf_op jit(solution)/shard_map/ppermute | solution.py:50
  25.4 10.7 %collective-permute-start.4 = (bf16[96,1152]{1,0:T(8,128)(2,1)S(1)}, bf16[96,1152]{1,0:T(8,128)(2,1)S(1)}, u32[]{:S(2)}, u32[]{:S(2)}) collective-permute-start(bf16[96,1152]{1,0:T(8,128)(2,1)S(1)} %pad_maximum_fusion.refs_0_), channel_id=1, source_target_pairs={{0,16},{8,24},{16,0},{24,8},{32,48},{40,56},{48,32},{56,40},{64,80... | collective-permute-start | bytes 663560 | tf_op jit(solution)/shard_map/ppermute | solution.py:50
  26.4 10.7 %collective-permute-start.3 = (bf16[96,1152]{1,0:T(8,128)(2,1)S(1)}, bf16[96,1152]{1,0:T(8,128)(2,1)S(1)}, u32[]{:S(2)}, u32[]{:S(2)}) collective-permute-start(bf16[96,1152]{1,0:T(8,128)(2,1)S(1)} %pad_maximum_fusion.refs_0_), channel_id=1, source_target_pairs={{0,8},{8,16},{16,24},{24,0},{32,40},{40,48},{48,56},{56,32},{64,72... | collective-permute-start | bytes 663560 | tf_op jit(solution)/shard_map/ppermute | solution.py:50
  27.1 10.0 %collective-permute-start.11 = (bf16[96,1152]{1,0:T(8,128)(2,1)S(1)}, bf16[96,1152]{1,0:T(8,128)(2,1)S(1)}, u32[]{:S(2)}, u32[]{:S(2)}) collective-permute-start(bf16[96,1152]{1,0:T(8,128)(2,1)S(1)} %pad_maximum_fusion.1.refs_4_), channel_id=1, source_target_pairs={{0,96},{8,104},{16,112},{24,120},{32,0},{40,8},{48,16},{56,24},{64... | collective-permute-start | bytes 663560 | tf_op jit(solution)/shard_map/ppermute | solution.py:46
  29.8 8.1 %collective-permute-start.10 = (bf16[96,1152]{1,0:T(8,128)(2,1)S(1)}, bf16[96,1152]{1,0:T(8,128)(2,1)S(1)}, u32[]{:S(2)}, u32[]{:S(2)}) collective-permute-start(bf16[96,1152]{1,0:T(8,128)(2,1)S(1)} %pad_maximum_fusion.1.refs_4_), channel_id=1, source_target_pairs={{0,64},{8,72},{16,80},{24,88},{32,96},{40,104},{48,112},{56,120},{... | collective-permute-start | bytes 663560 | tf_op jit(solution)/shard_map/ppermute | solution.py:46
  33.5 7.1 %collective-permute-start.9 = (bf16[96,1152]{1,0:T(8,128)(2,1)S(1)}, bf16[96,1152]{1,0:T(8,128)(2,1)S(1)}, u32[]{:S(2)}, u32[]{:S(2)}) collective-permute-start(bf16[96,1152]{1,0:T(8,128)(2,1)S(1)} %pad_maximum_fusion.1.refs_4_), channel_id=1, source_target_pairs={{0,32},{8,40},{16,48},{24,56},{32,64},{40,72},{48,80},{56,88},{64,... | collective-permute-start | bytes 663560 | tf_op jit(solution)/shard_map/ppermute | solution.py:46
  40.6 2.0 %copy-start.3 = (bf16[2304,768]{1,0:T(8,128)(2,1)S(1)}, bf16[2304,768]{1,0:T(8,128)(2,1)}, u32[]{:S(2)}) copy-start(bf16[2304,768]{1,0:T(8,128)(2,1)} %refs_8_.1) | copy-start | bytes 10616836
  45.9 2.2 %collective-permute-start.12 = (f32[4,48,896]{2,1,0:T(8,128)S(1)}, f32[4,48,896]{2,1,0:T(8,128)S(1)}, u32[]{:S(2)}, u32[]{:S(2)}) collective-permute-start(f32[4,48,896]{2,1,0:T(8,128)S(1)} %get-tuple-element.41), channel_id=1, source_target_pairs={{0,1},{1,0},{2,3},{3,2},{4,5},{5,4},{6,7},{7,6},{8,9},{9,8},{10,11... | collective-permute-start | bytes 2064392 | tf_op jit(solution)/shard_map/ppermute | solution.py:38
  48.2 13.4 %collective-permute-start.13 = (f32[48,896]{1,0:T(8,128)S(1)}, f32[48,896]{1,0:T(8,128)S(1)}, u32[]{:S(2)}, u32[]{:S(2)}) collective-permute-start(f32[48,896]{1,0:T(8,128)S(1)} %get-tuple-element.77), channel_id=1, source_target_pairs={{0,2},{1,3},{2,4},{3,5},{4,6},{5,7},{6,0},{7,1},{8,10},{9,11},{10,... | collective-permute-start | bytes 516104 | tf_op jit(solution)/shard_map/ppermute | solution.py:42
  48.9 12.8 %collective-permute-start.15 = (f32[48,896]{1,0:T(8,128)S(1)}, f32[48,896]{1,0:T(8,128)S(1)}, u32[]{:S(2)}, u32[]{:S(2)}) collective-permute-start(f32[48,896]{1,0:T(8,128)S(1)} %get-tuple-element.78), channel_id=1, source_target_pairs={{0,6},{1,7},{2,0},{3,1},{4,2},{5,3},{6,4},{7,5},{8,14},{9,15},{10,... | collective-permute-start | bytes 516104 | tf_op jit(solution)/shard_map/ppermute | solution.py:42
  51.5 10.1 %collective-permute-start.14 = (f32[48,896]{1,0:T(8,128)S(1)}, f32[48,896]{1,0:T(8,128)S(1)}, u32[]{:S(2)}, u32[]{:S(2)}) collective-permute-start(f32[48,896]{1,0:T(8,128)S(1)} %get-tuple-element.79), channel_id=1, source_target_pairs={{0,4},{1,5},{2,6},{3,7},{4,0},{5,1},{6,2},{7,3},{8,12},{9,13},{10,... | collective-permute-start | bytes 516104 | tf_op jit(solution)/shard_map/ppermute | solution.py:42
  51.5 4.0 %copy-start.8 = (bf16[2304,2304]{1,0:T(8,128)(2,1)S(1)}, bf16[2304,2304]{1,0:T(8,128)(2,1)}, u32[]{:S(2)}) copy-start(bf16[2304,2304]{1,0:T(8,128)(2,1)} %w_ref.2) | copy-start | bytes 31850500
  59.8 0.9 copy-start.5
  60.8 0.9 copy-start.10
  61.7 23.0 %copy-start = (bf16[24,256,256]{2,1,0:T(8,128)(2,1)S(1)}, bf16[24,256,256]{2,1,0:T(8,128)(2,1)}, u32[]{:S(2)}) copy-start(bf16[24,256,256]{2,1,0:T(8,128)(2,1)} %param.15) | copy-start | bytes 9437188
  61.7 23.0 %copy-start.7 = (s32[24]{0:T(128)S(1)}, s32[24]{0:T(128)}, u32[]{:S(2)}) copy-start(s32[24]{0:T(128)} %lengths.3) | copy-start | bytes 292
  83.0 1.7 %collective-permute-start.16 = (bf16[4,48,896]{2,1,0:T(8,128)(2,1)S(1)}, bf16[4,48,896]{2,1,0:T(8,128)(2,1)S(1)}, u32[]{:S(2)}, u32[]{:S(2)}) collective-permute-start(bf16[4,48,896]{2,1,0:T(8,128)(2,1)S(1)} %copy.37.q_ref), channel_id=1, source_target_pairs={{0,1},{1,0},{2,3},{3,2},{4,5},{5,4},{6,7},{7,6},{8,9},{9,8},{10,11... | collective-permute-start | bytes 1032200 | tf_op jit(solution)/shard_map/ppermute | solution.py:38
  84.7 1.9 %copy-start.1 = (bf16[24,256,256]{2,1,0:T(8,128)(2,1)S(1)}, bf16[24,256,256]{2,1,0:T(8,128)(2,1)}, u32[]{:S(2)}) copy-start(bf16[24,256,256]{2,1,0:T(8,128)(2,1)} %param.16) | copy-start | bytes 9437188
  86.6 2.2 %copy-start.11 = (bf16[4,48,2304]{2,1,0:T(8,128)(2,1)S(1)}, bf16[4,48,2304]{2,1,0:T(8,128)(2,1)}, u32[]{:S(2)}) copy-start(bf16[4,48,2304]{2,1,0:T(8,128)(2,1)} %copy-done.10) | copy-start | bytes 2654212
  86.6 2.8 %copy-start.2 = (bf16[24,256,256]{2,1,0:T(8,128)(2,1)S(1)}, bf16[24,256,256]{2,1,0:T(8,128)(2,1)}, u32[]{:S(2)}) copy-start(bf16[24,256,256]{2,1,0:T(8,128)(2,1)} %param.16) | copy-start | bytes 9437188
  88.8 3.2 %copy-start.6 = (bf16[4,48,2304]{2,1,0:T(8,128)(2,1)S(1)}, bf16[4,48,2304]{2,1,0:T(8,128)(2,1)}, u32[]{:S(2)}) copy-start(bf16[4,48,2304]{2,1,0:T(8,128)(2,1)} %copy-done.5) | copy-start | bytes 2654212
  88.8 3.1 %collective-permute-start.18 = (bf16[4,48,2304]{2,1,0:T(8,128)(2,1)S(1)}, bf16[4,48,2304]{2,1,0:T(8,128)(2,1)S(1)}, u32[]{:S(2)}, u32[]{:S(2)}) collective-permute-start(bf16[4,48,2304]{2,1,0:T(8,128)(2,1)S(1)} %copy-done.11), channel_id=1, source_target_pairs={{0,1},{1,0},{2,3},{3,2},{4,5},{5,4},{6,7},{7,6},{8,9},{9,8},{10,11... | collective-permute-start | bytes 2654216 | tf_op jit(solution)/shard_map/ppermute | solution.py:38
  89.1 2.9 %collective-permute-start.17 = (bf16[4,144,384]{2,1,0:T(8,128)(2,1)S(1)}, bf16[4,144,384]{2,1,0:T(8,128)(2,1)S(1)}, u32[]{:S(2)}, u32[]{:S(2)}) collective-permute-start(bf16[4,144,384]{2,1,0:T(8,128)(2,1)S(1)} %shard_map.115), channel_id=1, source_target_pairs={{0,1},{1,0},{2,3},{3,2},{4,5},{5,4},{6,7},{7,6},{8,9},{9,8},{10,11... | collective-permute-start | bytes 1327112 | tf_op jit(solution)/shard_map/ppermute | solution.py:38
  93.5 18.2 %collective-permute-start.19 = (bf16[48,3456]{1,0:T(8,128)(2,1)S(1)}, bf16[48,3456]{1,0:T(8,128)(2,1)S(1)}, u32[]{:S(2)}, u32[]{:S(2)}) collective-permute-start(bf16[48,3456]{1,0:T(8,128)(2,1)S(1)} %get-tuple-element.53), channel_id=1, source_target_pairs={{0,2},{1,3},{2,4},{3,5},{4,6},{5,7},{6,0},{7,1},{8,10},{9,11},{10,... | collective-permute-start | bytes 995336 | tf_op jit(solution)/shard_map/ppermute | solution.py:42
  94.3 17.5 %collective-permute-start.20 = (bf16[48,3456]{1,0:T(8,128)(2,1)S(1)}, bf16[48,3456]{1,0:T(8,128)(2,1)S(1)}, u32[]{:S(2)}, u32[]{:S(2)}) collective-permute-start(bf16[48,3456]{1,0:T(8,128)(2,1)S(1)} %get-tuple-element.54), channel_id=1, source_target_pairs={{0,4},{1,5},{2,6},{3,7},{4,0},{5,1},{6,2},{7,3},{8,12},{9,13},{10,... | collective-permute-start | bytes 995336 | tf_op jit(solution)/shard_map/ppermute | solution.py:42
  96.0 16.3 %collective-permute-start.21 = (bf16[48,3456]{1,0:T(8,128)(2,1)S(1)}, bf16[48,3456]{1,0:T(8,128)(2,1)S(1)}, u32[]{:S(2)}, u32[]{:S(2)}) collective-permute-start(bf16[48,3456]{1,0:T(8,128)(2,1)S(1)} %get-tuple-element.55), channel_id=1, source_target_pairs={{0,6},{1,7},{2,0},{3,1},{4,2},{5,3},{6,4},{7,5},{8,14},{9,15},{10,... | collective-permute-start | bytes 995336 | tf_op jit(solution)/shard_map/ppermute | solution.py:42
  132.1 35.2 %copy-start.4 = (bf16[24,2304]{1,0:T(8,128)(2,1)S(1)}, bf16[24,2304]{1,0:T(8,128)(2,1)}, u32[]{:S(2)}) copy-start(bf16[24,2304]{1,0:T(8,128)(2,1)} %residual_ref.1) | copy-start | bytes 331780
  132.1 1.8 %collective-permute-start.22 = (bf16[256,768]{1,0:T(8,128)(2,1)S(1)}, bf16[256,768]{1,0:T(8,128)(2,1)S(1)}, u32[]{:S(2)}, u32[]{:S(2)}) collective-permute-start(bf16[256,768]{1,0:T(8,128)(2,1)S(1)} %reshape.60.own_ref), channel_id=1, source_target_pairs={{0,1},{1,0},{2,3},{3,2},{4,5},{5,4},{6,7},{7,6},{8,9},{9,8},{10,11... | collective-permute-start | bytes 1179656 | tf_op jit(solution)/shard_map/ppermute | solution.py:38
  133.9 2.0 %copy-start.9 = (bf16[768,2304]{1,0:T(8,128)(2,1)S(1)}, bf16[768,2304]{1,0:T(8,128)(2,1)}, u32[]{:S(2)}) copy-start(bf16[768,2304]{1,0:T(8,128)(2,1)} %w_ref.3) | copy-start | bytes 10616836
  139.8 13.5 %collective-permute-start.23 = (bf16[96,1152]{1,0:T(8,128)(2,1)S(1)}, bf16[96,1152]{1,0:T(8,128)(2,1)S(1)}, u32[]{:S(2)}, u32[]{:S(2)}) collective-permute-start(bf16[96,1152]{1,0:T(8,128)(2,1)S(1)} %get-tuple-element.58), channel_id=1, source_target_pairs={{0,32},{8,40},{16,48},{24,56},{32,64},{40,72},{48,80},{56,88},{64,... | collective-permute-start | bytes 663560 | tf_op jit(solution)/shard_map/ppermute | solution.py:46
  140.4 13.3 %collective-permute-start.24 = (bf16[96,1152]{1,0:T(8,128)(2,1)S(1)}, bf16[96,1152]{1,0:T(8,128)(2,1)S(1)}, u32[]{:S(2)}, u32[]{:S(2)}) collective-permute-start(bf16[96,1152]{1,0:T(8,128)(2,1)S(1)} %get-tuple-element.59), channel_id=1, source_target_pairs={{0,64},{8,72},{16,80},{24,88},{32,96},{40,104},{48,112},{56,120},{... | collective-permute-start | bytes 663560 | tf_op jit(solution)/shard_map/ppermute | solution.py:46
  142.3 11.6 %collective-permute-start.25 = (bf16[96,1152]{1,0:T(8,128)(2,1)S(1)}, bf16[96,1152]{1,0:T(8,128)(2,1)S(1)}, u32[]{:S(2)}, u32[]{:S(2)}) collective-permute-start(bf16[96,1152]{1,0:T(8,128)(2,1)S(1)} %get-tuple-element.60), channel_id=1, source_target_pairs={{0,96},{8,104},{16,112},{24,120},{32,0},{40,8},{48,16},{56,24},{64... | collective-permute-start | bytes 663560 | tf_op jit(solution)/shard_map/ppermute | solution.py:46
  143.3 12.8 %collective-permute-start.29 = (bf16[96,1152]{1,0:T(8,128)(2,1)S(1)}, bf16[96,1152]{1,0:T(8,128)(2,1)S(1)}, u32[]{:S(2)}, u32[]{:S(2)}) collective-permute-start(bf16[96,1152]{1,0:T(8,128)(2,1)S(1)} %get-tuple-element.66), channel_id=1, source_target_pairs={{0,8},{8,16},{16,24},{24,0},{32,40},{40,48},{48,56},{56,32},{64,72... | collective-permute-start | bytes 663560 | tf_op jit(solution)/shard_map/ppermute | solution.py:50
  144.1 14.6 %collective-permute-start.30 = (bf16[96,1152]{1,0:T(8,128)(2,1)S(1)}, bf16[96,1152]{1,0:T(8,128)(2,1)S(1)}, u32[]{:S(2)}, u32[]{:S(2)}) collective-permute-start(bf16[96,1152]{1,0:T(8,128)(2,1)S(1)} %get-tuple-element.67), channel_id=1, source_target_pairs={{0,16},{8,24},{16,0},{24,8},{32,48},{40,56},{48,32},{56,40},{64,80... | collective-permute-start | bytes 663560 | tf_op jit(solution)/shard_map/ppermute | solution.py:50
  153.2 7.1 %collective-permute-start.31 = (bf16[96,1152]{1,0:T(8,128)(2,1)S(1)}, bf16[96,1152]{1,0:T(8,128)(2,1)S(1)}, u32[]{:S(2)}, u32[]{:S(2)}) collective-permute-start(bf16[96,1152]{1,0:T(8,128)(2,1)S(1)} %get-tuple-element.68), channel_id=1, source_target_pairs={{0,24},{8,0},{16,8},{24,16},{32,56},{40,32},{48,40},{56,48},{64,88... | collective-permute-start | bytes 663560 | tf_op jit(solution)/shard_map/ppermute | solution.py:50
  154.0 7.7 %collective-permute-start.26 = (bf16[24,1152]{1,0:T(8,128)(2,1)S(1)}, bf16[24,1152]{1,0:T(8,128)(2,1)S(1)}, u32[]{:S(2)}, u32[]{:S(2)}) collective-permute-start(bf16[24,1152]{1,0:T(8,128)(2,1)S(1)} %get-tuple-element.62), channel_id=1, source_target_pairs={{0,8},{8,16},{16,24},{24,0},{32,40},{40,48},{48,56},{56,32},{64,72... | collective-permute-start | bytes 165896 | tf_op jit(solution)/shard_map/ppermute | solution.py:50
  155.5 9.6 %collective-permute-start.27 = (bf16[24,1152]{1,0:T(8,128)(2,1)S(1)}, bf16[24,1152]{1,0:T(8,128)(2,1)S(1)}, u32[]{:S(2)}, u32[]{:S(2)}) collective-permute-start(bf16[24,1152]{1,0:T(8,128)(2,1)S(1)} %get-tuple-element.63), channel_id=1, source_target_pairs={{0,16},{8,24},{16,0},{24,8},{32,48},{40,56},{48,32},{56,40},{64,80... | collective-permute-start | bytes 165896 | tf_op jit(solution)/shard_map/ppermute | solution.py:50
  156.1 9.0 %collective-permute-start.28 = (bf16[24,1152]{1,0:T(8,128)(2,1)S(1)}, bf16[24,1152]{1,0:T(8,128)(2,1)S(1)}, u32[]{:S(2)}, u32[]{:S(2)}) collective-permute-start(bf16[24,1152]{1,0:T(8,128)(2,1)S(1)} %get-tuple-element.64), channel_id=1, source_target_pairs={{0,24},{8,0},{16,8},{24,16},{32,56},{40,32},{48,40},{56,48},{64,88... | collective-permute-start | bytes 165896 | tf_op jit(solution)/shard_map/ppermute | solution.py:50
  160.5 6.0 %collective-permute-start.32 = (bf16[24,1152]{1,0:T(8,128)(2,1)S(1)}, bf16[24,1152]{1,0:T(8,128)(2,1)S(1)}, u32[]{:S(2)}, u32[]{:S(2)}) collective-permute-start(bf16[24,1152]{1,0:T(8,128)(2,1)S(1)} %get-tuple-element.70), channel_id=1, source_target_pairs={{0,32},{8,40},{16,48},{24,56},{32,64},{40,72},{48,80},{56,88},{64,... | collective-permute-start | bytes 165896 | tf_op jit(solution)/shard_map/ppermute | solution.py:46
  160.6 5.9 %collective-permute-start.33 = (bf16[24,1152]{1,0:T(8,128)(2,1)S(1)}, bf16[24,1152]{1,0:T(8,128)(2,1)S(1)}, u32[]{:S(2)}, u32[]{:S(2)}) collective-permute-start(bf16[24,1152]{1,0:T(8,128)(2,1)S(1)} %get-tuple-element.71), channel_id=1, source_target_pairs={{0,64},{8,72},{16,80},{24,88},{32,96},{40,104},{48,112},{56,120},{... | collective-permute-start | bytes 165896 | tf_op jit(solution)/shard_map/ppermute | solution.py:46
  161.7 5.7 %collective-permute-start.34 = (bf16[24,1152]{1,0:T(8,128)(2,1)S(1)}, bf16[24,1152]{1,0:T(8,128)(2,1)S(1)}, u32[]{:S(2)}, u32[]{:S(2)}) collective-permute-start(bf16[24,1152]{1,0:T(8,128)(2,1)S(1)} %get-tuple-element.72), channel_id=1, source_target_pairs={{0,96},{8,104},{16,112},{24,120},{32,0},{40,8},{48,16},{56,24},{64... | collective-permute-start | bytes 165896 | tf_op jit(solution)/shard_map/ppermute | solution.py:46

commit v4 on v3

--- a/solution.py
+++ b/solution.py
@@ -26,6 +26,7 @@
 UPCOLS = 36864 // WIDE
 HALF = FEATS // 2
 SPAN = RING * LOCAL
+UP_PIECES = (256, 1024, 1024)
 
 norm_eps = 1e-05
 peak_eps = 1e-06
@@ -82,6 +83,7 @@
 
 
 WHOLE = pl.BlockSpec(memory_space=pltpu.VMEM)
+HBM = pl.BlockSpec(memory_space=pltpu.HBM)
 
 
 def slot_of(wide, z, c):
@@ -143,24 +145,45 @@
     )(place, *left, *right, w_query, w_keyval)
 
 
-def up_kernel(x_ref, w_ref, keep_ref, send_ref):
+def up_kernel(x_ref, weights_ref, keep_ref, send_ref, w_ref, sum_ref, sem):
     half, tile = ROWS // 2, 768
-    for first in range(0, UPCOLS, tile):
-        columns = slice(first, first + tile)
-        terms = dot(x_ref[...], w_ref[:, columns]).astype(bf16)
-        for at in range(RING):
-            keep_ref[at, :, columns] = terms[at * SHARE : (at + 1) * SHARE]
-            send_ref[at, :, columns] = terms[half + at * SHARE : half + (at + 1) * SHARE]
+    copies, spans, at = [], [], 0
+    for count in UP_PIECES:
+        span = slice(at, at + count)
+        copies.append(pltpu.make_async_copy(weights_ref.at[span], w_ref.at[span], sem.at[len(spans)]))
+        spans.append(span)
+        at += count
+    for copy in copies:
+        copy.start()
+    for piece, (copy, span) in enumerate(zip(copies, spans)):
+        copy.wait()
+        for first in range(0, UPCOLS, tile):
+            columns = slice(first, first + tile)
+            terms = dot(x_ref[:, span], w_ref[span, columns])
+            if piece:
+                terms += sum_ref[:, columns]
+            if piece + 1 < len(spans):
+                sum_ref[:, columns] = terms
+                continue
+            terms = terms.astype(bf16)
+            for at in range(RING):
+                keep_ref[at, :, columns] = terms[at * SHARE : (at + 1) * SHARE]
+                send_ref[at, :, columns] = terms[half + at * SHARE : half + (at + 1) * SHARE]
 
 
 def up_terms(x, w_up):
     out = jax.ShapeDtypeStruct((RING, SHARE, UPCOLS), bf16)
     return pl.pallas_call(
         up_kernel,
-        in_specs=[WHOLE] * 2,
+        in_specs=[WHOLE, HBM],
         out_specs=[WHOLE] * 2,
         out_shape=[out, out],
-        compiler_params=params(4),
+        scratch_shapes=[
+            pltpu.VMEM(w_up.shape, bf16),
+            pltpu.VMEM((ROWS, UPCOLS), f32),
+            pltpu.SemaphoreType.DMA((len(UP_PIECES),)),
+        ],
+        compiler_params=params(48),
         cost_estimate=cost(2 * ROWS * FEATS * UPCOLS, 2 * (FEATS * (ROWS + UPCOLS) + ROWS * UPCOLS)),
     )(x, w_up)
 
@@ -201,19 +224,28 @@
     return jnp.concatenate([rows[:, h * HEAD : (h + 1) * HEAD] for h in range(HELD)], axis=0)
 
 
-def attend_kernel(away, place, lengths, q_ref, k_ref, v_ref, out_ref):
+def attend_kernel(away, place, lengths, q_ref, keys_ref, values_ref, out_ref, k_ref, v_ref, sem):
+    groups = [group_of(away, step, place) for step in range(RING)]
+    copies = [
+        [pltpu.make_async_copy(source.at[:, group], held.at[step], sem.at[at, step]) for step, group in enumerate(groups)]
+        for at, (source, held) in enumerate(((keys_ref, k_ref), (values_ref, v_ref)))
+    ]
+    for copy in copies[0] + copies[1]:
+        copy.start()
     positions = k_ref.shape[2]
     start = (place[0] * 2 + place[1]) * positions
     position = lax.broadcasted_iota(jnp.int32, (HEADS, positions), 1) + start
-    for step in range(RING):
-        group = group_of(away, step, place)
-        rows = by_row(q_ref[lax.rem(place[0] + step, RING)])
+    rows = [by_row(q_ref[lax.rem(place[0] + step, RING)]) for step in range(RING)]
+    for copy in copies[0]:
+        copy.wait()
+    weights = []
+    for step, group in enumerate(groups):
         valid = jnp.concatenate([position < lengths[j * NARROW + group] for j in range(EACH)], axis=0)
         scores = jnp.concatenate(
             [
                 lax.dot_general(
-                    heads_of(rows[j * WIDE : (j + 1) * WIDE]).astype(bf16),
-                    k_ref[j, group],
+                    heads_of(rows[step][j * WIDE : (j + 1) * WIDE]).astype(bf16),
+                    k_ref[step, j],
                     (((1,), (1,)), ((), ())),
                     preferred_element_type=f32,
                 )
@@ -224,12 +256,14 @@
         masked = jnp.where(valid, scores * (1.0 / HEAD**0.5), f32(-1e30))
         top = jnp.max(masked, axis=1, keepdims=True)
         probs = jnp.where(valid, jnp.exp(masked - top), f32(0.0))
-        total = jnp.sum(probs, axis=1, keepdims=True)
-        weights = probs.astype(bf16)
+        out_ref[step, :, HEAD:] = packed(top, jnp.sum(probs, axis=1, keepdims=True))
+        weights.append(probs.astype(bf16))
+    for copy in copies[1]:
+        copy.wait()
+    for step in range(RING):
         for j in range(EACH):
             span = slice(j * HEADS, (j + 1) * HEADS)
-            out_ref[step, span, :HEAD] = dot(weights[span], v_ref[j, group]).astype(bf16)
-        out_ref[step, :, HEAD:] = packed(top, total)
+            out_ref[step, span, :HEAD] = dot(weights[step][span], v_ref[step, j]).astype(bf16)
 
 
 def group_of(away, step, place):
@@ -247,11 +281,12 @@
         grid_spec=pltpu.PrefetchScalarGridSpec(
             num_scalar_prefetch=2,
             grid=(1,),
-            in_specs=[WHOLE] * 3,
+            in_specs=[WHOLE, HBM, HBM],
             out_specs=WHOLE,
+            scratch_shapes=[pltpu.VMEM((RING, EACH, positions, HEAD), bf16)] * 2 + [pltpu.SemaphoreType.DMA((2, RING))],
         ),
         out_shape=out,
-        compiler_params=params(3),
+        compiler_params=params(53),
         cost_estimate=cost(2 * LOCAL * HEADS * positions * HEAD, 2 * k_cache.size + 2 * out.size + 2 * query.size),
     )(place, lengths, query, k_cache, v_cache)
 

time: 169 us -> 165 us (0.976)
  local copies, waits for them, and re-layouts: 14.1 us -> 6.39 us
  Pallas kernels: 20.5 us -> 25.3 us
    unnamed x25 -> x9, local copies, waits for them, and re-layouts: 13 us -> 5.24 us
    pallas_call x1, Pallas kernels: 4.27 us -> 7.1 us  [up_terms(): pl.pallas_call(up_kernel, in_specs=[WHOLE, HBM], out_specs=[WHOLE] * 2, o...]
    pallas_call x2, Pallas kernels: 4.41 us -> 6.35 us  [attend(): pl.pallas_call(functools.partial(attend_kernel, away), grid_spec=pltpu.Pr...]
  transfers between devices with their start and end apart: 35 -> 35, of which waited for: 15 -> 15; matrix products, arithmetic and copies ran while one was open for 1% -> 1% of each run, Pallas kernels for 4% -> 7%
where the time goes in v4:
time: 165 us
  blocking collectives  48.3 us (29%)
  starting transfers between devices  42.4 us (26%)
  waiting for transfers between devices  39.1 us (24%)
  Pallas kernels  25.3 us (15%)
  local copies, waits for them, and re-layouts  6.39 us (4%)
  other arithmetic  2.31 us (1%)
    all_to_all x2, blocking collectives, spread(): lax.all_to_all(x, ('wide', 'narrow'), 0, 0, axis_index_groups=SAME_CORE,...  37.8 us
    ppermute x12, starting transfers between devices, shift_y(): lax.ppermute(x, 'wide', [(i, i // RING * RING + (i + by) % RING) for i in...  17.2 us
    ppermute x12, starting transfers between devices, shift_x(): lax.ppermute(x, 'wide', [(i, (i // RING + by) % RING * RING + i % RING) f...  17 us
    ppermute x6, waiting for transfers between devices, shift_z(): lax.ppermute(x, 'narrow', [(i, (i // 2 + by) % RING * 2 + i % 2) for i in...  15.8 us
    ppermute x12, waiting for transfers between devices, shift_x(): lax.ppermute(x, 'wide', [(i, (i // RING + by) % RING * RING + i % RING) f...  13 us
    all_to_all x1, blocking collectives, shards(): lax.all_to_all(jnp.broadcast_to(sums[None], (NARROW,) + sums.shape), 'nar...  10.5 us
    ppermute x6, starting transfers between devices, shift_z(): lax.ppermute(x, 'narrow', [(i, (i // 2 + by) % RING * 2 + i % 2) for i in...  7.34 us
    pallas_call x1, Pallas kernels, up_terms(): pl.pallas_call(up_kernel, in_specs=[WHOLE, HBM], out_specs=[WHOLE] * 2, o...  7.1 us
  transfers between devices with their start and end apart: 35, of which 15 were waited for; matrix products, arithmetic and copies ran while one was open for 1% of the time, Pallas kernels for 7%

profile of v4, /device:TPU:0, one launch (start us, length us, event | category | flops | bytes accessed | tf_op | source)
XLA Modules:
  0.0 164.7 jit_solution(5986225931451622320)
XLA Ops:
  0.6 1.0 convert_reduce_fusion
  1.7 10.5 %all_to_all.15 = f32[8,2,24]{2,1,0:T(2,128)S(1)} all-to-all(f32[8,2,24]{2,1,0:T(2,128)S(1)} %broadcast_in_dim.10), channel_id=1, replica_groups=mesh['wide'=16,'narrow'=8] {'narrow'}, dimensions={0} | all-to-all | bytes 3072 | tf_op jit(solution)/shard_map/all_to_all | solution.py:499
  12.2 1.0 fusion.3
  13.3 2.8 %collective-permute-start.2 = (bf16[24,1152]{1,0:T(8,128)(2,1)S(1)}, bf16[24,1152]{1,0:T(8,128)(2,1)S(1)}, u32[]{:S(2)}, u32[]{:S(2)}) collective-permute-start(bf16[24,1152]{1,0:T(8,128)(2,1)S(1)} %get-tuple-element.81), channel_id=1, source_target_pairs={{0,96},{8,104},{16,112},{24,120},{32,0},{40,8},{48,16},{56,24},{64... | collective-permute-start | bytes 165896 | tf_op jit(solution)/shard_map/ppermute | solution.py:47
  16.1 0.8 collective-permute-start.1
  16.9 0.9 collective-permute-start
  17.8 3.0 %collective-permute-start.8 = (bf16[24,1152]{1,0:T(8,128)(2,1)S(1)}, bf16[24,1152]{1,0:T(8,128)(2,1)S(1)}, u32[]{:S(2)}, u32[]{:S(2)}) collective-permute-start(bf16[24,1152]{1,0:T(8,128)(2,1)S(1)} %get-tuple-element.80), channel_id=1, source_target_pairs={{0,24},{8,0},{16,8},{24,16},{32,56},{40,32},{48,40},{56,48},{64,88... | collective-permute-start | bytes 165896 | tf_op jit(solution)/shard_map/ppermute | solution.py:51
  20.8 0.6 collective-permute-start.7
  21.4 1.0 collective-permute-start.6
  22.4 3.0 %collective-permute-start.5 = (bf16[96,1152]{1,0:T(8,128)(2,1)S(1)}, bf16[96,1152]{1,0:T(8,128)(2,1)S(1)}, u32[]{:S(2)}, u32[]{:S(2)}) collective-permute-start(bf16[96,1152]{1,0:T(8,128)(2,1)S(1)} %pad_maximum_fusion.refs_0_), channel_id=1, source_target_pairs={{0,24},{8,0},{16,8},{24,16},{32,56},{40,32},{48,40},{56,48},{64,88... | collective-permute-start | bytes 663560 | tf_op jit(solution)/shard_map/ppermute | solution.py:51
  25.4 1.0 collective-permute-start.4
  26.4 0.6 collective-permute-start.3
  27.1 2.8 %collective-permute-start.11 = (bf16[96,1152]{1,0:T(8,128)(2,1)S(1)}, bf16[96,1152]{1,0:T(8,128)(2,1)S(1)}, u32[]{:S(2)}, u32[]{:S(2)}) collective-permute-start(bf16[96,1152]{1,0:T(8,128)(2,1)S(1)} %pad_maximum_fusion.1.refs_4_), channel_id=1, source_target_pairs={{0,96},{8,104},{16,112},{24,120},{32,0},{40,8},{48,16},{56,24},{64... | collective-permute-start | bytes 663560 | tf_op jit(solution)/shard_map/ppermute | solution.py:47
  29.8 1.5 collective-permute-start.10
  31.4 2.1 %collective-permute-done.5.refs_3_ = bf16[96,1152]{1,0:T(8,128)(2,1)S(1)} collective-permute-done((bf16[96,1152]{1,0:T(8,128)(2,1)S(1)}, bf16[96,1152]{1,0:T(8,128)(2,1)S(1)}, u32[]{:S(2)}, u32[]{:S(2)}) %collective-permute-start.5) | collective-permute-done | bytes 221216 | tf_op jit(solution)/shard_map/ppermute | solution.py:51
  33.5 1.3 collective-permute-start.9
  34.8 1.2 copy.32.refs_9_
  36.1 1.0 collective-permute-done.3.refs_1_
  37.1 0.8 collective-permute-done.10.refs_6_
  37.9 2.7 %collective-permute-done.9.refs_5_ = bf16[96,1152]{1,0:T(8,128)(2,1)S(1)} collective-permute-done((bf16[96,1152]{1,0:T(8,128)(2,1)S(1)}, bf16[96,1152]{1,0:T(8,128)(2,1)S(1)}, u32[]{:S(2)}, u32[]{:S(2)}) %collective-permute-start.9) | collective-permute-done | bytes 221216 | tf_op jit(solution)/shard_map/ppermute | solution.py:47
  40.6 2.0 %copy-done = bf16[2304,768]{1,0:T(8,128)(2,1)S(1)} copy-done((bf16[2304,768]{1,0:T(8,128)(2,1)S(1)}, bf16[2304,768]{1,0:T(8,128)(2,1)}, u32[]{:S(2)}) %copy-start) | copy-done | bytes 3538968
  42.6 3.2 %shard_map.112 = (f32[4,48,896]{2,1,0:T(8,128)S(1)}, f32[4,48,896]{2,1,0:T(8,128)S(1)}, bf16[384,2304]{1,0:T(8,128)(2,1)S(1)}) custom-call(s32[4]{0:T(128)S(1)} %pad_add_fusion.place, bf16[96,1152]{1,0:T(8,128)(2,1)S(1)} %pad_maximum_fusion.refs_0_, bf16[96,1152]{1,0:T(8,128)(2,1)S(1)} %collective-permute-done.3.refs_1_, ...), custom_call_target="tpu_custom_call" | custom-call | flops 1415577600 | bytes 7274496 | tf_op jit(solution)/shard_map/pallas_call | solution.py:133
  46.0 2.1 %collective-permute-done.12 = f32[4,48,896]{2,1,0:T(8,128)S(1)} collective-permute-done((f32[4,48,896]{2,1,0:T(8,128)S(1)}, f32[4,48,896]{2,1,0:T(8,128)S(1)}, u32[]{:S(2)}, u32[]{:S(2)}) %collective-permute-start.12) | collective-permute-done | bytes 688160 | tf_op jit(solution)/shard_map/ppermute | solution.py:39
  48.2 0.6 collective-permute-start.13
  48.9 2.7 %collective-permute-start.15 = (f32[48,896]{1,0:T(8,128)S(1)}, f32[48,896]{1,0:T(8,128)S(1)}, u32[]{:S(2)}, u32[]{:S(2)}) collective-permute-start(f32[48,896]{1,0:T(8,128)S(1)} %get-tuple-element.78), channel_id=1, source_target_pairs={{0,6},{1,7},{2,0},{3,1},{4,2},{5,3},{6,4},{7,5},{8,14},{9,15},{10,... | collective-permute-start | bytes 516104 | tf_op jit(solution)/shard_map/ppermute | solution.py:43
  51.5 7.1 %shard_map.113 = (bf16[4,48,2304]{2,1,0:T(8,128)(2,1)S(1)}, bf16[4,48,2304]{2,1,0:T(8,128)(2,1)S(1)}) custom-call(bf16[384,2304]{1,0:T(8,128)(2,1)S(1)} %get-tuple-element.43.x_ref, bf16[2304,2304]{1,0:T(8,128)(2,1)} %weights_ref.1), custom_call_target="tpu_custom_call" | custom-call | flops 4076863488 | bytes 14155776 | tf_op jit(solution)/shard_map/pallas_call | solution.py:176
  58.7 0.9 collective-permute-done.13
  59.9 19.8 %all_to_all.16 = bf16[64,3,896]{2,1,0:T(4,128)(2,1)S(1)} all-to-all(bf16[64,3,896]{2,1,0:T(4,128)(2,1)S(1)} %bitcast.46), channel_id=1, replica_groups={{0,2,4,6,8,10,12,14,16,18,20,22,24,26,28,30,32,34,36,38,40,42,44,46,48,..., dimensions={0} | all-to-all | bytes 688128 | tf_op jit(solution)/shard_map/all_to_all | solution.py:66
  79.6 0.1 copy.34
  79.9 1.6 collective-permute-done.16.q_ref
  81.6 3.2 %shard_map.115 = bf16[4,144,384]{2,1,0:T(8,128)(2,1)S(1)} custom-call(s32[4]{0:T(128)S(1)} %pad_add_fusion.place, s32[24]{0:T(128)S(1)} %copy-done.2, bf16[4,48,896]{2,1,0:T(8,128)(2,1)S(1)} %collective-permute-done.16.q_ref, bf16[3,8,256,256]{3,2,1,0:T(8,128)(2,1)} %bitcast.41, bf16[3,8,256,256]{3,2,1,0:T(8,128)(2,1)} %bitcast.43), custom_call_target="tpu_custom_call" | custom-call | flops 150994944 | bytes 3932160 | tf_op jit(solution)/shard_map/pallas_call | solution.py:279
  84.8 0.2 collective-permute-start.18
  85.0 0.4 collective-permute-start.17
  85.4 3.2 %shard_map.114.a_ref = bf16[4,144,384]{2,1,0:T(8,128)(2,1)S(1)} custom-call(s32[4]{0:T(128)S(1)} %pad_add_fusion.place, s32[24]{0:T(128)S(1)} %copy-done.2, bf16[4,48,896]{2,1,0:T(8,128)(2,1)S(1)} %copy.37.q_ref, bf16[3,8,256,256]{3,2,1,0:T(8,128)(2,1)} %bitcast.42, bf16[3,8,256,256]{3,2,1,0:T(8,128)(2,1)} %bitcast.44), custom_call_target="tpu_custom_call" | custom-call | flops 150994944 | bytes 3932160 | tf_op jit(solution)/shard_map/pallas_call | solution.py:279
  88.6 1.6 shard_map.116
  90.1 0.7 collective-permute-start.19
  90.8 1.9 %collective-permute-start.20 = (bf16[48,3456]{1,0:T(8,128)(2,1)S(1)}, bf16[48,3456]{1,0:T(8,128)(2,1)S(1)}, u32[]{:S(2)}, u32[]{:S(2)}) collective-permute-start(bf16[48,3456]{1,0:T(8,128)(2,1)S(1)} %get-tuple-element.54), channel_id=1, source_target_pairs={{0,4},{1,5},{2,6},{3,7},{4,0},{5,1},{6,2},{7,3},{8,12},{9,13},{10,... | collective-permute-start | bytes 995336 | tf_op jit(solution)/shard_map/ppermute | solution.py:43
  92.7 1.5 collective-permute-start.21
  94.1 14.2 %collective-permute-done.19.refs_0_ = bf16[48,3456]{1,0:T(8,128)(2,1)S(1)} collective-permute-done((bf16[48,3456]{1,0:T(8,128)(2,1)S(1)}, bf16[48,3456]{1,0:T(8,128)(2,1)S(1)}, u32[]{:S(2)}, u32[]{:S(2)}) %collective-permute-start.19) | collective-permute-done | bytes 331808 | tf_op jit(solution)/shard_map/ppermute | solution.py:43
  108.3 0.6 collective-permute-done.21.refs_2_
  109.0 1.5 shard_map.117
  110.6 18.0 %all_to_all.17 = bf16[64,4,768]{2,1,0:T(4,128)(2,1)S(1)} all-to-all(bf16[64,4,768]{2,1,0:T(4,128)(2,1)S(1)} %bitcast.47), channel_id=1, replica_groups={{0,2,4,6,8,10,12,14,16,18,20,22,24,26,28,30,32,34,36,38,40,42,44,46,48,..., dimensions={0} | all-to-all | bytes 786432 | tf_op jit(solution)/shard_map/all_to_all | solution.py:66
  128.8 1.7 %collective-permute-done.22.other_ref = bf16[256,768]{1,0:T(8,128)(2,1)S(1)} collective-permute-done((bf16[256,768]{1,0:T(8,128)(2,1)S(1)}, bf16[256,768]{1,0:T(8,128)(2,1)S(1)}, u32[]{:S(2)}, u32[]{:S(2)}) %collective-permute-start.22) | collective-permute-done | bytes 393248 | tf_op jit(solution)/shard_map/ppermute | solution.py:39
  130.5 2.0 %copy-done.3 = bf16[768,2304]{1,0:T(8,128)(2,1)S(1)} copy-done((bf16[768,2304]{1,0:T(8,128)(2,1)S(1)}, bf16[768,2304]{1,0:T(8,128)(2,1)}, u32[]{:S(2)}) %copy-start.3) | copy-done | bytes 3538968
  132.5 3.8 %shard_map.118 = (f32[1,128]{1,0:T(1,128)S(1)}, bf16[96,1152]{1,0:T(8,128)(2,1)S(1)}, bf16[96,1152]{1,0:T(8,128)(2,1)S(1)}, bf16[96,1152]{1,0:T(8,128)(2,1)S(1)}...) custom-call(s32[4]{0:T(128)S(1)} %pad_add_fusion.place, ...), custom_call_target="tpu_custom_call" | custom-call | flops 1358954496 | bytes 5308416 | tf_op jit(solution)/shard_map/pallas_call | solution.py:422
  136.3 0.7 collective-permute-start.23
  137.0 1.8 %collective-permute-start.24 = (bf16[96,1152]{1,0:T(8,128)(2,1)S(1)}, bf16[96,1152]{1,0:T(8,128)(2,1)S(1)}, u32[]{:S(2)}, u32[]{:S(2)}) collective-permute-start(bf16[96,1152]{1,0:T(8,128)(2,1)S(1)} %get-tuple-element.59), channel_id=1, source_target_pairs={{0,64},{8,72},{16,80},{24,88},{32,96},{40,104},{48,112},{56,120},{... | collective-permute-start | bytes 663560 | tf_op jit(solution)/shard_map/ppermute | solution.py:47
  138.8 1.0 collective-permute-start.25
  139.9 0.7 collective-permute-start.29
  140.6 2.1 %collective-permute-start.30 = (bf16[96,1152]{1,0:T(8,128)(2,1)S(1)}, bf16[96,1152]{1,0:T(8,128)(2,1)S(1)}, u32[]{:S(2)}, u32[]{:S(2)}) collective-permute-start(bf16[96,1152]{1,0:T(8,128)(2,1)S(1)} %get-tuple-element.67), channel_id=1, source_target_pairs={{0,16},{8,24},{16,0},{24,8},{32,48},{40,56},{48,32},{56,40},{64,80... | collective-permute-start | bytes 663560 | tf_op jit(solution)/shard_map/ppermute | solution.py:51
  142.7 7.1 %collective-permute-done.23.refs_1_ = bf16[96,1152]{1,0:T(8,128)(2,1)S(1)} collective-permute-done((bf16[96,1152]{1,0:T(8,128)(2,1)S(1)}, bf16[96,1152]{1,0:T(8,128)(2,1)S(1)}, u32[]{:S(2)}, u32[]{:S(2)}) %collective-permute-start.23) | collective-permute-done | bytes 221216 | tf_op jit(solution)/shard_map/ppermute | solution.py:47
  149.8 0.5 collective-permute-start.31
  150.3 0.1 collective-permute-done.25.refs_3_
  150.6 1.5 collective-permute-start.26
  152.0 0.7 collective-permute-start.27
  152.7 2.5 %collective-permute-start.28 = (bf16[24,1152]{1,0:T(8,128)(2,1)S(1)}, bf16[24,1152]{1,0:T(8,128)(2,1)S(1)}, u32[]{:S(2)}, u32[]{:S(2)}) collective-permute-start(bf16[24,1152]{1,0:T(8,128)(2,1)S(1)} %get-tuple-element.64), channel_id=1, source_target_pairs={{0,24},{8,0},{16,8},{24,16},{32,56},{40,32},{48,40},{56,48},{64,88... | collective-permute-start | bytes 165896 | tf_op jit(solution)/shard_map/ppermute | solution.py:51
  155.2 1.7 %collective-permute-done.31.refs_3_ = bf16[96,1152]{1,0:T(8,128)(2,1)S(1)} collective-permute-done((bf16[96,1152]{1,0:T(8,128)(2,1)S(1)}, bf16[96,1152]{1,0:T(8,128)(2,1)S(1)}, u32[]{:S(2)}, u32[]{:S(2)}) %collective-permute-start.31) | collective-permute-done | bytes 221216 | tf_op jit(solution)/shard_map/ppermute | solution.py:51
  157.1 1.1 collective-permute-start.33
  158.2 2.1 %collective-permute-start.34 = (bf16[24,1152]{1,0:T(8,128)(2,1)S(1)}, bf16[24,1152]{1,0:T(8,128)(2,1)S(1)}, u32[]{:S(2)}, u32[]{:S(2)}) collective-permute-start(bf16[24,1152]{1,0:T(8,128)(2,1)S(1)} %get-tuple-element.72), channel_id=1, source_target_pairs={{0,96},{8,104},{16,112},{24,120},{32,0},{40,8},{48,16},{56,24},{64... | collective-permute-start | bytes 165896 | tf_op jit(solution)/shard_map/ppermute | solution.py:47
  160.4 0.5 slice_bitcast_fusion.3
  160.9 0.8 shard_map.122
  161.7 1.4 collective-permute-done.32.refs_5_
  163.1 0.9 collective-permute-done.34.refs_7_
  163.9 0.7 shard_map.121
  (51 shorter events, 1.4 us)
Async XLA Ops:
  13.3 8.2 %collective-permute-start.2 = (bf16[24,1152]{1,0:T(8,128)(2,1)S(1)}, bf16[24,1152]{1,0:T(8,128)(2,1)S(1)}, u32[]{:S(2)}, u32[]{:S(2)}) collective-permute-start(bf16[24,1152]{1,0:T(8,128)(2,1)S(1)} %get-tuple-element.81), channel_id=1, source_target_pairs={{0,96},{8,104},{16,112},{24,120},{32,0},{40,8},{48,16},{56,24},{64... | collective-permute-start | bytes 165896 | tf_op jit(solution)/shard_map/ppermute | solution.py:47
  16.1 6.3 %collective-permute-start.1 = (bf16[24,1152]{1,0:T(8,128)(2,1)S(1)}, bf16[24,1152]{1,0:T(8,128)(2,1)S(1)}, u32[]{:S(2)}, u32[]{:S(2)}) collective-permute-start(bf16[24,1152]{1,0:T(8,128)(2,1)S(1)} %get-tuple-element.81), channel_id=1, source_target_pairs={{0,64},{8,72},{16,80},{24,88},{32,96},{40,104},{48,112},{56,120},{... | collective-permute-start | bytes 165896 | tf_op jit(solution)/shard_map/ppermute | solution.py:47
  16.9 5.5 %collective-permute-start = (bf16[24,1152]{1,0:T(8,128)(2,1)S(1)}, bf16[24,1152]{1,0:T(8,128)(2,1)S(1)}, u32[]{:S(2)}, u32[]{:S(2)}) collective-permute-start(bf16[24,1152]{1,0:T(8,128)(2,1)S(1)} %get-tuple-element.81), channel_id=1, source_target_pairs={{0,32},{8,40},{16,48},{24,56},{32,64},{40,72},{48,80},{56,88},{64,... | collective-permute-start | bytes 165896 | tf_op jit(solution)/shard_map/ppermute | solution.py:47
  17.8 8.7 %collective-permute-start.8 = (bf16[24,1152]{1,0:T(8,128)(2,1)S(1)}, bf16[24,1152]{1,0:T(8,128)(2,1)S(1)}, u32[]{:S(2)}, u32[]{:S(2)}) collective-permute-start(bf16[24,1152]{1,0:T(8,128)(2,1)S(1)} %get-tuple-element.80), channel_id=1, source_target_pairs={{0,24},{8,0},{16,8},{24,16},{32,56},{40,32},{48,40},{56,48},{64,88... | collective-permute-start | bytes 165896 | tf_op jit(solution)/shard_map/ppermute | solution.py:51
  20.8 6.3 %collective-permute-start.7 = (bf16[24,1152]{1,0:T(8,128)(2,1)S(1)}, bf16[24,1152]{1,0:T(8,128)(2,1)S(1)}, u32[]{:S(2)}, u32[]{:S(2)}) collective-permute-start(bf16[24,1152]{1,0:T(8,128)(2,1)S(1)} %get-tuple-element.80), channel_id=1, source_target_pairs={{0,16},{8,24},{16,0},{24,8},{32,48},{40,56},{48,32},{56,40},{64,80... | collective-permute-start | bytes 165896 | tf_op jit(solution)/shard_map/ppermute | solution.py:51
  21.4 5.6 %collective-permute-start.6 = (bf16[24,1152]{1,0:T(8,128)(2,1)S(1)}, bf16[24,1152]{1,0:T(8,128)(2,1)S(1)}, u32[]{:S(2)}, u32[]{:S(2)}) collective-permute-start(bf16[24,1152]{1,0:T(8,128)(2,1)S(1)} %get-tuple-element.80), channel_id=1, source_target_pairs={{0,8},{8,16},{16,24},{24,0},{32,40},{40,48},{48,56},{56,32},{64,72... | collective-permute-start | bytes 165896 | tf_op jit(solution)/shard_map/ppermute | solution.py:51
  22.4 11.1 %collective-permute-start.5 = (bf16[96,1152]{1,0:T(8,128)(2,1)S(1)}, bf16[96,1152]{1,0:T(8,128)(2,1)S(1)}, u32[]{:S(2)}, u32[]{:S(2)}) collective-permute-start(bf16[96,1152]{1,0:T(8,128)(2,1)S(1)} %pad_maximum_fusion.refs_0_), channel_id=1, source_target_pairs={{0,24},{8,0},{16,8},{24,16},{32,56},{40,32},{48,40},{56,48},{64,88... | collective-permute-start | bytes 663560 | tf_op jit(solution)/shard_map/ppermute | solution.py:51
  25.4 10.7 %collective-permute-start.4 = (bf16[96,1152]{1,0:T(8,128)(2,1)S(1)}, bf16[96,1152]{1,0:T(8,128)(2,1)S(1)}, u32[]{:S(2)}, u32[]{:S(2)}) collective-permute-start(bf16[96,1152]{1,0:T(8,128)(2,1)S(1)} %pad_maximum_fusion.refs_0_), channel_id=1, source_target_pairs={{0,16},{8,24},{16,0},{24,8},{32,48},{40,56},{48,32},{56,40},{64,80... | collective-permute-start | bytes 663560 | tf_op jit(solution)/shard_map/ppermute | solution.py:51
  26.4 10.7 %collective-permute-start.3 = (bf16[96,1152]{1,0:T(8,128)(2,1)S(1)}, bf16[96,1152]{1,0:T(8,128)(2,1)S(1)}, u32[]{:S(2)}, u32[]{:S(2)}) collective-permute-start(bf16[96,1152]{1,0:T(8,128)(2,1)S(1)} %pad_maximum_fusion.refs_0_), channel_id=1, source_target_pairs={{0,8},{8,16},{16,24},{24,0},{32,40},{40,48},{48,56},{56,32},{64,72... | collective-permute-start | bytes 663560 | tf_op jit(solution)/shard_map/ppermute | solution.py:51
  27.1 10.0 %collective-permute-start.11 = (bf16[96,1152]{1,0:T(8,128)(2,1)S(1)}, bf16[96,1152]{1,0:T(8,128)(2,1)S(1)}, u32[]{:S(2)}, u32[]{:S(2)}) collective-permute-start(bf16[96,1152]{1,0:T(8,128)(2,1)S(1)} %pad_maximum_fusion.1.refs_4_), channel_id=1, source_target_pairs={{0,96},{8,104},{16,112},{24,120},{32,0},{40,8},{48,16},{56,24},{64... | collective-permute-start | bytes 663560 | tf_op jit(solution)/shard_map/ppermute | solution.py:47
  29.8 8.1 %collective-permute-start.10 = (bf16[96,1152]{1,0:T(8,128)(2,1)S(1)}, bf16[96,1152]{1,0:T(8,128)(2,1)S(1)}, u32[]{:S(2)}, u32[]{:S(2)}) collective-permute-start(bf16[96,1152]{1,0:T(8,128)(2,1)S(1)} %pad_maximum_fusion.1.refs_4_), channel_id=1, source_target_pairs={{0,64},{8,72},{16,80},{24,88},{32,96},{40,104},{48,112},{56,120},{... | collective-permute-start | bytes 663560 | tf_op jit(solution)/shard_map/ppermute | solution.py:47
  33.5 7.1 %collective-permute-start.9 = (bf16[96,1152]{1,0:T(8,128)(2,1)S(1)}, bf16[96,1152]{1,0:T(8,128)(2,1)S(1)}, u32[]{:S(2)}, u32[]{:S(2)}) collective-permute-start(bf16[96,1152]{1,0:T(8,128)(2,1)S(1)} %pad_maximum_fusion.1.refs_4_), channel_id=1, source_target_pairs={{0,32},{8,40},{16,48},{24,56},{32,64},{40,72},{48,80},{56,88},{64,... | collective-permute-start | bytes 663560 | tf_op jit(solution)/shard_map/ppermute | solution.py:47
  40.6 2.0 %copy-start = (bf16[2304,768]{1,0:T(8,128)(2,1)S(1)}, bf16[2304,768]{1,0:T(8,128)(2,1)}, u32[]{:S(2)}) copy-start(bf16[2304,768]{1,0:T(8,128)(2,1)} %refs_8_.1) | copy-start | bytes 10616836
  45.9 2.2 %collective-permute-start.12 = (f32[4,48,896]{2,1,0:T(8,128)S(1)}, f32[4,48,896]{2,1,0:T(8,128)S(1)}, u32[]{:S(2)}, u32[]{:S(2)}) collective-permute-start(f32[4,48,896]{2,1,0:T(8,128)S(1)} %get-tuple-element.41), channel_id=1, source_target_pairs={{0,1},{1,0},{2,3},{3,2},{4,5},{5,4},{6,7},{7,6},{8,9},{9,8},{10,11... | collective-permute-start | bytes 2064392 | tf_op jit(solution)/shard_map/ppermute | solution.py:39
  48.2 11.4 %collective-permute-start.13 = (f32[48,896]{1,0:T(8,128)S(1)}, f32[48,896]{1,0:T(8,128)S(1)}, u32[]{:S(2)}, u32[]{:S(2)}) collective-permute-start(f32[48,896]{1,0:T(8,128)S(1)} %get-tuple-element.77), channel_id=1, source_target_pairs={{0,2},{1,3},{2,4},{3,5},{4,6},{5,7},{6,0},{7,1},{8,10},{9,11},{10,... | collective-permute-start | bytes 516104 | tf_op jit(solution)/shard_map/ppermute | solution.py:43
  48.9 10.7 %collective-permute-start.15 = (f32[48,896]{1,0:T(8,128)S(1)}, f32[48,896]{1,0:T(8,128)S(1)}, u32[]{:S(2)}, u32[]{:S(2)}) collective-permute-start(f32[48,896]{1,0:T(8,128)S(1)} %get-tuple-element.78), channel_id=1, source_target_pairs={{0,6},{1,7},{2,0},{3,1},{4,2},{5,3},{6,4},{7,5},{8,14},{9,15},{10,... | collective-permute-start | bytes 516104 | tf_op jit(solution)/shard_map/ppermute | solution.py:43
  51.5 8.1 %collective-permute-start.14 = (f32[48,896]{1,0:T(8,128)S(1)}, f32[48,896]{1,0:T(8,128)S(1)}, u32[]{:S(2)}, u32[]{:S(2)}) collective-permute-start(f32[48,896]{1,0:T(8,128)S(1)} %get-tuple-element.79), channel_id=1, source_target_pairs={{0,4},{1,5},{2,6},{3,7},{4,0},{5,1},{6,2},{7,3},{8,12},{9,13},{10,... | collective-permute-start | bytes 516104 | tf_op jit(solution)/shard_map/ppermute | solution.py:43
  58.7 22.9 %copy-start.2 = (s32[24]{0:T(128)S(1)}, s32[24]{0:T(128)}, u32[]{:S(2)}) copy-start(s32[24]{0:T(128)} %lengths.3) | copy-start | bytes 292
  79.8 1.7 %collective-permute-start.16 = (bf16[4,48,896]{2,1,0:T(8,128)(2,1)S(1)}, bf16[4,48,896]{2,1,0:T(8,128)(2,1)S(1)}, u32[]{:S(2)}, u32[]{:S(2)}) collective-permute-start(bf16[4,48,896]{2,1,0:T(8,128)(2,1)S(1)} %copy.37.q_ref), channel_id=1, source_target_pairs={{0,1},{1,0},{2,3},{3,2},{4,5},{5,4},{6,7},{7,6},{8,9},{9,8},{10,11... | collective-permute-start | bytes 1032200 | tf_op jit(solution)/shard_map/ppermute | solution.py:39
  84.8 3.8 %collective-permute-start.18 = (bf16[4,48,2304]{2,1,0:T(8,128)(2,1)S(1)}, bf16[4,48,2304]{2,1,0:T(8,128)(2,1)S(1)}, u32[]{:S(2)}, u32[]{:S(2)}) collective-permute-start(bf16[4,48,2304]{2,1,0:T(8,128)(2,1)S(1)} %get-tuple-element.50), channel_id=1, source_target_pairs={{0,1},{1,0},{2,3},{3,2},{4,5},{5,4},{6,7},{7,6},{8,9},{9,8},{10,11... | collective-permute-start | bytes 2654216 | tf_op jit(solution)/shard_map/ppermute | solution.py:39
  85.0 3.6 %collective-permute-start.17 = (bf16[4,144,384]{2,1,0:T(8,128)(2,1)S(1)}, bf16[4,144,384]{2,1,0:T(8,128)(2,1)S(1)}, u32[]{:S(2)}, u32[]{:S(2)}) collective-permute-start(bf16[4,144,384]{2,1,0:T(8,128)(2,1)S(1)} %shard_map.115), channel_id=1, source_target_pairs={{0,1},{1,0},{2,3},{3,2},{4,5},{5,4},{6,7},{7,6},{8,9},{9,8},{10,11... | collective-permute-start | bytes 1327112 | tf_op jit(solution)/shard_map/ppermute | solution.py:39
  90.1 18.2 %collective-permute-start.19 = (bf16[48,3456]{1,0:T(8,128)(2,1)S(1)}, bf16[48,3456]{1,0:T(8,128)(2,1)S(1)}, u32[]{:S(2)}, u32[]{:S(2)}) collective-permute-start(bf16[48,3456]{1,0:T(8,128)(2,1)S(1)} %get-tuple-element.53), channel_id=1, source_target_pairs={{0,2},{1,3},{2,4},{3,5},{4,6},{5,7},{6,0},{7,1},{8,10},{9,11},{10,... | collective-permute-start | bytes 995336 | tf_op jit(solution)/shard_map/ppermute | solution.py:43
  90.8 17.5 %collective-permute-start.20 = (bf16[48,3456]{1,0:T(8,128)(2,1)S(1)}, bf16[48,3456]{1,0:T(8,128)(2,1)S(1)}, u32[]{:S(2)}, u32[]{:S(2)}) collective-permute-start(bf16[48,3456]{1,0:T(8,128)(2,1)S(1)} %get-tuple-element.54), channel_id=1, source_target_pairs={{0,4},{1,5},{2,6},{3,7},{4,0},{5,1},{6,2},{7,3},{8,12},{9,13},{10,... | collective-permute-start | bytes 995336 | tf_op jit(solution)/shard_map/ppermute | solution.py:43
  92.7 16.3 %collective-permute-start.21 = (bf16[48,3456]{1,0:T(8,128)(2,1)S(1)}, bf16[48,3456]{1,0:T(8,128)(2,1)S(1)}, u32[]{:S(2)}, u32[]{:S(2)}) collective-permute-start(bf16[48,3456]{1,0:T(8,128)(2,1)S(1)} %get-tuple-element.55), channel_id=1, source_target_pairs={{0,6},{1,7},{2,0},{3,1},{4,2},{5,3},{6,4},{7,5},{8,14},{9,15},{10,... | collective-permute-start | bytes 995336 | tf_op jit(solution)/shard_map/ppermute | solution.py:43
  128.7 35.2 %copy-start.1 = (bf16[24,2304]{1,0:T(8,128)(2,1)S(1)}, bf16[24,2304]{1,0:T(8,128)(2,1)}, u32[]{:S(2)}) copy-start(bf16[24,2304]{1,0:T(8,128)(2,1)} %residual_ref.1) | copy-start | bytes 331780
  128.7 1.8 %collective-permute-start.22 = (bf16[256,768]{1,0:T(8,128)(2,1)S(1)}, bf16[256,768]{1,0:T(8,128)(2,1)S(1)}, u32[]{:S(2)}, u32[]{:S(2)}) collective-permute-start(bf16[256,768]{1,0:T(8,128)(2,1)S(1)} %reshape.60.own_ref), channel_id=1, source_target_pairs={{0,1},{1,0},{2,3},{3,2},{4,5},{5,4},{6,7},{7,6},{8,9},{9,8},{10,11... | collective-permute-start | bytes 1179656 | tf_op jit(solution)/shard_map/ppermute | solution.py:39
  130.5 2.0 %copy-start.3 = (bf16[768,2304]{1,0:T(8,128)(2,1)S(1)}, bf16[768,2304]{1,0:T(8,128)(2,1)}, u32[]{:S(2)}) copy-start(bf16[768,2304]{1,0:T(8,128)(2,1)} %w_ref.1) | copy-start | bytes 10616836
  136.3 13.5 %collective-permute-start.23 = (bf16[96,1152]{1,0:T(8,128)(2,1)S(1)}, bf16[96,1152]{1,0:T(8,128)(2,1)S(1)}, u32[]{:S(2)}, u32[]{:S(2)}) collective-permute-start(bf16[96,1152]{1,0:T(8,128)(2,1)S(1)} %get-tuple-element.58), channel_id=1, source_target_pairs={{0,32},{8,40},{16,48},{24,56},{32,64},{40,72},{48,80},{56,88},{64,... | collective-permute-start | bytes 663560 | tf_op jit(solution)/shard_map/ppermute | solution.py:47
  137.0 13.3 %collective-permute-start.24 = (bf16[96,1152]{1,0:T(8,128)(2,1)S(1)}, bf16[96,1152]{1,0:T(8,128)(2,1)S(1)}, u32[]{:S(2)}, u32[]{:S(2)}) collective-permute-start(bf16[96,1152]{1,0:T(8,128)(2,1)S(1)} %get-tuple-element.59), channel_id=1, source_target_pairs={{0,64},{8,72},{16,80},{24,88},{32,96},{40,104},{48,112},{56,120},{... | collective-permute-start | bytes 663560 | tf_op jit(solution)/shard_map/ppermute | solution.py:47
  138.8 11.6 %collective-permute-start.25 = (bf16[96,1152]{1,0:T(8,128)(2,1)S(1)}, bf16[96,1152]{1,0:T(8,128)(2,1)S(1)}, u32[]{:S(2)}, u32[]{:S(2)}) collective-permute-start(bf16[96,1152]{1,0:T(8,128)(2,1)S(1)} %get-tuple-element.60), channel_id=1, source_target_pairs={{0,96},{8,104},{16,112},{24,120},{32,0},{40,8},{48,16},{56,24},{64... | collective-permute-start | bytes 663560 | tf_op jit(solution)/shard_map/ppermute | solution.py:47
  139.9 12.8 %collective-permute-start.29 = (bf16[96,1152]{1,0:T(8,128)(2,1)S(1)}, bf16[96,1152]{1,0:T(8,128)(2,1)S(1)}, u32[]{:S(2)}, u32[]{:S(2)}) collective-permute-start(bf16[96,1152]{1,0:T(8,128)(2,1)S(1)} %get-tuple-element.66), channel_id=1, source_target_pairs={{0,8},{8,16},{16,24},{24,0},{32,40},{40,48},{48,56},{56,32},{64,72... | collective-permute-start | bytes 663560 | tf_op jit(solution)/shard_map/ppermute | solution.py:51
  140.6 14.6 %collective-permute-start.30 = (bf16[96,1152]{1,0:T(8,128)(2,1)S(1)}, bf16[96,1152]{1,0:T(8,128)(2,1)S(1)}, u32[]{:S(2)}, u32[]{:S(2)}) collective-permute-start(bf16[96,1152]{1,0:T(8,128)(2,1)S(1)} %get-tuple-element.67), channel_id=1, source_target_pairs={{0,16},{8,24},{16,0},{24,8},{32,48},{40,56},{48,32},{56,40},{64,80... | collective-permute-start | bytes 663560 | tf_op jit(solution)/shard_map/ppermute | solution.py:51
  149.8 7.1 %collective-permute-start.31 = (bf16[96,1152]{1,0:T(8,128)(2,1)S(1)}, bf16[96,1152]{1,0:T(8,128)(2,1)S(1)}, u32[]{:S(2)}, u32[]{:S(2)}) collective-permute-start(bf16[96,1152]{1,0:T(8,128)(2,1)S(1)} %get-tuple-element.68), channel_id=1, source_target_pairs={{0,24},{8,0},{16,8},{24,16},{32,56},{40,32},{48,40},{56,48},{64,88... | collective-permute-start | bytes 663560 | tf_op jit(solution)/shard_map/ppermute | solution.py:51
  150.6 7.7 %collective-permute-start.26 = (bf16[24,1152]{1,0:T(8,128)(2,1)S(1)}, bf16[24,1152]{1,0:T(8,128)(2,1)S(1)}, u32[]{:S(2)}, u32[]{:S(2)}) collective-permute-start(bf16[24,1152]{1,0:T(8,128)(2,1)S(1)} %get-tuple-element.62), channel_id=1, source_target_pairs={{0,8},{8,16},{16,24},{24,0},{32,40},{40,48},{48,56},{56,32},{64,72... | collective-permute-start | bytes 165896 | tf_op jit(solution)/shard_map/ppermute | solution.py:51
  152.0 9.6 %collective-permute-start.27 = (bf16[24,1152]{1,0:T(8,128)(2,1)S(1)}, bf16[24,1152]{1,0:T(8,128)(2,1)S(1)}, u32[]{:S(2)}, u32[]{:S(2)}) collective-permute-start(bf16[24,1152]{1,0:T(8,128)(2,1)S(1)} %get-tuple-element.63), channel_id=1, source_target_pairs={{0,16},{8,24},{16,0},{24,8},{32,48},{40,56},{48,32},{56,40},{64,80... | collective-permute-start | bytes 165896 | tf_op jit(solution)/shard_map/ppermute | solution.py:51
  152.7 9.0 %collective-permute-start.28 = (bf16[24,1152]{1,0:T(8,128)(2,1)S(1)}, bf16[24,1152]{1,0:T(8,128)(2,1)S(1)}, u32[]{:S(2)}, u32[]{:S(2)}) collective-permute-start(bf16[24,1152]{1,0:T(8,128)(2,1)S(1)} %get-tuple-element.64), channel_id=1, source_target_pairs={{0,24},{8,0},{16,8},{24,16},{32,56},{40,32},{48,40},{56,48},{64,88... | collective-permute-start | bytes 165896 | tf_op jit(solution)/shard_map/ppermute | solution.py:51
  157.0 6.0 %collective-permute-start.32 = (bf16[24,1152]{1,0:T(8,128)(2,1)S(1)}, bf16[24,1152]{1,0:T(8,128)(2,1)S(1)}, u32[]{:S(2)}, u32[]{:S(2)}) collective-permute-start(bf16[24,1152]{1,0:T(8,128)(2,1)S(1)} %get-tuple-element.70), channel_id=1, source_target_pairs={{0,32},{8,40},{16,48},{24,56},{32,64},{40,72},{48,80},{56,88},{64,... | collective-permute-start | bytes 165896 | tf_op jit(solution)/shard_map/ppermute | solution.py:47
  157.1 5.9 %collective-permute-start.33 = (bf16[24,1152]{1,0:T(8,128)(2,1)S(1)}, bf16[24,1152]{1,0:T(8,128)(2,1)S(1)}, u32[]{:S(2)}, u32[]{:S(2)}) collective-permute-start(bf16[24,1152]{1,0:T(8,128)(2,1)S(1)} %get-tuple-element.71), channel_id=1, source_target_pairs={{0,64},{8,72},{16,80},{24,88},{32,96},{40,104},{48,112},{56,120},{... | collective-permute-start | bytes 165896 | tf_op jit(solution)/shard_map/ppermute | solution.py:47
  158.2 5.7 %collective-permute-start.34 = (bf16[24,1152]{1,0:T(8,128)(2,1)S(1)}, bf16[24,1152]{1,0:T(8,128)(2,1)S(1)}, u32[]{:S(2)}, u32[]{:S(2)}) collective-permute-start(bf16[24,1152]{1,0:T(8,128)(2,1)S(1)} %get-tuple-element.72), channel_id=1, source_target_pairs={{0,96},{8,104},{16,112},{24,120},{32,0},{40,8},{48,16},{56,24},{64... | collective-permute-start | bytes 165896 | tf_op jit(solution)/shard_map/ppermute | solution.py:47

commit v5 on v4

--- a/solution.py
+++ b/solution.py
@@ -20,11 +20,12 @@
 HELD = QCOLS // HEAD
 KVCOLS = 2 * HEAD // WIDE
 HCOLS = QCOLS + 128
-PACK = HEAD + 128
+PACK = EACH * HEAD + 128
 FEATS = D // NARROW
 SHARE = ROWS // NARROW
 UPCOLS = 36864 // WIDE
-HALF = FEATS // 2
+GATHERED = 1280
+SUMMED = 1152
 SPAN = RING * LOCAL
 UP_PIECES = (256, 1024, 1024)
 
@@ -52,7 +53,7 @@
 
 
 def gathered(normed):
-    left, right = normed[:, :HALF], normed[:, HALF:]
+    left, right = normed[:, :GATHERED], normed[:, GATHERED:]
     left = jnp.concatenate([left] + [shift_x(left, by) for by in range(1, RING)])
     right = jnp.concatenate([right] + [shift_y(right, by) for by in range(1, RING)])
     return (
@@ -101,13 +102,13 @@
     wq_ref, wkv_ref, keep_ref, send_ref, x_ref, acc_ref, rows_ref = refs[2 * RING :]
     z, c, x, y = place[0], place[1], place[2], place[3]
     for outer in range(RING):
-        for first, ref in ((0, left[outer]), (HALF, right[outer])):
+        for first, ref in ((0, left[outer]), (GATHERED, right[outer])):
             held = ref[...].astype(f32)
             for inner in range(RING):
                 by_x, by_y = (inner, outer) if first == 0 else (outer, inner)
                 source = lax.rem(x - by_x + RING, RING) * RING + lax.rem(y - by_y + RING, RING)
                 at = pl.ds(pl.multiple_of(slot_of(source, z, c) * LOCAL, 8), LOCAL)
-                rows_ref[at, first : first + HALF] = held[inner * LOCAL : (inner + 1) * LOCAL]
+                rows_ref[at, first : first + held.shape[1]] = held[inner * LOCAL : (inner + 1) * LOCAL]
     x_ref[...] = rows_ref[...].astype(bf16)
 
     def deal(terms, first):
@@ -195,19 +196,19 @@
     return high, middle, (rest - middle).astype(bf16).astype(f32)
 
 
-def packed(top, total):
-    lane = lax.broadcasted_iota(jnp.int32, (top.shape[0], 128), 1)
+def packed(tops, totals):
+    lane = lax.broadcasted_iota(jnp.int32, (tops[0].shape[0], 128), 1)
     out = jnp.zeros(lane.shape, f32)
-    for at, part in enumerate(parts(top) + parts(total)):
-        out = jnp.where(lane == at, part, out)
+    for j, (top, total) in enumerate(zip(tops, totals)):
+        for at, part in enumerate(parts(top) + parts(total)):
+            out = jnp.where(lane == 6 * j + at, part, out)
     return out.astype(bf16)
 
 
-def unpacked(block):
-    held = block[:, HEAD:PACK].astype(f32)
-    top = held[:, 0:1] + held[:, 1:2] + held[:, 2:3]
-    total = held[:, 3:4] + held[:, 4:5] + held[:, 5:6]
-    return block[:, :HEAD].astype(f32), top, total
+def unpacked(block, j):
+    held = block[:, EACH * HEAD : PACK].astype(f32)
+    lanes = [held[:, 6 * j + at : 6 * j + at + 1] for at in range(6)]
+    return block[:, j * HEAD : (j + 1) * HEAD].astype(f32), lanes[0] + lanes[1] + lanes[2], lanes[3] + lanes[4] + lanes[5]
 
 
 def chosen(rows, columns, source):
@@ -256,14 +257,16 @@
         masked = jnp.where(valid, scores * (1.0 / HEAD**0.5), f32(-1e30))
         top = jnp.max(masked, axis=1, keepdims=True)
         probs = jnp.where(valid, jnp.exp(masked - top), f32(0.0))
-        out_ref[step, :, HEAD:] = packed(top, jnp.sum(probs, axis=1, keepdims=True))
+        total = jnp.sum(probs, axis=1, keepdims=True)
+        spans = [slice(j * HEADS, (j + 1) * HEADS) for j in range(EACH)]
+        out_ref[step, :, EACH * HEAD :] = packed([top[span] for span in spans], [total[span] for span in spans])
         weights.append(probs.astype(bf16))
     for copy in copies[1]:
         copy.wait()
     for step in range(RING):
         for j in range(EACH):
             span = slice(j * HEADS, (j + 1) * HEADS)
-            out_ref[step, span, :HEAD] = dot(weights[step][span], v_ref[step, j]).astype(bf16)
+            out_ref[step, :, j * HEAD : (j + 1) * HEAD] = dot(weights[step][span], v_ref[step, j]).astype(bf16)
 
 
 def group_of(away, step, place):
@@ -275,7 +278,7 @@
     positions = k_cache.shape[1]
     k_cache = k_cache.reshape(EACH, NARROW, positions, HEAD)
     v_cache = v_cache.reshape(EACH, NARROW, positions, HEAD)
-    out = jax.ShapeDtypeStruct((RING, EACH * HEADS, PACK), bf16)
+    out = jax.ShapeDtypeStruct((RING, HEADS, PACK), bf16)
     return pl.pallas_call(
         functools.partial(attend_kernel, away),
         grid_spec=pltpu.PrefetchScalarGridSpec(
@@ -302,22 +305,24 @@
 
 def pair_kernel(a_ref, b_ref, up_a_ref, up_b_ref, own_ref, up_ref, *send_refs):
     for at in range(RING):
-        value, top, total = joined(unpacked(a_ref[at]), unpacked(b_ref[at]))
-        block = jnp.concatenate([value.astype(bf16), packed(top, total)], axis=1)
+        made = [joined(unpacked(a_ref[at], j), unpacked(b_ref[at], j)) for j in range(EACH)]
+        block = jnp.concatenate(
+            [value.astype(bf16) for value, _, _ in made] + [packed([top for _, top, _ in made], [total for _, _, total in made])],
+            axis=1,
+        )
         up = up_a_ref[at].astype(f32) + up_b_ref[at].astype(f32)
         if at == 0:
             own_ref[...] = block
             up_ref[...] = up
         else:
             ref = send_refs[at - 1]
-            for j in range(EACH):
-                ref[:, j * PACK : (j + 1) * PACK] = block[j * HEADS : (j + 1) * HEADS]
-            ref[:, EACH * PACK :] = up.astype(bf16)
+            ref[:, :PACK] = block
+            ref[:, PACK:] = up.astype(bf16)
 
 
 def pair(a, b, up_a, up_b):
     out = [jax.ShapeDtypeStruct(a.shape[1:], bf16), jax.ShapeDtypeStruct(up_a.shape[1:], f32)]
-    out += [jax.ShapeDtypeStruct((SHARE, EACH * PACK + UPCOLS), bf16)] * (RING - 1)
+    out += [jax.ShapeDtypeStruct((SHARE, PACK + UPCOLS), bf16)] * (RING - 1)
     return pl.pallas_call(
         pair_kernel,
         out_shape=out,
@@ -337,7 +342,7 @@
 
 def finish_kernel(place, q_ref, own_ref, up_own_ref, *refs):
     blocks, (out_ref, up_ref) = refs[: RING - 1], refs[RING - 1 :]
-    up = sum((ref[:, EACH * PACK :].astype(f32) for ref in blocks), up_own_ref[...])
+    up = sum((ref[:, PACK:].astype(f32) for ref in blocks), up_own_ref[...])
     up_ref[...] = up
     rows = by_row(q_ref[place[0]])
     made = []
@@ -348,9 +353,7 @@
         new_key = row_of(keyval[: WIDE // 2])
         new_value = row_of(keyval[WIDE // 2 :])
         own = jnp.sum(query * new_key, axis=1, keepdims=True) * (1.0 / HEAD**0.5)
-        span = slice(j * HEADS, (j + 1) * HEADS)
-        held = [own_ref[span, :]] + [ref[:, j * PACK : (j + 1) * PACK] for ref in blocks]
-        value, top, total = functools.reduce(joined, [unpacked(block) for block in held])
+        value, top, total = functools.reduce(joined, [unpacked(ref, j) for ref in (own_ref, *blocks)])
         both = jnp.maximum(top, own)
         keep = jnp.exp(top - both)
         fresh = jnp.exp(own - both)
@@ -406,8 +409,8 @@
             rows += dot(pick.astype(bf16), ref[...])
         rows = rows.astype(bf16)
         refs = out_refs[:RING] if along_x else out_refs[RING:]
-        start = 0 if along_x else HALF
-        for first in range(0, HALF, 384):
+        start, width = (0, SUMMED) if along_x else (SUMMED, FEATS - SUMMED)
+        for first in range(0, width, 384):
             terms = dot(rows, w_ref[:, start + first : start + first + 384]).astype(bf16)
             for slot, ref in enumerate(refs):
                 ref[:, first : first + 384] = terms[slot * SPAN : (slot + 1) * SPAN]
@@ -427,7 +430,9 @@
             in_specs=[WHOLE] * 3,
             out_specs=[WHOLE] * (1 + 2 * RING),
         ),
-        out_shape=[jax.ShapeDtypeStruct((1, 128), f32)] + [jax.ShapeDtypeStruct((SPAN, HALF), bf16)] * (2 * RING),
+        out_shape=[jax.ShapeDtypeStruct((1, 128), f32)]
+        + [jax.ShapeDtypeStruct((SPAN, SUMMED), bf16)] * RING
+        + [jax.ShapeDtypeStruct((SPAN, FEATS - SUMMED), bf16)] * RING,
         compiler_params=params(6),
         cost_estimate=cost(2 * ROWS * QCOLS * FEATS, 2 * (QCOLS * FEATS + ROWS * FEATS)),
     )(place, own, other, w_out)
@@ -442,9 +447,10 @@
 
 
 def middle(blocks):
+    width = blocks[0].shape[1]
     return pl.pallas_call(
         middle_kernel,
-        out_shape=[jax.ShapeDtypeStruct((LOCAL, HALF), f32)] + [jax.ShapeDtypeStruct((LOCAL, HALF), bf16)] * (RING - 1),
+        out_shape=[jax.ShapeDtypeStruct((LOCAL, width), f32)] + [jax.ShapeDtypeStruct((LOCAL, width), bf16)] * (RING - 1),
         compiler_params=params(4),
         cost_estimate=cost(4 * blocks[0].size, 12 * blocks[0].size),
     )(*blocks)
@@ -452,9 +458,9 @@
 
 def last_kernel(residual_ref, *refs):
     left, right, out_ref = refs[:RING], refs[RING : 2 * RING], refs[2 * RING]
-    for first, blocks in ((0, left), (HALF, right)):
+    for first, blocks in ((0, left), (SUMMED, right)):
         total = sum((ref[...].astype(f32) for ref in blocks[1:]), blocks[0][...])
-        columns = slice(first, first + HALF)
+        columns = slice(first, first + total.shape[1])
         out_ref[:, columns] = (residual_ref[:, columns].astype(f32) + total).astype(bf16)
 
 

time: 165 us -> 164 us (level)
    ppermute x12, waiting for transfers between devices: 13 us -> 17.8 us  [shift_x(): lax.ppermute(x, 'wide', [(i, (i // RING + by) % RING * RING + i % RING) f...]
    ppermute x12, waiting for transfers between devices: 4.83 us -> 2.46 us  [shift_y(): lax.ppermute(x, 'wide', [(i, i // RING * RING + (i + by) % RING) for i in...]
  transfers between devices with their start and end apart: 35 -> 35, of which waited for: 15 -> 17; matrix products, arithmetic and copies ran while one was open for 1% -> 1% of each run, Pallas kernels for 7% -> 7%
where the time goes in v5:
time: 164 us
  blocking collectives  47.7 us (29%)
  starting transfers between devices  40.9 us (25%)
  waiting for transfers between devices  40.5 us (25%)
  Pallas kernels  24.9 us (15%)
  local copies, waits for them, and re-layouts  6.39 us (4%)
  other arithmetic  2.31 us (1%)
    all_to_all x2, blocking collectives, spread(): lax.all_to_all(x, ('wide', 'narrow'), 0, 0, axis_index_groups=SAME_CORE,...  37.1 us
    ppermute x12, waiting for transfers between devices, shift_x(): lax.ppermute(x, 'wide', [(i, (i // RING + by) % RING * RING + i % RING) f...  17.8 us
    ppermute x12, starting transfers between devices, shift_y(): lax.ppermute(x, 'wide', [(i, i // RING * RING + (i + by) % RING) for i in...  16.7 us
    ppermute x12, starting transfers between devices, shift_x(): lax.ppermute(x, 'wide', [(i, (i // RING + by) % RING * RING + i % RING) f...  15.8 us
    ppermute x6, waiting for transfers between devices, shift_z(): lax.ppermute(x, 'narrow', [(i, (i // 2 + by) % RING * 2 + i % 2) for i in...  14.7 us
    all_to_all x1, blocking collectives, shards(): lax.all_to_all(jnp.broadcast_to(sums[None], (NARROW,) + sums.shape), 'nar...  10.5 us
    ppermute x6, starting transfers between devices, shift_z(): lax.ppermute(x, 'narrow', [(i, (i // 2 + by) % RING * 2 + i % 2) for i in...  7.34 us
    pallas_call x1, Pallas kernels, up_terms(): pl.pallas_call(up_kernel, in_specs=[WHOLE, HBM], out_specs=[WHOLE] * 2, o...  7.1 us
  transfers between devices with their start and end apart: 35, of which 17 were waited for; matrix products, arithmetic and copies ran while one was open for 1% of the time, Pallas kernels for 7%

profile of v5, /device:TPU:0, one launch (start us, length us, event | category | flops | bytes accessed | tf_op | source)
XLA Modules:
  0.0 163.5 jit_solution(11566357582954476506)
XLA Ops:
  0.6 1.0 convert_reduce_fusion
  1.7 10.5 %all_to_all.15 = f32[8,2,24]{2,1,0:T(2,128)S(1)} all-to-all(f32[8,2,24]{2,1,0:T(2,128)S(1)} %broadcast_in_dim.10), channel_id=1, replica_groups=mesh['wide'=16,'narrow'=8] {'narrow'}, dimensions={0} | all-to-all | bytes 3072 | tf_op jit(solution)/shard_map/all_to_all | solution.py:505
  12.2 1.0 fusion.3
  13.2 3.1 %collective-permute-start.8 = (bf16[24,1024]{1,0:T(8,128)(2,1)S(1)}, bf16[24,1024]{1,0:T(8,128)(2,1)S(1)}, u32[]{:S(2)}, u32[]{:S(2)}) collective-permute-start(bf16[24,1024]{1,0:T(8,128)(2,1)S(1)} %slice.37), channel_id=1, source_target_pairs={{0,24},{8,0},{16,8},{24,16},{32,56},{40,32},{48,40},{56,48},{64,88... | collective-permute-start | bytes 147464 | tf_op jit(solution)/shard_map/ppermute | solution.py:52
  16.3 0.6 collective-permute-start.7
  17.0 1.0 collective-permute-start.6
  17.9 2.8 %collective-permute-start.2 = (bf16[24,1280]{1,0:T(8,128)(2,1)S(1)}, bf16[24,1280]{1,0:T(8,128)(2,1)S(1)}, u32[]{:S(2)}, u32[]{:S(2)}) collective-permute-start(bf16[24,1280]{1,0:T(8,128)(2,1)S(1)} %slice.36), channel_id=1, source_target_pairs={{0,96},{8,104},{16,112},{24,120},{32,0},{40,8},{48,16},{56,24},{64... | collective-permute-start | bytes 184328 | tf_op jit(solution)/shard_map/ppermute | solution.py:48
  20.7 0.8 collective-permute-start.1
  21.5 0.9 collective-permute-start
  22.5 2.8 %collective-permute-start.11 = (bf16[96,1024]{1,0:T(8,128)(2,1)S(1)}, bf16[96,1024]{1,0:T(8,128)(2,1)S(1)}, u32[]{:S(2)}, u32[]{:S(2)}) collective-permute-start(bf16[96,1024]{1,0:T(8,128)(2,1)S(1)} %pad_maximum_fusion.1.refs_4_), channel_id=1, source_target_pairs={{0,96},{8,104},{16,112},{24,120},{32,0},{40,8},{48,16},{56,24},{64... | collective-permute-start | bytes 589832 | tf_op jit(solution)/shard_map/ppermute | solution.py:48
  25.3 1.1 collective-permute-done.1
  26.4 0.6 collective-permute-done
  27.1 2.3 %collective-permute-start.5 = (bf16[96,1280]{1,0:T(8,128)(2,1)S(1)}, bf16[96,1280]{1,0:T(8,128)(2,1)S(1)}, u32[]{:S(2)}, u32[]{:S(2)}) collective-permute-start(bf16[96,1280]{1,0:T(8,128)(2,1)S(1)} %pad_maximum_fusion.refs_0_), channel_id=1, source_target_pairs={{0,24},{8,0},{16,8},{24,16},{32,56},{40,32},{48,40},{56,48},{64,88... | collective-permute-start | bytes 737288 | tf_op jit(solution)/shard_map/ppermute | solution.py:52
  29.4 1.7 %collective-permute-start.4 = (bf16[96,1280]{1,0:T(8,128)(2,1)S(1)}, bf16[96,1280]{1,0:T(8,128)(2,1)S(1)}, u32[]{:S(2)}, u32[]{:S(2)}) collective-permute-start(bf16[96,1280]{1,0:T(8,128)(2,1)S(1)} %pad_maximum_fusion.refs_0_), channel_id=1, source_target_pairs={{0,16},{8,24},{16,0},{24,8},{32,48},{40,56},{48,32},{56,40},{64,80... | collective-permute-start | bytes 737288 | tf_op jit(solution)/shard_map/ppermute | solution.py:52
  31.1 1.4 collective-permute-start.10
  32.5 0.3 collective-permute-start.9
  32.8 1.2 copy.32.refs_9_
  34.1 4.6 %collective-permute-done.10.refs_6_ = bf16[96,1024]{1,0:T(8,128)(2,1)S(1)} collective-permute-done((bf16[96,1024]{1,0:T(8,128)(2,1)S(1)}, bf16[96,1024]{1,0:T(8,128)(2,1)S(1)}, u32[]{:S(2)}, u32[]{:S(2)}) %collective-permute-start.10) | collective-permute-done | bytes 196640 | tf_op jit(solution)/shard_map/ppermute | solution.py:48
  38.6 2.0 %collective-permute-done.9.refs_5_ = bf16[96,1024]{1,0:T(8,128)(2,1)S(1)} collective-permute-done((bf16[96,1024]{1,0:T(8,128)(2,1)S(1)}, bf16[96,1024]{1,0:T(8,128)(2,1)S(1)}, u32[]{:S(2)}, u32[]{:S(2)}) %collective-permute-start.9) | collective-permute-done | bytes 196640 | tf_op jit(solution)/shard_map/ppermute | solution.py:48
  40.7 0.7 collective-permute-done.3.refs_1_
  41.3 2.0 %copy-done = bf16[2304,768]{1,0:T(8,128)(2,1)S(1)} copy-done((bf16[2304,768]{1,0:T(8,128)(2,1)S(1)}, bf16[2304,768]{1,0:T(8,128)(2,1)}, u32[]{:S(2)}) %copy-start) | copy-done | bytes 3538968
  43.3 3.2 %shard_map.112 = (f32[4,48,896]{2,1,0:T(8,128)S(1)}, f32[4,48,896]{2,1,0:T(8,128)S(1)}, bf16[384,2304]{1,0:T(8,128)(2,1)S(1)}) custom-call(s32[4]{0:T(128)S(1)} %pad_add_fusion.place, bf16[96,1280]{1,0:T(8,128)(2,1)S(1)} %pad_maximum_fusion.refs_0_, bf16[96,1280]{1,0:T(8,128)(2,1)S(1)} %collective-permute-done.3.refs_1_, ...), custom_call_target="tpu_custom_call" | custom-call | flops 1415577600 | bytes 7274496 | tf_op jit(solution)/shard_map/pallas_call | solution.py:134
  46.7 2.1 %collective-permute-done.12 = f32[4,48,896]{2,1,0:T(8,128)S(1)} collective-permute-done((f32[4,48,896]{2,1,0:T(8,128)S(1)}, f32[4,48,896]{2,1,0:T(8,128)S(1)}, u32[]{:S(2)}, u32[]{:S(2)}) %collective-permute-start.12) | collective-permute-done | bytes 688160 | tf_op jit(solution)/shard_map/ppermute | solution.py:40
  48.9 0.6 collective-permute-start.13
  49.6 2.7 %collective-permute-start.15 = (f32[48,896]{1,0:T(8,128)S(1)}, f32[48,896]{1,0:T(8,128)S(1)}, u32[]{:S(2)}, u32[]{:S(2)}) collective-permute-start(f32[48,896]{1,0:T(8,128)S(1)} %get-tuple-element.78), channel_id=1, source_target_pairs={{0,6},{1,7},{2,0},{3,1},{4,2},{5,3},{6,4},{7,5},{8,14},{9,15},{10,... | collective-permute-start | bytes 516104 | tf_op jit(solution)/shard_map/ppermute | solution.py:44
  52.2 7.1 %shard_map.113 = (bf16[4,48,2304]{2,1,0:T(8,128)(2,1)S(1)}, bf16[4,48,2304]{2,1,0:T(8,128)(2,1)S(1)}) custom-call(bf16[384,2304]{1,0:T(8,128)(2,1)S(1)} %get-tuple-element.43.x_ref, bf16[2304,2304]{1,0:T(8,128)(2,1)} %weights_ref.1), custom_call_target="tpu_custom_call" | custom-call | flops 4076863488 | bytes 14155776 | tf_op jit(solution)/shard_map/pallas_call | solution.py:177
  59.4 0.9 collective-permute-done.13
  60.5 19.2 %all_to_all.16 = bf16[64,3,896]{2,1,0:T(4,128)(2,1)S(1)} all-to-all(bf16[64,3,896]{2,1,0:T(4,128)(2,1)S(1)} %bitcast.46), channel_id=1, replica_groups={{0,2,4,6,8,10,12,14,16,18,20,22,24,26,28,30,32,34,36,38,40,42,44,46,48,..., dimensions={0} | all-to-all | bytes 688128 | tf_op jit(solution)/shard_map/all_to_all | solution.py:67
  79.7 0.1 copy.34
  80.0 1.6 %collective-permute-done.16.q_ref = bf16[4,48,896]{2,1,0:T(8,128)(2,1)S(1)} collective-permute-done((bf16[4,48,896]{2,1,0:T(8,128)(2,1)S(1)}, bf16[4,48,896]{2,1,0:T(8,128)(2,1)S(1)}, u32[]{:S(2)}, u32[]{:S(2)}) %collective-permute-start.16) | collective-permute-done | bytes 344096 | tf_op jit(solution)/shard_map/ppermute | solution.py:40
  81.6 3.2 %shard_map.115 = bf16[4,48,896]{2,1,0:T(8,128)(2,1)S(1)} custom-call(s32[4]{0:T(128)S(1)} %pad_add_fusion.place, s32[24]{0:T(128)S(1)} %copy-done.2, bf16[4,48,896]{2,1,0:T(8,128)(2,1)S(1)} %collective-permute-done.16.q_ref, bf16[3,8,256,256]{3,2,1,0:T(8,128)(2,1)} %bitcast.41, bf16[3,8,256,256]{3,2,1,0:T(8,128)(2,1)} %bitcast.43), custom_call_target="tpu_custom_call" | custom-call | flops 150994944 | bytes 3833856 | tf_op jit(solution)/shard_map/pallas_call | solution.py:282
  84.8 0.2 collective-permute-start.18
  85.1 0.4 collective-permute-start.17
  85.4 3.2 %shard_map.114.a_ref = bf16[4,48,896]{2,1,0:T(8,128)(2,1)S(1)} custom-call(s32[4]{0:T(128)S(1)} %pad_add_fusion.place, s32[24]{0:T(128)S(1)} %copy-done.2, bf16[4,48,896]{2,1,0:T(8,128)(2,1)S(1)} %copy.37.q_ref, bf16[3,8,256,256]{3,2,1,0:T(8,128)(2,1)} %bitcast.42, bf16[3,8,256,256]{3,2,1,0:T(8,128)(2,1)} %bitcast.44), custom_call_target="tpu_custom_call" | custom-call | flops 150994944 | bytes 3833856 | tf_op jit(solution)/shard_map/pallas_call | solution.py:282
  88.6 1.3 shard_map.116
  90.0 0.7 collective-permute-start.19
  90.7 1.9 %collective-permute-start.20 = (bf16[48,3200]{1,0:T(8,128)(2,1)S(1)}, bf16[48,3200]{1,0:T(8,128)(2,1)S(1)}, u32[]{:S(2)}, u32[]{:S(2)}) collective-permute-start(bf16[48,3200]{1,0:T(8,128)(2,1)S(1)} %get-tuple-element.54), channel_id=1, source_target_pairs={{0,4},{1,5},{2,6},{3,7},{4,0},{5,1},{6,2},{7,3},{8,12},{9,13},{10,... | collective-permute-start | bytes 921608 | tf_op jit(solution)/shard_map/ppermute | solution.py:44
  92.6 1.5 collective-permute-start.21
  94.0 13.1 %collective-permute-done.19.refs_0_ = bf16[48,3200]{1,0:T(8,128)(2,1)S(1)} collective-permute-done((bf16[48,3200]{1,0:T(8,128)(2,1)S(1)}, bf16[48,3200]{1,0:T(8,128)(2,1)S(1)}, u32[]{:S(2)}, u32[]{:S(2)}) %collective-permute-start.19) | collective-permute-done | bytes 307232 | tf_op jit(solution)/shard_map/ppermute | solution.py:44
  107.2 0.6 collective-permute-done.21.refs_2_
  107.8 1.3 shard_map.117
  109.3 18.0 %all_to_all.17 = bf16[64,4,768]{2,1,0:T(4,128)(2,1)S(1)} all-to-all(bf16[64,4,768]{2,1,0:T(4,128)(2,1)S(1)} %bitcast.47), channel_id=1, replica_groups={{0,2,4,6,8,10,12,14,16,18,20,22,24,26,28,30,32,34,36,38,40,42,44,46,48,..., dimensions={0} | all-to-all | bytes 786432 | tf_op jit(solution)/shard_map/all_to_all | solution.py:67
  127.3 0.3 collective-permute-start.22
  127.7 1.7 %collective-permute-done.22.other_ref = bf16[256,768]{1,0:T(8,128)(2,1)S(1)} collective-permute-done((bf16[256,768]{1,0:T(8,128)(2,1)S(1)}, bf16[256,768]{1,0:T(8,128)(2,1)S(1)}, u32[]{:S(2)}, u32[]{:S(2)}) %collective-permute-start.22) | collective-permute-done | bytes 393248 | tf_op jit(solution)/shard_map/ppermute | solution.py:40
  129.4 2.0 %copy-done.3 = bf16[768,2304]{1,0:T(8,128)(2,1)S(1)} copy-done((bf16[768,2304]{1,0:T(8,128)(2,1)S(1)}, bf16[768,2304]{1,0:T(8,128)(2,1)}, u32[]{:S(2)}) %copy-start.3) | copy-done | bytes 3538968
  131.4 3.8 %shard_map.118 = (f32[1,128]{1,0:T(1,128)S(1)}, bf16[96,1152]{1,0:T(8,128)(2,1)S(1)}, bf16[96,1152]{1,0:T(8,128)(2,1)S(1)}, bf16[96,1152]{1,0:T(8,128)(2,1)S(1)}...) custom-call(s32[4]{0:T(128)S(1)} %pad_add_fusion.place, ...), custom_call_target="tpu_custom_call" | custom-call | flops 1358954496 | bytes 5308416 | tf_op jit(solution)/shard_map/pallas_call | solution.py:425
  135.2 0.7 collective-permute-start.23
  135.8 1.8 %collective-permute-start.24 = (bf16[96,1152]{1,0:T(8,128)(2,1)S(1)}, bf16[96,1152]{1,0:T(8,128)(2,1)S(1)}, u32[]{:S(2)}, u32[]{:S(2)}) collective-permute-start(bf16[96,1152]{1,0:T(8,128)(2,1)S(1)} %get-tuple-element.59), channel_id=1, source_target_pairs={{0,64},{8,72},{16,80},{24,88},{32,96},{40,104},{48,112},{56,120},{... | collective-permute-start | bytes 663560 | tf_op jit(solution)/shard_map/ppermute | solution.py:48
  137.7 1.0 collective-permute-start.25
  138.7 0.7 collective-permute-start.29
  139.5 2.1 %collective-permute-start.30 = (bf16[96,1152]{1,0:T(8,128)(2,1)S(1)}, bf16[96,1152]{1,0:T(8,128)(2,1)S(1)}, u32[]{:S(2)}, u32[]{:S(2)}) collective-permute-start(bf16[96,1152]{1,0:T(8,128)(2,1)S(1)} %get-tuple-element.67), channel_id=1, source_target_pairs={{0,16},{8,24},{16,0},{24,8},{32,48},{40,56},{48,32},{56,40},{64,80... | collective-permute-start | bytes 663560 | tf_op jit(solution)/shard_map/ppermute | solution.py:52
  141.6 7.1 %collective-permute-done.23.refs_1_ = bf16[96,1152]{1,0:T(8,128)(2,1)S(1)} collective-permute-done((bf16[96,1152]{1,0:T(8,128)(2,1)S(1)}, bf16[96,1152]{1,0:T(8,128)(2,1)S(1)}, u32[]{:S(2)}, u32[]{:S(2)}) %collective-permute-start.23) | collective-permute-done | bytes 221216 | tf_op jit(solution)/shard_map/ppermute | solution.py:48
  148.7 0.5 collective-permute-start.31
  149.4 1.5 collective-permute-start.26
  150.9 0.7 collective-permute-start.27
  151.6 2.5 %collective-permute-start.28 = (bf16[24,1152]{1,0:T(8,128)(2,1)S(1)}, bf16[24,1152]{1,0:T(8,128)(2,1)S(1)}, u32[]{:S(2)}, u32[]{:S(2)}) collective-permute-start(bf16[24,1152]{1,0:T(8,128)(2,1)S(1)} %get-tuple-element.64), channel_id=1, source_target_pairs={{0,24},{8,0},{16,8},{24,16},{32,56},{40,32},{48,40},{56,48},{64,88... | collective-permute-start | bytes 165896 | tf_op jit(solution)/shard_map/ppermute | solution.py:52
  154.1 1.7 %collective-permute-done.31.refs_3_ = bf16[96,1152]{1,0:T(8,128)(2,1)S(1)} collective-permute-done((bf16[96,1152]{1,0:T(8,128)(2,1)S(1)}, bf16[96,1152]{1,0:T(8,128)(2,1)S(1)}, u32[]{:S(2)}, u32[]{:S(2)}) %collective-permute-start.31) | collective-permute-done | bytes 221216 | tf_op jit(solution)/shard_map/ppermute | solution.py:52
  156.0 1.1 collective-permute-start.33
  157.1 2.1 %collective-permute-start.34 = (bf16[24,1152]{1,0:T(8,128)(2,1)S(1)}, bf16[24,1152]{1,0:T(8,128)(2,1)S(1)}, u32[]{:S(2)}, u32[]{:S(2)}) collective-permute-start(bf16[24,1152]{1,0:T(8,128)(2,1)S(1)} %get-tuple-element.72), channel_id=1, source_target_pairs={{0,96},{8,104},{16,112},{24,120},{32,0},{40,8},{48,16},{56,24},{64... | collective-permute-start | bytes 165896 | tf_op jit(solution)/shard_map/ppermute | solution.py:48
  159.2 0.5 slice_bitcast_fusion.3
  159.7 0.8 shard_map.122
  160.5 1.4 collective-permute-done.32.refs_5_
  161.9 0.9 collective-permute-done.34.refs_7_
  162.8 0.7 shard_map.121
  (52 shorter events, 1.5 us)
Async XLA Ops:
  13.2 8.3 %collective-permute-start.8 = (bf16[24,1024]{1,0:T(8,128)(2,1)S(1)}, bf16[24,1024]{1,0:T(8,128)(2,1)S(1)}, u32[]{:S(2)}, u32[]{:S(2)}) collective-permute-start(bf16[24,1024]{1,0:T(8,128)(2,1)S(1)} %slice.37), channel_id=1, source_target_pairs={{0,24},{8,0},{16,8},{24,16},{32,56},{40,32},{48,40},{56,48},{64,88... | collective-permute-start | bytes 147464 | tf_op jit(solution)/shard_map/ppermute | solution.py:52
  16.3 6.1 %collective-permute-start.7 = (bf16[24,1024]{1,0:T(8,128)(2,1)S(1)}, bf16[24,1024]{1,0:T(8,128)(2,1)S(1)}, u32[]{:S(2)}, u32[]{:S(2)}) collective-permute-start(bf16[24,1024]{1,0:T(8,128)(2,1)S(1)} %slice.37), channel_id=1, source_target_pairs={{0,16},{8,24},{16,0},{24,8},{32,48},{40,56},{48,32},{56,40},{64,80... | collective-permute-start | bytes 147464 | tf_op jit(solution)/shard_map/ppermute | solution.py:52
  17.0 5.5 %collective-permute-start.6 = (bf16[24,1024]{1,0:T(8,128)(2,1)S(1)}, bf16[24,1024]{1,0:T(8,128)(2,1)S(1)}, u32[]{:S(2)}, u32[]{:S(2)}) collective-permute-start(bf16[24,1024]{1,0:T(8,128)(2,1)S(1)} %slice.37), channel_id=1, source_target_pairs={{0,8},{8,16},{16,24},{24,0},{32,40},{40,48},{48,56},{56,32},{64,72... | collective-permute-start | bytes 147464 | tf_op jit(solution)/shard_map/ppermute | solution.py:52
  17.9 7.4 %collective-permute-start.2 = (bf16[24,1280]{1,0:T(8,128)(2,1)S(1)}, bf16[24,1280]{1,0:T(8,128)(2,1)S(1)}, u32[]{:S(2)}, u32[]{:S(2)}) collective-permute-start(bf16[24,1280]{1,0:T(8,128)(2,1)S(1)} %slice.36), channel_id=1, source_target_pairs={{0,96},{8,104},{16,112},{24,120},{32,0},{40,8},{48,16},{56,24},{64... | collective-permute-start | bytes 184328 | tf_op jit(solution)/shard_map/ppermute | solution.py:48
  20.7 5.7 %collective-permute-start.1 = (bf16[24,1280]{1,0:T(8,128)(2,1)S(1)}, bf16[24,1280]{1,0:T(8,128)(2,1)S(1)}, u32[]{:S(2)}, u32[]{:S(2)}) collective-permute-start(bf16[24,1280]{1,0:T(8,128)(2,1)S(1)} %slice.36), channel_id=1, source_target_pairs={{0,64},{8,72},{16,80},{24,88},{32,96},{40,104},{48,112},{56,120},{... | collective-permute-start | bytes 184328 | tf_op jit(solution)/shard_map/ppermute | solution.py:48
  21.5 5.6 %collective-permute-start = (bf16[24,1280]{1,0:T(8,128)(2,1)S(1)}, bf16[24,1280]{1,0:T(8,128)(2,1)S(1)}, u32[]{:S(2)}, u32[]{:S(2)}) collective-permute-start(bf16[24,1280]{1,0:T(8,128)(2,1)S(1)} %slice.36), channel_id=1, source_target_pairs={{0,32},{8,40},{16,48},{24,56},{32,64},{40,72},{48,80},{56,88},{64,... | collective-permute-start | bytes 184328 | tf_op jit(solution)/shard_map/ppermute | solution.py:48
  22.5 10.0 %collective-permute-start.11 = (bf16[96,1024]{1,0:T(8,128)(2,1)S(1)}, bf16[96,1024]{1,0:T(8,128)(2,1)S(1)}, u32[]{:S(2)}, u32[]{:S(2)}) collective-permute-start(bf16[96,1024]{1,0:T(8,128)(2,1)S(1)} %pad_maximum_fusion.1.refs_4_), channel_id=1, source_target_pairs={{0,96},{8,104},{16,112},{24,120},{32,0},{40,8},{48,16},{56,24},{64... | collective-permute-start | bytes 589832 | tf_op jit(solution)/shard_map/ppermute | solution.py:48
  27.1 13.5 %collective-permute-start.5 = (bf16[96,1280]{1,0:T(8,128)(2,1)S(1)}, bf16[96,1280]{1,0:T(8,128)(2,1)S(1)}, u32[]{:S(2)}, u32[]{:S(2)}) collective-permute-start(bf16[96,1280]{1,0:T(8,128)(2,1)S(1)} %pad_maximum_fusion.refs_0_), channel_id=1, source_target_pairs={{0,24},{8,0},{16,8},{24,16},{32,56},{40,32},{48,40},{56,48},{64,88... | collective-permute-start | bytes 737288 | tf_op jit(solution)/shard_map/ppermute | solution.py:52
  29.4 11.2 %collective-permute-start.4 = (bf16[96,1280]{1,0:T(8,128)(2,1)S(1)}, bf16[96,1280]{1,0:T(8,128)(2,1)S(1)}, u32[]{:S(2)}, u32[]{:S(2)}) collective-permute-start(bf16[96,1280]{1,0:T(8,128)(2,1)S(1)} %pad_maximum_fusion.refs_0_), channel_id=1, source_target_pairs={{0,16},{8,24},{16,0},{24,8},{32,48},{40,56},{48,32},{56,40},{64,80... | collective-permute-start | bytes 737288 | tf_op jit(solution)/shard_map/ppermute | solution.py:52
  31.1 10.2 %collective-permute-start.3 = (bf16[96,1280]{1,0:T(8,128)(2,1)S(1)}, bf16[96,1280]{1,0:T(8,128)(2,1)S(1)}, u32[]{:S(2)}, u32[]{:S(2)}) collective-permute-start(bf16[96,1280]{1,0:T(8,128)(2,1)S(1)} %pad_maximum_fusion.refs_0_), channel_id=1, source_target_pairs={{0,8},{8,16},{16,24},{24,0},{32,40},{40,48},{48,56},{56,32},{64,72... | collective-permute-start | bytes 737288 | tf_op jit(solution)/shard_map/ppermute | solution.py:52
  31.1 7.5 %collective-permute-start.10 = (bf16[96,1024]{1,0:T(8,128)(2,1)S(1)}, bf16[96,1024]{1,0:T(8,128)(2,1)S(1)}, u32[]{:S(2)}, u32[]{:S(2)}) collective-permute-start(bf16[96,1024]{1,0:T(8,128)(2,1)S(1)} %pad_maximum_fusion.1.refs_4_), channel_id=1, source_target_pairs={{0,64},{8,72},{16,80},{24,88},{32,96},{40,104},{48,112},{56,120},{... | collective-permute-start | bytes 589832 | tf_op jit(solution)/shard_map/ppermute | solution.py:48
  32.5 8.1 %collective-permute-start.9 = (bf16[96,1024]{1,0:T(8,128)(2,1)S(1)}, bf16[96,1024]{1,0:T(8,128)(2,1)S(1)}, u32[]{:S(2)}, u32[]{:S(2)}) collective-permute-start(bf16[96,1024]{1,0:T(8,128)(2,1)S(1)} %pad_maximum_fusion.1.refs_4_), channel_id=1, source_target_pairs={{0,32},{8,40},{16,48},{24,56},{32,64},{40,72},{48,80},{56,88},{64,... | collective-permute-start | bytes 589832 | tf_op jit(solution)/shard_map/ppermute | solution.py:48
  41.3 2.0 %copy-start = (bf16[2304,768]{1,0:T(8,128)(2,1)S(1)}, bf16[2304,768]{1,0:T(8,128)(2,1)}, u32[]{:S(2)}) copy-start(bf16[2304,768]{1,0:T(8,128)(2,1)} %refs_8_.1) | copy-start | bytes 10616836
  46.6 2.2 %collective-permute-start.12 = (f32[4,48,896]{2,1,0:T(8,128)S(1)}, f32[4,48,896]{2,1,0:T(8,128)S(1)}, u32[]{:S(2)}, u32[]{:S(2)}) collective-permute-start(f32[4,48,896]{2,1,0:T(8,128)S(1)} %get-tuple-element.41), channel_id=1, source_target_pairs={{0,1},{1,0},{2,3},{3,2},{4,5},{5,4},{6,7},{7,6},{8,9},{9,8},{10,11... | collective-permute-start | bytes 2064392 | tf_op jit(solution)/shard_map/ppermute | solution.py:40
  48.9 11.4 %collective-permute-start.13 = (f32[48,896]{1,0:T(8,128)S(1)}, f32[48,896]{1,0:T(8,128)S(1)}, u32[]{:S(2)}, u32[]{:S(2)}) collective-permute-start(f32[48,896]{1,0:T(8,128)S(1)} %get-tuple-element.77), channel_id=1, source_target_pairs={{0,2},{1,3},{2,4},{3,5},{4,6},{5,7},{6,0},{7,1},{8,10},{9,11},{10,... | collective-permute-start | bytes 516104 | tf_op jit(solution)/shard_map/ppermute | solution.py:44
  49.6 10.7 %collective-permute-start.15 = (f32[48,896]{1,0:T(8,128)S(1)}, f32[48,896]{1,0:T(8,128)S(1)}, u32[]{:S(2)}, u32[]{:S(2)}) collective-permute-start(f32[48,896]{1,0:T(8,128)S(1)} %get-tuple-element.78), channel_id=1, source_target_pairs={{0,6},{1,7},{2,0},{3,1},{4,2},{5,3},{6,4},{7,5},{8,14},{9,15},{10,... | collective-permute-start | bytes 516104 | tf_op jit(solution)/shard_map/ppermute | solution.py:44
  52.2 8.1 %collective-permute-start.14 = (f32[48,896]{1,0:T(8,128)S(1)}, f32[48,896]{1,0:T(8,128)S(1)}, u32[]{:S(2)}, u32[]{:S(2)}) collective-permute-start(f32[48,896]{1,0:T(8,128)S(1)} %get-tuple-element.79), channel_id=1, source_target_pairs={{0,4},{1,5},{2,6},{3,7},{4,0},{5,1},{6,2},{7,3},{8,12},{9,13},{10,... | collective-permute-start | bytes 516104 | tf_op jit(solution)/shard_map/ppermute | solution.py:44
  59.3 22.3 %copy-start.2 = (s32[24]{0:T(128)S(1)}, s32[24]{0:T(128)}, u32[]{:S(2)}) copy-start(s32[24]{0:T(128)} %lengths.3) | copy-start | bytes 292
  79.9 1.7 %collective-permute-start.16 = (bf16[4,48,896]{2,1,0:T(8,128)(2,1)S(1)}, bf16[4,48,896]{2,1,0:T(8,128)(2,1)S(1)}, u32[]{:S(2)}, u32[]{:S(2)}) collective-permute-start(bf16[4,48,896]{2,1,0:T(8,128)(2,1)S(1)} %copy.37.q_ref), channel_id=1, source_target_pairs={{0,1},{1,0},{2,3},{3,2},{4,5},{5,4},{6,7},{7,6},{8,9},{9,8},{10,11... | collective-permute-start | bytes 1032200 | tf_op jit(solution)/shard_map/ppermute | solution.py:40
  84.8 3.8 %collective-permute-start.18 = (bf16[4,48,2304]{2,1,0:T(8,128)(2,1)S(1)}, bf16[4,48,2304]{2,1,0:T(8,128)(2,1)S(1)}, u32[]{:S(2)}, u32[]{:S(2)}) collective-permute-start(bf16[4,48,2304]{2,1,0:T(8,128)(2,1)S(1)} %get-tuple-element.50), channel_id=1, source_target_pairs={{0,1},{1,0},{2,3},{3,2},{4,5},{5,4},{6,7},{7,6},{8,9},{9,8},{10,11... | collective-permute-start | bytes 2654216 | tf_op jit(solution)/shard_map/ppermute | solution.py:40
  85.1 3.6 %collective-permute-start.17 = (bf16[4,48,896]{2,1,0:T(8,128)(2,1)S(1)}, bf16[4,48,896]{2,1,0:T(8,128)(2,1)S(1)}, u32[]{:S(2)}, u32[]{:S(2)}) collective-permute-start(bf16[4,48,896]{2,1,0:T(8,128)(2,1)S(1)} %shard_map.115), channel_id=1, source_target_pairs={{0,1},{1,0},{2,3},{3,2},{4,5},{5,4},{6,7},{7,6},{8,9},{9,8},{10,11... | collective-permute-start | bytes 1032200 | tf_op jit(solution)/shard_map/ppermute | solution.py:40
  90.0 17.2 %collective-permute-start.19 = (bf16[48,3200]{1,0:T(8,128)(2,1)S(1)}, bf16[48,3200]{1,0:T(8,128)(2,1)S(1)}, u32[]{:S(2)}, u32[]{:S(2)}) collective-permute-start(bf16[48,3200]{1,0:T(8,128)(2,1)S(1)} %get-tuple-element.53), channel_id=1, source_target_pairs={{0,2},{1,3},{2,4},{3,5},{4,6},{5,7},{6,0},{7,1},{8,10},{9,11},{10,... | collective-permute-start | bytes 921608 | tf_op jit(solution)/shard_map/ppermute | solution.py:44
  90.7 16.5 %collective-permute-start.20 = (bf16[48,3200]{1,0:T(8,128)(2,1)S(1)}, bf16[48,3200]{1,0:T(8,128)(2,1)S(1)}, u32[]{:S(2)}, u32[]{:S(2)}) collective-permute-start(bf16[48,3200]{1,0:T(8,128)(2,1)S(1)} %get-tuple-element.54), channel_id=1, source_target_pairs={{0,4},{1,5},{2,6},{3,7},{4,0},{5,1},{6,2},{7,3},{8,12},{9,13},{10,... | collective-permute-start | bytes 921608 | tf_op jit(solution)/shard_map/ppermute | solution.py:44
  92.6 15.2 %collective-permute-start.21 = (bf16[48,3200]{1,0:T(8,128)(2,1)S(1)}, bf16[48,3200]{1,0:T(8,128)(2,1)S(1)}, u32[]{:S(2)}, u32[]{:S(2)}) collective-permute-start(bf16[48,3200]{1,0:T(8,128)(2,1)S(1)} %get-tuple-element.55), channel_id=1, source_target_pairs={{0,6},{1,7},{2,0},{3,1},{4,2},{5,3},{6,4},{7,5},{8,14},{9,15},{10,... | collective-permute-start | bytes 921608 | tf_op jit(solution)/shard_map/ppermute | solution.py:44
  127.3 35.5 %copy-start.1 = (bf16[24,2304]{1,0:T(8,128)(2,1)S(1)}, bf16[24,2304]{1,0:T(8,128)(2,1)}, u32[]{:S(2)}) copy-start(bf16[24,2304]{1,0:T(8,128)(2,1)} %residual_ref.1) | copy-start | bytes 331780
  127.3 2.0 %collective-permute-start.22 = (bf16[256,768]{1,0:T(8,128)(2,1)S(1)}, bf16[256,768]{1,0:T(8,128)(2,1)S(1)}, u32[]{:S(2)}, u32[]{:S(2)}) collective-permute-start(bf16[256,768]{1,0:T(8,128)(2,1)S(1)} %reshape.60.own_ref), channel_id=1, source_target_pairs={{0,1},{1,0},{2,3},{3,2},{4,5},{5,4},{6,7},{7,6},{8,9},{9,8},{10,11... | collective-permute-start | bytes 1179656 | tf_op jit(solution)/shard_map/ppermute | solution.py:40
  129.4 2.0 %copy-start.3 = (bf16[768,2304]{1,0:T(8,128)(2,1)S(1)}, bf16[768,2304]{1,0:T(8,128)(2,1)}, u32[]{:S(2)}) copy-start(bf16[768,2304]{1,0:T(8,128)(2,1)} %w_ref.1) | copy-start | bytes 10616836
  135.2 13.5 %collective-permute-start.23 = (bf16[96,1152]{1,0:T(8,128)(2,1)S(1)}, bf16[96,1152]{1,0:T(8,128)(2,1)S(1)}, u32[]{:S(2)}, u32[]{:S(2)}) collective-permute-start(bf16[96,1152]{1,0:T(8,128)(2,1)S(1)} %get-tuple-element.58), channel_id=1, source_target_pairs={{0,32},{8,40},{16,48},{24,56},{32,64},{40,72},{48,80},{56,88},{64,... | collective-permute-start | bytes 663560 | tf_op jit(solution)/shard_map/ppermute | solution.py:48
  135.8 13.3 %collective-permute-start.24 = (bf16[96,1152]{1,0:T(8,128)(2,1)S(1)}, bf16[96,1152]{1,0:T(8,128)(2,1)S(1)}, u32[]{:S(2)}, u32[]{:S(2)}) collective-permute-start(bf16[96,1152]{1,0:T(8,128)(2,1)S(1)} %get-tuple-element.59), channel_id=1, source_target_pairs={{0,64},{8,72},{16,80},{24,88},{32,96},{40,104},{48,112},{56,120},{... | collective-permute-start | bytes 663560 | tf_op jit(solution)/shard_map/ppermute | solution.py:48
  137.7 11.6 %collective-permute-start.25 = (bf16[96,1152]{1,0:T(8,128)(2,1)S(1)}, bf16[96,1152]{1,0:T(8,128)(2,1)S(1)}, u32[]{:S(2)}, u32[]{:S(2)}) collective-permute-start(bf16[96,1152]{1,0:T(8,128)(2,1)S(1)} %get-tuple-element.60), channel_id=1, source_target_pairs={{0,96},{8,104},{16,112},{24,120},{32,0},{40,8},{48,16},{56,24},{64... | collective-permute-start | bytes 663560 | tf_op jit(solution)/shard_map/ppermute | solution.py:48
  138.7 12.8 %collective-permute-start.29 = (bf16[96,1152]{1,0:T(8,128)(2,1)S(1)}, bf16[96,1152]{1,0:T(8,128)(2,1)S(1)}, u32[]{:S(2)}, u32[]{:S(2)}) collective-permute-start(bf16[96,1152]{1,0:T(8,128)(2,1)S(1)} %get-tuple-element.66), channel_id=1, source_target_pairs={{0,8},{8,16},{16,24},{24,0},{32,40},{40,48},{48,56},{56,32},{64,72... | collective-permute-start | bytes 663560 | tf_op jit(solution)/shard_map/ppermute | solution.py:52
  139.5 14.6 %collective-permute-start.30 = (bf16[96,1152]{1,0:T(8,128)(2,1)S(1)}, bf16[96,1152]{1,0:T(8,128)(2,1)S(1)}, u32[]{:S(2)}, u32[]{:S(2)}) collective-permute-start(bf16[96,1152]{1,0:T(8,128)(2,1)S(1)} %get-tuple-element.67), channel_id=1, source_target_pairs={{0,16},{8,24},{16,0},{24,8},{32,48},{40,56},{48,32},{56,40},{64,80... | collective-permute-start | bytes 663560 | tf_op jit(solution)/shard_map/ppermute | solution.py:52
  148.7 7.1 %collective-permute-start.31 = (bf16[96,1152]{1,0:T(8,128)(2,1)S(1)}, bf16[96,1152]{1,0:T(8,128)(2,1)S(1)}, u32[]{:S(2)}, u32[]{:S(2)}) collective-permute-start(bf16[96,1152]{1,0:T(8,128)(2,1)S(1)} %get-tuple-element.68), channel_id=1, source_target_pairs={{0,24},{8,0},{16,8},{24,16},{32,56},{40,32},{48,40},{56,48},{64,88... | collective-permute-start | bytes 663560 | tf_op jit(solution)/shard_map/ppermute | solution.py:52
  149.4 7.7 %collective-permute-start.26 = (bf16[24,1152]{1,0:T(8,128)(2,1)S(1)}, bf16[24,1152]{1,0:T(8,128)(2,1)S(1)}, u32[]{:S(2)}, u32[]{:S(2)}) collective-permute-start(bf16[24,1152]{1,0:T(8,128)(2,1)S(1)} %get-tuple-element.62), channel_id=1, source_target_pairs={{0,8},{8,16},{16,24},{24,0},{32,40},{40,48},{48,56},{56,32},{64,72... | collective-permute-start | bytes 165896 | tf_op jit(solution)/shard_map/ppermute | solution.py:52
  150.9 9.6 %collective-permute-start.27 = (bf16[24,1152]{1,0:T(8,128)(2,1)S(1)}, bf16[24,1152]{1,0:T(8,128)(2,1)S(1)}, u32[]{:S(2)}, u32[]{:S(2)}) collective-permute-start(bf16[24,1152]{1,0:T(8,128)(2,1)S(1)} %get-tuple-element.63), channel_id=1, source_target_pairs={{0,16},{8,24},{16,0},{24,8},{32,48},{40,56},{48,32},{56,40},{64,80... | collective-permute-start | bytes 165896 | tf_op jit(solution)/shard_map/ppermute | solution.py:52
  151.6 9.0 %collective-permute-start.28 = (bf16[24,1152]{1,0:T(8,128)(2,1)S(1)}, bf16[24,1152]{1,0:T(8,128)(2,1)S(1)}, u32[]{:S(2)}, u32[]{:S(2)}) collective-permute-start(bf16[24,1152]{1,0:T(8,128)(2,1)S(1)} %get-tuple-element.64), channel_id=1, source_target_pairs={{0,24},{8,0},{16,8},{24,16},{32,56},{40,32},{48,40},{56,48},{64,88... | collective-permute-start | bytes 165896 | tf_op jit(solution)/shard_map/ppermute | solution.py:52
  155.9 6.0 %collective-permute-start.32 = (bf16[24,1152]{1,0:T(8,128)(2,1)S(1)}, bf16[24,1152]{1,0:T(8,128)(2,1)S(1)}, u32[]{:S(2)}, u32[]{:S(2)}) collective-permute-start(bf16[24,1152]{1,0:T(8,128)(2,1)S(1)} %get-tuple-element.70), channel_id=1, source_target_pairs={{0,32},{8,40},{16,48},{24,56},{32,64},{40,72},{48,80},{56,88},{64,... | collective-permute-start | bytes 165896 | tf_op jit(solution)/shard_map/ppermute | solution.py:48
  156.0 5.9 %collective-permute-start.33 = (bf16[24,1152]{1,0:T(8,128)(2,1)S(1)}, bf16[24,1152]{1,0:T(8,128)(2,1)S(1)}, u32[]{:S(2)}, u32[]{:S(2)}) collective-permute-start(bf16[24,1152]{1,0:T(8,128)(2,1)S(1)} %get-tuple-element.71), channel_id=1, source_target_pairs={{0,64},{8,72},{16,80},{24,88},{32,96},{40,104},{48,112},{56,120},{... | collective-permute-start | bytes 165896 | tf_op jit(solution)/shard_map/ppermute | solution.py:48
  157.1 5.7 %collective-permute-start.34 = (bf16[24,1152]{1,0:T(8,128)(2,1)S(1)}, bf16[24,1152]{1,0:T(8,128)(2,1)S(1)}, u32[]{:S(2)}, u32[]{:S(2)}) collective-permute-start(bf16[24,1152]{1,0:T(8,128)(2,1)S(1)} %get-tuple-element.72), channel_id=1, source_target_pairs={{0,96},{8,104},{16,112},{24,120},{32,0},{40,8},{48,16},{56,24},{64... | collective-permute-start | bytes 165896 | tf_op jit(solution)/shard_map/ppermute | solution.py:48

commit v6 on v5

--- a/solution.py
+++ b/solution.py
@@ -123,8 +123,7 @@
                 keep_ref[at, :, columns] = acc_ref[lanes, pl.ds(n + c, SHARE, stride=NARROW), :]
                 send_ref[at, :, columns] = acc_ref[lanes, pl.ds(n + 1 - c, SHARE, stride=NARROW), :]
 
-    for first in range(0, QCOLS, 256):
-        deal(dot(x_ref[...], wq_ref[:, first : first + 256]), first)
+    deal(dot(x_ref[...], wq_ref[...]), 0)
     deal(jnp.concatenate([dot(x_ref[...], wkv_ref[...]), jnp.zeros((ROWS, 128 - KVCOLS), f32)], axis=1), QCOLS)
 
 
@@ -138,7 +137,7 @@
             grid=(1,),
             in_specs=[WHOLE] * (2 * RING + 2),
             out_specs=[WHOLE] * 3,
-            scratch_shapes=[pltpu.VMEM((2, ROWS, 128), f32), pltpu.VMEM((ROWS, FEATS), f32)],
+            scratch_shapes=[pltpu.VMEM((QCOLS // 128, ROWS, 128), f32), pltpu.VMEM((ROWS, FEATS), f32)],
         ),
         out_shape=[out, out, rows],
         compiler_params=params(8),
@@ -410,10 +409,10 @@
         rows = rows.astype(bf16)
         refs = out_refs[:RING] if along_x else out_refs[RING:]
         start, width = (0, SUMMED) if along_x else (SUMMED, FEATS - SUMMED)
-        for first in range(0, width, 384):
-            terms = dot(rows, w_ref[:, start + first : start + first + 384]).astype(bf16)
+        for first in range(0, width, 1152):
+            terms = dot(rows, w_ref[:, start + first : start + first + 1152]).astype(bf16)
             for slot, ref in enumerate(refs):
-                ref[:, first : first + 384] = terms[slot * SPAN : (slot + 1) * SPAN]
+                ref[:, first : first + 1152] = terms[slot * SPAN : (slot + 1) * SPAN]
     peaks = own_ref[...].astype(f32)
     peaks = peaks[:, 0:128] + peaks[:, 128:256] + peaks[:, 256:384]
     row = lax.broadcasted_iota(jnp.int32, peaks.shape, 0)

time: 164 us -> 164 us (level)
  no operation moved by 1% of the time
where the time goes in v6:
time: 164 us; the launch traced here: 163 us
  blocking collectives  47.7 us (29%)
  starting transfers between devices  40.9 us (25%)
  waiting for transfers between devices  40.5 us (25%)
  Pallas kernels  24.8 us (15%)
  local copies, waits for them, and re-layouts  6.39 us (4%)
  other arithmetic  2.31 us (1%)
    all_to_all x2, blocking collectives, spread(): lax.all_to_all(x, ('wide', 'narrow'), 0, 0, axis_index_groups=SAME_CORE,...  37.2 us
    ppermute x12, waiting for transfers between devices, shift_x(): lax.ppermute(x, 'wide', [(i, (i // RING + by) % RING * RING + i % RING) f...  17.8 us
    ppermute x12, starting transfers between devices, shift_y(): lax.ppermute(x, 'wide', [(i, i // RING * RING + (i + by) % RING) for i in...  16.7 us
    ppermute x12, starting transfers between devices, shift_x(): lax.ppermute(x, 'wide', [(i, (i // RING + by) % RING * RING + i % RING) f...  15.8 us
    ppermute x6, waiting for transfers between devices, shift_z(): lax.ppermute(x, 'narrow', [(i, (i // 2 + by) % RING * 2 + i % 2) for i in...  14.7 us
    all_to_all x1, blocking collectives, shards(): lax.all_to_all(jnp.broadcast_to(sums[None], (NARROW,) + sums.shape), 'nar...  10.5 us
    ppermute x6, starting transfers between devices, shift_z(): lax.ppermute(x, 'narrow', [(i, (i // 2 + by) % RING * 2 + i % 2) for i in...  7.34 us
    pallas_call x1, Pallas kernels, up_terms(): pl.pallas_call(up_kernel, in_specs=[WHOLE, HBM], out_specs=[WHOLE] * 2, o...  7.11 us
  transfers between devices with their start and end apart: 35, of which 17 were waited for; matrix products, arithmetic and copies ran while one was open for 1% of the time, Pallas kernels for 7%

profile of v6, /device:TPU:0, one launch (start us, length us, event | category | flops | bytes accessed | tf_op | source)
XLA Modules:
  0.0 163.4 jit_solution(7068993249042088125)
XLA Ops:
  0.6 1.0 convert_reduce_fusion
  1.7 10.5 %all_to_all.15 = f32[8,2,24]{2,1,0:T(2,128)S(1)} all-to-all(f32[8,2,24]{2,1,0:T(2,128)S(1)} %broadcast_in_dim.10), channel_id=1, replica_groups=mesh['wide'=16,'narrow'=8] {'narrow'}, dimensions={0} | all-to-all | bytes 3072 | tf_op jit(solution)/shard_map/all_to_all | solution.py:504
  12.2 1.0 fusion.3
  13.2 3.1 %collective-permute-start.8 = (bf16[24,1024]{1,0:T(8,128)(2,1)S(1)}, bf16[24,1024]{1,0:T(8,128)(2,1)S(1)}, u32[]{:S(2)}, u32[]{:S(2)}) collective-permute-start(bf16[24,1024]{1,0:T(8,128)(2,1)S(1)} %slice.37), channel_id=1, source_target_pairs={{0,24},{8,0},{16,8},{24,16},{32,56},{40,32},{48,40},{56,48},{64,88... | collective-permute-start | bytes 147464 | tf_op jit(solution)/shard_map/ppermute | solution.py:52
  16.3 0.6 collective-permute-start.7
  17.0 1.0 collective-permute-start.6
  17.9 2.8 %collective-permute-start.2 = (bf16[24,1280]{1,0:T(8,128)(2,1)S(1)}, bf16[24,1280]{1,0:T(8,128)(2,1)S(1)}, u32[]{:S(2)}, u32[]{:S(2)}) collective-permute-start(bf16[24,1280]{1,0:T(8,128)(2,1)S(1)} %slice.36), channel_id=1, source_target_pairs={{0,96},{8,104},{16,112},{24,120},{32,0},{40,8},{48,16},{56,24},{64... | collective-permute-start | bytes 184328 | tf_op jit(solution)/shard_map/ppermute | solution.py:48
  20.7 0.8 collective-permute-start.1
  21.5 0.9 collective-permute-start
  22.5 2.8 %collective-permute-start.11 = (bf16[96,1024]{1,0:T(8,128)(2,1)S(1)}, bf16[96,1024]{1,0:T(8,128)(2,1)S(1)}, u32[]{:S(2)}, u32[]{:S(2)}) collective-permute-start(bf16[96,1024]{1,0:T(8,128)(2,1)S(1)} %pad_maximum_fusion.1.refs_4_), channel_id=1, source_target_pairs={{0,96},{8,104},{16,112},{24,120},{32,0},{40,8},{48,16},{56,24},{64... | collective-permute-start | bytes 589832 | tf_op jit(solution)/shard_map/ppermute | solution.py:48
  25.3 1.1 collective-permute-done.1
  26.4 0.6 collective-permute-done
  27.1 2.3 %collective-permute-start.5 = (bf16[96,1280]{1,0:T(8,128)(2,1)S(1)}, bf16[96,1280]{1,0:T(8,128)(2,1)S(1)}, u32[]{:S(2)}, u32[]{:S(2)}) collective-permute-start(bf16[96,1280]{1,0:T(8,128)(2,1)S(1)} %pad_maximum_fusion.refs_0_), channel_id=1, source_target_pairs={{0,24},{8,0},{16,8},{24,16},{32,56},{40,32},{48,40},{56,48},{64,88... | collective-permute-start | bytes 737288 | tf_op jit(solution)/shard_map/ppermute | solution.py:52
  29.4 1.7 %collective-permute-start.4 = (bf16[96,1280]{1,0:T(8,128)(2,1)S(1)}, bf16[96,1280]{1,0:T(8,128)(2,1)S(1)}, u32[]{:S(2)}, u32[]{:S(2)}) collective-permute-start(bf16[96,1280]{1,0:T(8,128)(2,1)S(1)} %pad_maximum_fusion.refs_0_), channel_id=1, source_target_pairs={{0,16},{8,24},{16,0},{24,8},{32,48},{40,56},{48,32},{56,40},{64,80... | collective-permute-start | bytes 737288 | tf_op jit(solution)/shard_map/ppermute | solution.py:52
  31.1 1.4 collective-permute-start.10
  32.5 0.3 collective-permute-start.9
  32.8 1.2 copy.32.refs_9_
  34.1 4.6 %collective-permute-done.10.refs_6_ = bf16[96,1024]{1,0:T(8,128)(2,1)S(1)} collective-permute-done((bf16[96,1024]{1,0:T(8,128)(2,1)S(1)}, bf16[96,1024]{1,0:T(8,128)(2,1)S(1)}, u32[]{:S(2)}, u32[]{:S(2)}) %collective-permute-start.10) | collective-permute-done | bytes 196640 | tf_op jit(solution)/shard_map/ppermute | solution.py:48
  38.6 2.0 %collective-permute-done.9.refs_5_ = bf16[96,1024]{1,0:T(8,128)(2,1)S(1)} collective-permute-done((bf16[96,1024]{1,0:T(8,128)(2,1)S(1)}, bf16[96,1024]{1,0:T(8,128)(2,1)S(1)}, u32[]{:S(2)}, u32[]{:S(2)}) %collective-permute-start.9) | collective-permute-done | bytes 196640 | tf_op jit(solution)/shard_map/ppermute | solution.py:48
  40.7 0.7 collective-permute-done.3.refs_1_
  41.3 2.0 %copy-done = bf16[2304,768]{1,0:T(8,128)(2,1)S(1)} copy-done((bf16[2304,768]{1,0:T(8,128)(2,1)S(1)}, bf16[2304,768]{1,0:T(8,128)(2,1)}, u32[]{:S(2)}) %copy-start) | copy-done | bytes 3538968
  43.3 3.2 %shard_map.112 = (f32[4,48,896]{2,1,0:T(8,128)S(1)}, f32[4,48,896]{2,1,0:T(8,128)S(1)}, bf16[384,2304]{1,0:T(8,128)(2,1)S(1)}) custom-call(s32[4]{0:T(128)S(1)} %pad_add_fusion.place, bf16[96,1280]{1,0:T(8,128)(2,1)S(1)} %pad_maximum_fusion.refs_0_, bf16[96,1280]{1,0:T(8,128)(2,1)S(1)} %collective-permute-done.3.refs_1_, ...), custom_call_target="tpu_custom_call" | custom-call | flops 1415577600 | bytes 7274496 | tf_op jit(solution)/shard_map/pallas_call | solution.py:133
  46.6 2.1 %collective-permute-done.12 = f32[4,48,896]{2,1,0:T(8,128)S(1)} collective-permute-done((f32[4,48,896]{2,1,0:T(8,128)S(1)}, f32[4,48,896]{2,1,0:T(8,128)S(1)}, u32[]{:S(2)}, u32[]{:S(2)}) %collective-permute-start.12) | collective-permute-done | bytes 688160 | tf_op jit(solution)/shard_map/ppermute | solution.py:40
  48.9 0.6 collective-permute-start.13
  49.5 2.7 %collective-permute-start.15 = (f32[48,896]{1,0:T(8,128)S(1)}, f32[48,896]{1,0:T(8,128)S(1)}, u32[]{:S(2)}, u32[]{:S(2)}) collective-permute-start(f32[48,896]{1,0:T(8,128)S(1)} %get-tuple-element.78), channel_id=1, source_target_pairs={{0,6},{1,7},{2,0},{3,1},{4,2},{5,3},{6,4},{7,5},{8,14},{9,15},{10,... | collective-permute-start | bytes 516104 | tf_op jit(solution)/shard_map/ppermute | solution.py:44
  52.2 7.1 %shard_map.113 = (bf16[4,48,2304]{2,1,0:T(8,128)(2,1)S(1)}, bf16[4,48,2304]{2,1,0:T(8,128)(2,1)S(1)}) custom-call(bf16[384,2304]{1,0:T(8,128)(2,1)S(1)} %get-tuple-element.43.x_ref, bf16[2304,2304]{1,0:T(8,128)(2,1)} %weights_ref.1), custom_call_target="tpu_custom_call" | custom-call | flops 4076863488 | bytes 14155776 | tf_op jit(solution)/shard_map/pallas_call | solution.py:176
  59.3 0.9 collective-permute-done.13
  60.5 19.2 %all_to_all.16 = bf16[64,3,896]{2,1,0:T(4,128)(2,1)S(1)} all-to-all(bf16[64,3,896]{2,1,0:T(4,128)(2,1)S(1)} %bitcast.46), channel_id=1, replica_groups={{0,2,4,6,8,10,12,14,16,18,20,22,24,26,28,30,32,34,36,38,40,42,44,46,48,..., dimensions={0} | all-to-all | bytes 688128 | tf_op jit(solution)/shard_map/all_to_all | solution.py:67
  79.7 0.1 copy.34
  80.0 1.6 %collective-permute-done.16.q_ref = bf16[4,48,896]{2,1,0:T(8,128)(2,1)S(1)} collective-permute-done((bf16[4,48,896]{2,1,0:T(8,128)(2,1)S(1)}, bf16[4,48,896]{2,1,0:T(8,128)(2,1)S(1)}, u32[]{:S(2)}, u32[]{:S(2)}) %collective-permute-start.16) | collective-permute-done | bytes 344096 | tf_op jit(solution)/shard_map/ppermute | solution.py:40
  81.6 3.2 %shard_map.115 = bf16[4,48,896]{2,1,0:T(8,128)(2,1)S(1)} custom-call(s32[4]{0:T(128)S(1)} %pad_add_fusion.place, s32[24]{0:T(128)S(1)} %copy-done.2, bf16[4,48,896]{2,1,0:T(8,128)(2,1)S(1)} %collective-permute-done.16.q_ref, bf16[3,8,256,256]{3,2,1,0:T(8,128)(2,1)} %bitcast.41, bf16[3,8,256,256]{3,2,1,0:T(8,128)(2,1)} %bitcast.43), custom_call_target="tpu_custom_call" | custom-call | flops 150994944 | bytes 3833856 | tf_op jit(solution)/shard_map/pallas_call | solution.py:281
  84.8 0.2 collective-permute-start.18
  85.0 0.4 collective-permute-start.17
  85.4 3.2 %shard_map.114.a_ref = bf16[4,48,896]{2,1,0:T(8,128)(2,1)S(1)} custom-call(s32[4]{0:T(128)S(1)} %pad_add_fusion.place, s32[24]{0:T(128)S(1)} %copy-done.2, bf16[4,48,896]{2,1,0:T(8,128)(2,1)S(1)} %copy.37.q_ref, bf16[3,8,256,256]{3,2,1,0:T(8,128)(2,1)} %bitcast.42, bf16[3,8,256,256]{3,2,1,0:T(8,128)(2,1)} %bitcast.44), custom_call_target="tpu_custom_call" | custom-call | flops 150994944 | bytes 3833856 | tf_op jit(solution)/shard_map/pallas_call | solution.py:281
  88.6 1.3 shard_map.116
  90.0 0.7 collective-permute-start.19
  90.7 1.9 %collective-permute-start.20 = (bf16[48,3200]{1,0:T(8,128)(2,1)S(1)}, bf16[48,3200]{1,0:T(8,128)(2,1)S(1)}, u32[]{:S(2)}, u32[]{:S(2)}) collective-permute-start(bf16[48,3200]{1,0:T(8,128)(2,1)S(1)} %get-tuple-element.54), channel_id=1, source_target_pairs={{0,4},{1,5},{2,6},{3,7},{4,0},{5,1},{6,2},{7,3},{8,12},{9,13},{10,... | collective-permute-start | bytes 921608 | tf_op jit(solution)/shard_map/ppermute | solution.py:44
  92.6 1.5 collective-permute-start.21
  94.0 13.1 %collective-permute-done.19.refs_0_ = bf16[48,3200]{1,0:T(8,128)(2,1)S(1)} collective-permute-done((bf16[48,3200]{1,0:T(8,128)(2,1)S(1)}, bf16[48,3200]{1,0:T(8,128)(2,1)S(1)}, u32[]{:S(2)}, u32[]{:S(2)}) %collective-permute-start.19) | collective-permute-done | bytes 307232 | tf_op jit(solution)/shard_map/ppermute | solution.py:44
  107.1 0.6 collective-permute-done.21.refs_2_
  107.8 1.3 shard_map.117
  109.2 18.0 %all_to_all.17 = bf16[64,4,768]{2,1,0:T(4,128)(2,1)S(1)} all-to-all(bf16[64,4,768]{2,1,0:T(4,128)(2,1)S(1)} %bitcast.47), channel_id=1, replica_groups={{0,2,4,6,8,10,12,14,16,18,20,22,24,26,28,30,32,34,36,38,40,42,44,46,48,..., dimensions={0} | all-to-all | bytes 786432 | tf_op jit(solution)/shard_map/all_to_all | solution.py:67
  127.3 0.3 collective-permute-start.22
  127.6 1.7 %collective-permute-done.22.other_ref = bf16[256,768]{1,0:T(8,128)(2,1)S(1)} collective-permute-done((bf16[256,768]{1,0:T(8,128)(2,1)S(1)}, bf16[256,768]{1,0:T(8,128)(2,1)S(1)}, u32[]{:S(2)}, u32[]{:S(2)}) %collective-permute-start.22) | collective-permute-done | bytes 393248 | tf_op jit(solution)/shard_map/ppermute | solution.py:40
  129.3 2.0 %copy-done.3 = bf16[768,2304]{1,0:T(8,128)(2,1)S(1)} copy-done((bf16[768,2304]{1,0:T(8,128)(2,1)S(1)}, bf16[768,2304]{1,0:T(8,128)(2,1)}, u32[]{:S(2)}) %copy-start.3) | copy-done | bytes 3538968
  131.3 3.7 %shard_map.118 = (f32[1,128]{1,0:T(1,128)S(1)}, bf16[96,1152]{1,0:T(8,128)(2,1)S(1)}, bf16[96,1152]{1,0:T(8,128)(2,1)S(1)}, bf16[96,1152]{1,0:T(8,128)(2,1)S(1)}...) custom-call(s32[4]{0:T(128)S(1)} %pad_add_fusion.place, ...), custom_call_target="tpu_custom_call" | custom-call | flops 1358954496 | bytes 5308416 | tf_op jit(solution)/shard_map/pallas_call | solution.py:424
  135.0 0.7 collective-permute-start.23
  135.7 1.8 %collective-permute-start.24 = (bf16[96,1152]{1,0:T(8,128)(2,1)S(1)}, bf16[96,1152]{1,0:T(8,128)(2,1)S(1)}, u32[]{:S(2)}, u32[]{:S(2)}) collective-permute-start(bf16[96,1152]{1,0:T(8,128)(2,1)S(1)} %get-tuple-element.59), channel_id=1, source_target_pairs={{0,64},{8,72},{16,80},{24,88},{32,96},{40,104},{48,112},{56,120},{... | collective-permute-start | bytes 663560 | tf_op jit(solution)/shard_map/ppermute | solution.py:48
  137.6 1.0 collective-permute-start.25
  138.6 0.7 collective-permute-start.29
  139.3 2.1 %collective-permute-start.30 = (bf16[96,1152]{1,0:T(8,128)(2,1)S(1)}, bf16[96,1152]{1,0:T(8,128)(2,1)S(1)}, u32[]{:S(2)}, u32[]{:S(2)}) collective-permute-start(bf16[96,1152]{1,0:T(8,128)(2,1)S(1)} %get-tuple-element.67), channel_id=1, source_target_pairs={{0,16},{8,24},{16,0},{24,8},{32,48},{40,56},{48,32},{56,40},{64,80... | collective-permute-start | bytes 663560 | tf_op jit(solution)/shard_map/ppermute | solution.py:52
  141.4 7.1 %collective-permute-done.23.refs_1_ = bf16[96,1152]{1,0:T(8,128)(2,1)S(1)} collective-permute-done((bf16[96,1152]{1,0:T(8,128)(2,1)S(1)}, bf16[96,1152]{1,0:T(8,128)(2,1)S(1)}, u32[]{:S(2)}, u32[]{:S(2)}) %collective-permute-start.23) | collective-permute-done | bytes 221216 | tf_op jit(solution)/shard_map/ppermute | solution.py:48
  148.5 0.5 collective-permute-start.31
  149.3 1.5 collective-permute-start.26
  150.8 0.7 collective-permute-start.27
  151.4 2.5 %collective-permute-start.28 = (bf16[24,1152]{1,0:T(8,128)(2,1)S(1)}, bf16[24,1152]{1,0:T(8,128)(2,1)S(1)}, u32[]{:S(2)}, u32[]{:S(2)}) collective-permute-start(bf16[24,1152]{1,0:T(8,128)(2,1)S(1)} %get-tuple-element.64), channel_id=1, source_target_pairs={{0,24},{8,0},{16,8},{24,16},{32,56},{40,32},{48,40},{56,48},{64,88... | collective-permute-start | bytes 165896 | tf_op jit(solution)/shard_map/ppermute | solution.py:52
  154.0 1.7 %collective-permute-done.31.refs_3_ = bf16[96,1152]{1,0:T(8,128)(2,1)S(1)} collective-permute-done((bf16[96,1152]{1,0:T(8,128)(2,1)S(1)}, bf16[96,1152]{1,0:T(8,128)(2,1)S(1)}, u32[]{:S(2)}, u32[]{:S(2)}) %collective-permute-start.31) | collective-permute-done | bytes 221216 | tf_op jit(solution)/shard_map/ppermute | solution.py:52
  155.8 1.1 collective-permute-start.33
  156.9 2.1 %collective-permute-start.34 = (bf16[24,1152]{1,0:T(8,128)(2,1)S(1)}, bf16[24,1152]{1,0:T(8,128)(2,1)S(1)}, u32[]{:S(2)}, u32[]{:S(2)}) collective-permute-start(bf16[24,1152]{1,0:T(8,128)(2,1)S(1)} %get-tuple-element.72), channel_id=1, source_target_pairs={{0,96},{8,104},{16,112},{24,120},{32,0},{40,8},{48,16},{56,24},{64... | collective-permute-start | bytes 165896 | tf_op jit(solution)/shard_map/ppermute | solution.py:48
  159.1 0.5 slice_bitcast_fusion.3
  159.6 0.8 shard_map.122
  160.4 1.4 collective-permute-done.32.refs_5_
  161.8 0.9 collective-permute-done.34.refs_7_
  162.7 0.7 shard_map.121
  (52 shorter events, 1.5 us)
Async XLA Ops:
  13.2 8.3 %collective-permute-start.8 = (bf16[24,1024]{1,0:T(8,128)(2,1)S(1)}, bf16[24,1024]{1,0:T(8,128)(2,1)S(1)}, u32[]{:S(2)}, u32[]{:S(2)}) collective-permute-start(bf16[24,1024]{1,0:T(8,128)(2,1)S(1)} %slice.37), channel_id=1, source_target_pairs={{0,24},{8,0},{16,8},{24,16},{32,56},{40,32},{48,40},{56,48},{64,88... | collective-permute-start | bytes 147464 | tf_op jit(solution)/shard_map/ppermute | solution.py:52
  16.3 6.1 %collective-permute-start.7 = (bf16[24,1024]{1,0:T(8,128)(2,1)S(1)}, bf16[24,1024]{1,0:T(8,128)(2,1)S(1)}, u32[]{:S(2)}, u32[]{:S(2)}) collective-permute-start(bf16[24,1024]{1,0:T(8,128)(2,1)S(1)} %slice.37), channel_id=1, source_target_pairs={{0,16},{8,24},{16,0},{24,8},{32,48},{40,56},{48,32},{56,40},{64,80... | collective-permute-start | bytes 147464 | tf_op jit(solution)/shard_map/ppermute | solution.py:52
  17.0 5.5 %collective-permute-start.6 = (bf16[24,1024]{1,0:T(8,128)(2,1)S(1)}, bf16[24,1024]{1,0:T(8,128)(2,1)S(1)}, u32[]{:S(2)}, u32[]{:S(2)}) collective-permute-start(bf16[24,1024]{1,0:T(8,128)(2,1)S(1)} %slice.37), channel_id=1, source_target_pairs={{0,8},{8,16},{16,24},{24,0},{32,40},{40,48},{48,56},{56,32},{64,72... | collective-permute-start | bytes 147464 | tf_op jit(solution)/shard_map/ppermute | solution.py:52
  17.9 7.4 %collective-permute-start.2 = (bf16[24,1280]{1,0:T(8,128)(2,1)S(1)}, bf16[24,1280]{1,0:T(8,128)(2,1)S(1)}, u32[]{:S(2)}, u32[]{:S(2)}) collective-permute-start(bf16[24,1280]{1,0:T(8,128)(2,1)S(1)} %slice.36), channel_id=1, source_target_pairs={{0,96},{8,104},{16,112},{24,120},{32,0},{40,8},{48,16},{56,24},{64... | collective-permute-start | bytes 184328 | tf_op jit(solution)/shard_map/ppermute | solution.py:48
  20.7 5.7 %collective-permute-start.1 = (bf16[24,1280]{1,0:T(8,128)(2,1)S(1)}, bf16[24,1280]{1,0:T(8,128)(2,1)S(1)}, u32[]{:S(2)}, u32[]{:S(2)}) collective-permute-start(bf16[24,1280]{1,0:T(8,128)(2,1)S(1)} %slice.36), channel_id=1, source_target_pairs={{0,64},{8,72},{16,80},{24,88},{32,96},{40,104},{48,112},{56,120},{... | collective-permute-start | bytes 184328 | tf_op jit(solution)/shard_map/ppermute | solution.py:48
  21.5 5.6 %collective-permute-start = (bf16[24,1280]{1,0:T(8,128)(2,1)S(1)}, bf16[24,1280]{1,0:T(8,128)(2,1)S(1)}, u32[]{:S(2)}, u32[]{:S(2)}) collective-permute-start(bf16[24,1280]{1,0:T(8,128)(2,1)S(1)} %slice.36), channel_id=1, source_target_pairs={{0,32},{8,40},{16,48},{24,56},{32,64},{40,72},{48,80},{56,88},{64,... | collective-permute-start | bytes 184328 | tf_op jit(solution)/shard_map/ppermute | solution.py:48
  22.5 10.0 %collective-permute-start.11 = (bf16[96,1024]{1,0:T(8,128)(2,1)S(1)}, bf16[96,1024]{1,0:T(8,128)(2,1)S(1)}, u32[]{:S(2)}, u32[]{:S(2)}) collective-permute-start(bf16[96,1024]{1,0:T(8,128)(2,1)S(1)} %pad_maximum_fusion.1.refs_4_), channel_id=1, source_target_pairs={{0,96},{8,104},{16,112},{24,120},{32,0},{40,8},{48,16},{56,24},{64... | collective-permute-start | bytes 589832 | tf_op jit(solution)/shard_map/ppermute | solution.py:48
  27.1 13.5 %collective-permute-start.5 = (bf16[96,1280]{1,0:T(8,128)(2,1)S(1)}, bf16[96,1280]{1,0:T(8,128)(2,1)S(1)}, u32[]{:S(2)}, u32[]{:S(2)}) collective-permute-start(bf16[96,1280]{1,0:T(8,128)(2,1)S(1)} %pad_maximum_fusion.refs_0_), channel_id=1, source_target_pairs={{0,24},{8,0},{16,8},{24,16},{32,56},{40,32},{48,40},{56,48},{64,88... | collective-permute-start | bytes 737288 | tf_op jit(solution)/shard_map/ppermute | solution.py:52
  29.4 11.2 %collective-permute-start.4 = (bf16[96,1280]{1,0:T(8,128)(2,1)S(1)}, bf16[96,1280]{1,0:T(8,128)(2,1)S(1)}, u32[]{:S(2)}, u32[]{:S(2)}) collective-permute-start(bf16[96,1280]{1,0:T(8,128)(2,1)S(1)} %pad_maximum_fusion.refs_0_), channel_id=1, source_target_pairs={{0,16},{8,24},{16,0},{24,8},{32,48},{40,56},{48,32},{56,40},{64,80... | collective-permute-start | bytes 737288 | tf_op jit(solution)/shard_map/ppermute | solution.py:52
  31.1 10.2 %collective-permute-start.3 = (bf16[96,1280]{1,0:T(8,128)(2,1)S(1)}, bf16[96,1280]{1,0:T(8,128)(2,1)S(1)}, u32[]{:S(2)}, u32[]{:S(2)}) collective-permute-start(bf16[96,1280]{1,0:T(8,128)(2,1)S(1)} %pad_maximum_fusion.refs_0_), channel_id=1, source_target_pairs={{0,8},{8,16},{16,24},{24,0},{32,40},{40,48},{48,56},{56,32},{64,72... | collective-permute-start | bytes 737288 | tf_op jit(solution)/shard_map/ppermute | solution.py:52
  31.1 7.5 %collective-permute-start.10 = (bf16[96,1024]{1,0:T(8,128)(2,1)S(1)}, bf16[96,1024]{1,0:T(8,128)(2,1)S(1)}, u32[]{:S(2)}, u32[]{:S(2)}) collective-permute-start(bf16[96,1024]{1,0:T(8,128)(2,1)S(1)} %pad_maximum_fusion.1.refs_4_), channel_id=1, source_target_pairs={{0,64},{8,72},{16,80},{24,88},{32,96},{40,104},{48,112},{56,120},{... | collective-permute-start | bytes 589832 | tf_op jit(solution)/shard_map/ppermute | solution.py:48
  32.5 8.1 %collective-permute-start.9 = (bf16[96,1024]{1,0:T(8,128)(2,1)S(1)}, bf16[96,1024]{1,0:T(8,128)(2,1)S(1)}, u32[]{:S(2)}, u32[]{:S(2)}) collective-permute-start(bf16[96,1024]{1,0:T(8,128)(2,1)S(1)} %pad_maximum_fusion.1.refs_4_), channel_id=1, source_target_pairs={{0,32},{8,40},{16,48},{24,56},{32,64},{40,72},{48,80},{56,88},{64,... | collective-permute-start | bytes 589832 | tf_op jit(solution)/shard_map/ppermute | solution.py:48
  41.3 2.0 %copy-start = (bf16[2304,768]{1,0:T(8,128)(2,1)S(1)}, bf16[2304,768]{1,0:T(8,128)(2,1)}, u32[]{:S(2)}) copy-start(bf16[2304,768]{1,0:T(8,128)(2,1)} %refs_8_.1) | copy-start | bytes 10616836
  46.5 2.2 %collective-permute-start.12 = (f32[4,48,896]{2,1,0:T(8,128)S(1)}, f32[4,48,896]{2,1,0:T(8,128)S(1)}, u32[]{:S(2)}, u32[]{:S(2)}) collective-permute-start(f32[4,48,896]{2,1,0:T(8,128)S(1)} %get-tuple-element.41), channel_id=1, source_target_pairs={{0,1},{1,0},{2,3},{3,2},{4,5},{5,4},{6,7},{7,6},{8,9},{9,8},{10,11... | collective-permute-start | bytes 2064392 | tf_op jit(solution)/shard_map/ppermute | solution.py:40
  48.9 11.4 %collective-permute-start.13 = (f32[48,896]{1,0:T(8,128)S(1)}, f32[48,896]{1,0:T(8,128)S(1)}, u32[]{:S(2)}, u32[]{:S(2)}) collective-permute-start(f32[48,896]{1,0:T(8,128)S(1)} %get-tuple-element.77), channel_id=1, source_target_pairs={{0,2},{1,3},{2,4},{3,5},{4,6},{5,7},{6,0},{7,1},{8,10},{9,11},{10,... | collective-permute-start | bytes 516104 | tf_op jit(solution)/shard_map/ppermute | solution.py:44
  49.5 10.8 %collective-permute-start.15 = (f32[48,896]{1,0:T(8,128)S(1)}, f32[48,896]{1,0:T(8,128)S(1)}, u32[]{:S(2)}, u32[]{:S(2)}) collective-permute-start(f32[48,896]{1,0:T(8,128)S(1)} %get-tuple-element.78), channel_id=1, source_target_pairs={{0,6},{1,7},{2,0},{3,1},{4,2},{5,3},{6,4},{7,5},{8,14},{9,15},{10,... | collective-permute-start | bytes 516104 | tf_op jit(solution)/shard_map/ppermute | solution.py:44
  52.2 8.1 %collective-permute-start.14 = (f32[48,896]{1,0:T(8,128)S(1)}, f32[48,896]{1,0:T(8,128)S(1)}, u32[]{:S(2)}, u32[]{:S(2)}) collective-permute-start(f32[48,896]{1,0:T(8,128)S(1)} %get-tuple-element.79), channel_id=1, source_target_pairs={{0,4},{1,5},{2,6},{3,7},{4,0},{5,1},{6,2},{7,3},{8,12},{9,13},{10,... | collective-permute-start | bytes 516104 | tf_op jit(solution)/shard_map/ppermute | solution.py:44
  59.3 22.3 %copy-start.2 = (s32[24]{0:T(128)S(1)}, s32[24]{0:T(128)}, u32[]{:S(2)}) copy-start(s32[24]{0:T(128)} %lengths.3) | copy-start | bytes 292
  79.9 1.7 %collective-permute-start.16 = (bf16[4,48,896]{2,1,0:T(8,128)(2,1)S(1)}, bf16[4,48,896]{2,1,0:T(8,128)(2,1)S(1)}, u32[]{:S(2)}, u32[]{:S(2)}) collective-permute-start(bf16[4,48,896]{2,1,0:T(8,128)(2,1)S(1)} %copy.37.q_ref), channel_id=1, source_target_pairs={{0,1},{1,0},{2,3},{3,2},{4,5},{5,4},{6,7},{7,6},{8,9},{9,8},{10,11... | collective-permute-start | bytes 1032200 | tf_op jit(solution)/shard_map/ppermute | solution.py:40
  84.8 3.8 %collective-permute-start.18 = (bf16[4,48,2304]{2,1,0:T(8,128)(2,1)S(1)}, bf16[4,48,2304]{2,1,0:T(8,128)(2,1)S(1)}, u32[]{:S(2)}, u32[]{:S(2)}) collective-permute-start(bf16[4,48,2304]{2,1,0:T(8,128)(2,1)S(1)} %get-tuple-element.50), channel_id=1, source_target_pairs={{0,1},{1,0},{2,3},{3,2},{4,5},{5,4},{6,7},{7,6},{8,9},{9,8},{10,11... | collective-permute-start | bytes 2654216 | tf_op jit(solution)/shard_map/ppermute | solution.py:40
  85.0 3.6 %collective-permute-start.17 = (bf16[4,48,896]{2,1,0:T(8,128)(2,1)S(1)}, bf16[4,48,896]{2,1,0:T(8,128)(2,1)S(1)}, u32[]{:S(2)}, u32[]{:S(2)}) collective-permute-start(bf16[4,48,896]{2,1,0:T(8,128)(2,1)S(1)} %shard_map.115), channel_id=1, source_target_pairs={{0,1},{1,0},{2,3},{3,2},{4,5},{5,4},{6,7},{7,6},{8,9},{9,8},{10,11... | collective-permute-start | bytes 1032200 | tf_op jit(solution)/shard_map/ppermute | solution.py:40
  90.0 17.2 %collective-permute-start.19 = (bf16[48,3200]{1,0:T(8,128)(2,1)S(1)}, bf16[48,3200]{1,0:T(8,128)(2,1)S(1)}, u32[]{:S(2)}, u32[]{:S(2)}) collective-permute-start(bf16[48,3200]{1,0:T(8,128)(2,1)S(1)} %get-tuple-element.53), channel_id=1, source_target_pairs={{0,2},{1,3},{2,4},{3,5},{4,6},{5,7},{6,0},{7,1},{8,10},{9,11},{10,... | collective-permute-start | bytes 921608 | tf_op jit(solution)/shard_map/ppermute | solution.py:44
  90.7 16.5 %collective-permute-start.20 = (bf16[48,3200]{1,0:T(8,128)(2,1)S(1)}, bf16[48,3200]{1,0:T(8,128)(2,1)S(1)}, u32[]{:S(2)}, u32[]{:S(2)}) collective-permute-start(bf16[48,3200]{1,0:T(8,128)(2,1)S(1)} %get-tuple-element.54), channel_id=1, source_target_pairs={{0,4},{1,5},{2,6},{3,7},{4,0},{5,1},{6,2},{7,3},{8,12},{9,13},{10,... | collective-permute-start | bytes 921608 | tf_op jit(solution)/shard_map/ppermute | solution.py:44
  92.6 15.2 %collective-permute-start.21 = (bf16[48,3200]{1,0:T(8,128)(2,1)S(1)}, bf16[48,3200]{1,0:T(8,128)(2,1)S(1)}, u32[]{:S(2)}, u32[]{:S(2)}) collective-permute-start(bf16[48,3200]{1,0:T(8,128)(2,1)S(1)} %get-tuple-element.55), channel_id=1, source_target_pairs={{0,6},{1,7},{2,0},{3,1},{4,2},{5,3},{6,4},{7,5},{8,14},{9,15},{10,... | collective-permute-start | bytes 921608 | tf_op jit(solution)/shard_map/ppermute | solution.py:44
  127.3 35.3 %copy-start.1 = (bf16[24,2304]{1,0:T(8,128)(2,1)S(1)}, bf16[24,2304]{1,0:T(8,128)(2,1)}, u32[]{:S(2)}) copy-start(bf16[24,2304]{1,0:T(8,128)(2,1)} %residual_ref.1) | copy-start | bytes 331780
  127.3 2.0 %collective-permute-start.22 = (bf16[256,768]{1,0:T(8,128)(2,1)S(1)}, bf16[256,768]{1,0:T(8,128)(2,1)S(1)}, u32[]{:S(2)}, u32[]{:S(2)}) collective-permute-start(bf16[256,768]{1,0:T(8,128)(2,1)S(1)} %reshape.60.own_ref), channel_id=1, source_target_pairs={{0,1},{1,0},{2,3},{3,2},{4,5},{5,4},{6,7},{7,6},{8,9},{9,8},{10,11... | collective-permute-start | bytes 1179656 | tf_op jit(solution)/shard_map/ppermute | solution.py:40
  129.3 2.0 %copy-start.3 = (bf16[768,2304]{1,0:T(8,128)(2,1)S(1)}, bf16[768,2304]{1,0:T(8,128)(2,1)}, u32[]{:S(2)}) copy-start(bf16[768,2304]{1,0:T(8,128)(2,1)} %w_ref.1) | copy-start | bytes 10616836
  135.0 13.5 %collective-permute-start.23 = (bf16[96,1152]{1,0:T(8,128)(2,1)S(1)}, bf16[96,1152]{1,0:T(8,128)(2,1)S(1)}, u32[]{:S(2)}, u32[]{:S(2)}) collective-permute-start(bf16[96,1152]{1,0:T(8,128)(2,1)S(1)} %get-tuple-element.58), channel_id=1, source_target_pairs={{0,32},{8,40},{16,48},{24,56},{32,64},{40,72},{48,80},{56,88},{64,... | collective-permute-start | bytes 663560 | tf_op jit(solution)/shard_map/ppermute | solution.py:48
  135.7 13.3 %collective-permute-start.24 = (bf16[96,1152]{1,0:T(8,128)(2,1)S(1)}, bf16[96,1152]{1,0:T(8,128)(2,1)S(1)}, u32[]{:S(2)}, u32[]{:S(2)}) collective-permute-start(bf16[96,1152]{1,0:T(8,128)(2,1)S(1)} %get-tuple-element.59), channel_id=1, source_target_pairs={{0,64},{8,72},{16,80},{24,88},{32,96},{40,104},{48,112},{56,120},{... | collective-permute-start | bytes 663560 | tf_op jit(solution)/shard_map/ppermute | solution.py:48
  137.6 11.6 %collective-permute-start.25 = (bf16[96,1152]{1,0:T(8,128)(2,1)S(1)}, bf16[96,1152]{1,0:T(8,128)(2,1)S(1)}, u32[]{:S(2)}, u32[]{:S(2)}) collective-permute-start(bf16[96,1152]{1,0:T(8,128)(2,1)S(1)} %get-tuple-element.60), channel_id=1, source_target_pairs={{0,96},{8,104},{16,112},{24,120},{32,0},{40,8},{48,16},{56,24},{64... | collective-permute-start | bytes 663560 | tf_op jit(solution)/shard_map/ppermute | solution.py:48
  138.6 12.8 %collective-permute-start.29 = (bf16[96,1152]{1,0:T(8,128)(2,1)S(1)}, bf16[96,1152]{1,0:T(8,128)(2,1)S(1)}, u32[]{:S(2)}, u32[]{:S(2)}) collective-permute-start(bf16[96,1152]{1,0:T(8,128)(2,1)S(1)} %get-tuple-element.66), channel_id=1, source_target_pairs={{0,8},{8,16},{16,24},{24,0},{32,40},{40,48},{48,56},{56,32},{64,72... | collective-permute-start | bytes 663560 | tf_op jit(solution)/shard_map/ppermute | solution.py:52
  139.3 14.6 %collective-permute-start.30 = (bf16[96,1152]{1,0:T(8,128)(2,1)S(1)}, bf16[96,1152]{1,0:T(8,128)(2,1)S(1)}, u32[]{:S(2)}, u32[]{:S(2)}) collective-permute-start(bf16[96,1152]{1,0:T(8,128)(2,1)S(1)} %get-tuple-element.67), channel_id=1, source_target_pairs={{0,16},{8,24},{16,0},{24,8},{32,48},{40,56},{48,32},{56,40},{64,80... | collective-permute-start | bytes 663560 | tf_op jit(solution)/shard_map/ppermute | solution.py:52
  148.5 7.1 %collective-permute-start.31 = (bf16[96,1152]{1,0:T(8,128)(2,1)S(1)}, bf16[96,1152]{1,0:T(8,128)(2,1)S(1)}, u32[]{:S(2)}, u32[]{:S(2)}) collective-permute-start(bf16[96,1152]{1,0:T(8,128)(2,1)S(1)} %get-tuple-element.68), channel_id=1, source_target_pairs={{0,24},{8,0},{16,8},{24,16},{32,56},{40,32},{48,40},{56,48},{64,88... | collective-permute-start | bytes 663560 | tf_op jit(solution)/shard_map/ppermute | solution.py:52
  149.3 7.7 %collective-permute-start.26 = (bf16[24,1152]{1,0:T(8,128)(2,1)S(1)}, bf16[24,1152]{1,0:T(8,128)(2,1)S(1)}, u32[]{:S(2)}, u32[]{:S(2)}) collective-permute-start(bf16[24,1152]{1,0:T(8,128)(2,1)S(1)} %get-tuple-element.62), channel_id=1, source_target_pairs={{0,8},{8,16},{16,24},{24,0},{32,40},{40,48},{48,56},{56,32},{64,72... | collective-permute-start | bytes 165896 | tf_op jit(solution)/shard_map/ppermute | solution.py:52
  150.8 9.6 %collective-permute-start.27 = (bf16[24,1152]{1,0:T(8,128)(2,1)S(1)}, bf16[24,1152]{1,0:T(8,128)(2,1)S(1)}, u32[]{:S(2)}, u32[]{:S(2)}) collective-permute-start(bf16[24,1152]{1,0:T(8,128)(2,1)S(1)} %get-tuple-element.63), channel_id=1, source_target_pairs={{0,16},{8,24},{16,0},{24,8},{32,48},{40,56},{48,32},{56,40},{64,80... | collective-permute-start | bytes 165896 | tf_op jit(solution)/shard_map/ppermute | solution.py:52
  151.4 9.0 %collective-permute-start.28 = (bf16[24,1152]{1,0:T(8,128)(2,1)S(1)}, bf16[24,1152]{1,0:T(8,128)(2,1)S(1)}, u32[]{:S(2)}, u32[]{:S(2)}) collective-permute-start(bf16[24,1152]{1,0:T(8,128)(2,1)S(1)} %get-tuple-element.64), channel_id=1, source_target_pairs={{0,24},{8,0},{16,8},{24,16},{32,56},{40,32},{48,40},{56,48},{64,88... | collective-permute-start | bytes 165896 | tf_op jit(solution)/shard_map/ppermute | solution.py:52
  155.8 6.0 %collective-permute-start.32 = (bf16[24,1152]{1,0:T(8,128)(2,1)S(1)}, bf16[24,1152]{1,0:T(8,128)(2,1)S(1)}, u32[]{:S(2)}, u32[]{:S(2)}) collective-permute-start(bf16[24,1152]{1,0:T(8,128)(2,1)S(1)} %get-tuple-element.70), channel_id=1, source_target_pairs={{0,32},{8,40},{16,48},{24,56},{32,64},{40,72},{48,80},{56,88},{64,... | collective-permute-start | bytes 165896 | tf_op jit(solution)/shard_map/ppermute | solution.py:48
  155.8 5.9 %collective-permute-start.33 = (bf16[24,1152]{1,0:T(8,128)(2,1)S(1)}, bf16[24,1152]{1,0:T(8,128)(2,1)S(1)}, u32[]{:S(2)}, u32[]{:S(2)}) collective-permute-start(bf16[24,1152]{1,0:T(8,128)(2,1)S(1)} %get-tuple-element.71), channel_id=1, source_target_pairs={{0,64},{8,72},{16,80},{24,88},{32,96},{40,104},{48,112},{56,120},{... | collective-permute-start | bytes 165896 | tf_op jit(solution)/shard_map/ppermute | solution.py:48
  156.9 5.7 %collective-permute-start.34 = (bf16[24,1152]{1,0:T(8,128)(2,1)S(1)}, bf16[24,1152]{1,0:T(8,128)(2,1)S(1)}, u32[]{:S(2)}, u32[]{:S(2)}) collective-permute-start(bf16[24,1152]{1,0:T(8,128)(2,1)S(1)} %get-tuple-element.72), channel_id=1, source_target_pairs={{0,96},{8,104},{16,112},{24,120},{32,0},{40,8},{48,16},{56,24},{64... | collective-permute-start | bytes 165896 | tf_op jit(solution)/shard_map/ppermute | solution.py:48
